TPU v7x, 128 devices: a whole 4x4x4 slice. The times are simulated.
128 devices in a mesh: section: 8 (over x, core), dp: 16 (over z, y).
Axes of the slice: x: 4, y: 4, z: 4, core: 2. Of those that a mesh axis runs over, the one named last changes fastest.
Arguments:
- layer_inputs: bfloat16 [8, 4, 64, 6144], P('section', None, None, 'dp'), may hold values from -6 to 6
- expert_ids: int32 [8, 4, 64, 2], P('section'), may hold values from 0 to 7, as said below
- hidden: bfloat16 [8, 4, 32, 8192], P('section', None, None, 'dp'), may hold values from -6 to 6
- down_weight: bfloat16 [8, 6144, 8192], P('section', None, 'dp'), may hold values from -0.0625 to 0.0625
- router_weight: bfloat16 [8, 6144, 8], P('section', 'dp'), may hold values from -0.078125 to 0.078125
- grad_out: bfloat16 [4, 64, 6144], P(None, None, 'dp'), may hold values from -1.796875 to 1.796875
Outputs:
- input_grad: bfloat16 [4, 64, 6144], P(None, 'section', 'dp')
- hidden_grad: bfloat16 [8, 4, 32, 8192], P('section', None, None, 'dp')
- down_grad: bfloat16 [8, 6144, 8192], P('section', None, 'dp')
- router_grad: float32 [8, 6144, 8], P('section', 'dp')
Inputs may be any that keep to these rules, and one draw needn't show every extreme that they name: `expert_ids`: the 2 ids of a token differ. In each layer and micro-batch expert 0 is named by 16 to 32 tokens, and in at least one micro-batch of every layer by exactly 32.
All inputs are finite; a program needn't handle non-finite values.
Results may differ from a plain program's by a relative error of at most 0.0062.
Values may be sent and summed in bfloat16 or wider, within the bound.
No kernel may reach another device: no remote copies, remote signals or barrier semaphores. Data moves between devices by JAX's collectives and lax.ppermute only.
A program may use at most 64 MiB of HBM per device.

v0:
```python
import jax
import jax.numpy as jnp
from jax import lax
from jax.sharding import PartitionSpec as P


def from_behind(value, axis, steps):
    count = lax.axis_size(axis)
    initial, last = (max(0, -steps), min(count, count - steps))
    return lax.ppermute(value, axis, [(source, source + steps) for source in range(initial, last)])


def write_slice(buffer, which_micro, fresh, active):
    previous = lax.dynamic_index_in_dim(buffer, which_micro, 0, keepdims=False)
    updated = jnp.where(active, fresh, previous)
    return lax.dynamic_update_index_in_dim(buffer, updated, which_micro, 0)


def per_device(layer_inputs, expert_ids, hidden, down_weight, router_weight, grad_out):
    sections = lax.axis_size("section")
    my_section = lax.axis_index("section")
    micro_count = grad_out.shape[0]
    tok_rows = grad_out.shape[1]
    local_width = grad_out.shape[2]
    capacity = hidden.shape[2]
    weights = down_weight[0]
    router = router_weight[0]
    inputs = layer_inputs[0]
    routes_all = expert_ids[0]
    stored_all = hidden[0]
    expert_count = router.shape[1]
    full_width = weights.shape[0]
    unit_count = weights.shape[1]
    slot_range = jnp.arange(capacity, dtype=jnp.int32)
    expert_range = jnp.arange(expert_count, dtype=jnp.int32)
    own_hot = (expert_range == 0).astype(jnp.float32)
    carried_width = grad_out.shape[2]

    def turn(turn_index, state_all):
        upstream, hid_buf, rows_buf, router_acc, final_buf = state_all
        micro_now = turn_index - (sections - 1 - my_section)
        active = (micro_now >= 0) & (micro_now < micro_count)
        which_micro = jnp.clip(micro_now, 0, micro_count - 1)
        seed_grad = lax.dynamic_index_in_dim(grad_out, which_micro, 0, keepdims=False)
        incoming = jnp.where(my_section == sections - 1, seed_grad, upstream)
        x_now = lax.dynamic_index_in_dim(inputs, which_micro, 0, keepdims=False)
        routes_now = lax.dynamic_index_in_dim(routes_all, which_micro, 0, keepdims=False)
        stored_now = lax.dynamic_index_in_dim(stored_all, which_micro, 0, keepdims=False)
        member = ((routes_now[:, 0] == 0) | (routes_now[:, 1] == 0)).astype(jnp.int32)
        position = jnp.cumsum(member) - member
        picks = (position[None, :] == slot_range[:, None]) & (member[None, :] > 0)
        pick_bf = picks.astype(jnp.bfloat16)
        pick_f = picks.astype(jnp.float32)
        local_rows = jnp.dot(pick_bf, incoming, preferred_element_type=jnp.float32).astype(
            jnp.bfloat16
        )
        logit_part = jnp.dot(x_now, router, preferred_element_type=jnp.float32)
        logits = lax.psum(logit_part, "dp")
        rows = lax.all_gather(local_rows, "dp", axis=1, tiled=True)
        product = jnp.dot(rows, weights, preferred_element_type=jnp.float32)
        score_part = jnp.sum(stored_now.astype(jnp.float32) * product, axis=1)
        score = lax.psum(score_part, "dp")
        other = jnp.where(routes_now[:, 0] == 0, routes_now[:, 1], routes_now[:, 0])
        other_hot = (other[:, None] == expert_range[None, :]).astype(jnp.float32)
        gate = 1.0 / (1.0 + jnp.exp(jnp.sum(other_hot * logits, axis=1) - logits[:, 0]))
        gate_slot = jnp.sum(pick_f * gate[None, :], axis=1)
        hidden_slot = (gate_slot[:, None] * product).astype(jnp.bfloat16)
        weighted = (gate_slot[:, None] * rows.astype(jnp.float32)).astype(jnp.bfloat16)
        token_score = jnp.sum(pick_f * score[:, None], axis=0)
        delta = gate * (1.0 - gate) * token_score
        logit_grads = (delta[:, None] * (own_hot[None, :] - other_hot)).astype(jnp.bfloat16)
        router_part = lax.dot_general(
            x_now, logit_grads, (((0,), (0,)), ((), ())), preferred_element_type=jnp.float32
        )
        passed = (
            incoming.astype(jnp.float32)
            + lax.dot_general(
                logit_grads, router, (((1,), (1,)), ((), ())), preferred_element_type=jnp.float32
            )
        ).astype(jnp.bfloat16)
        hid_buf = write_slice(hid_buf, which_micro, hidden_slot, active)
        rows_buf = write_slice(rows_buf, which_micro, weighted, active)
        router_acc = router_acc + jnp.where(active, router_part, 0.0)
        final_buf = write_slice(final_buf, which_micro, passed, active & (my_section == 0))
        upstream = from_behind(passed, "section", -1)
        return (upstream, hid_buf, rows_buf, router_acc, final_buf)

    start_state = (
        jnp.zeros((tok_rows, carried_width), jnp.bfloat16),
        jnp.zeros((micro_count, capacity, unit_count), jnp.bfloat16),
        jnp.zeros((micro_count, capacity, full_width), jnp.bfloat16),
        jnp.zeros((local_width, expert_count), jnp.float32),
        jnp.zeros((micro_count, tok_rows, carried_width), jnp.bfloat16),
    )
    end_state = lax.fori_loop(0, sections + micro_count - 1, turn, start_state)
    upstream, hid_buf, rows_buf, router_acc, final_buf = end_state
    weight_part = lax.dot_general(
        rows_buf, stored_all, (((0, 1), (0, 1)), ((), ())), preferred_element_type=jnp.float32
    )
    down_grad = weight_part.astype(jnp.bfloat16)[None]
    input_grad = lax.psum_scatter(
        final_buf.astype(jnp.float32).astype(jnp.bfloat16),
        "section",
        scatter_dimension=1,
        tiled=True,
    )
    return (input_grad, hid_buf[None], down_grad, router_acc[None])


def solution(mesh):
    return jax.shard_map(
        per_device,
        mesh=mesh,
        in_specs=(
            P("section", None, None, "dp"),
            P("section", None, None, None),
            P("section", None, None, "dp"),
            P("section", None, "dp"),
            P("section", "dp", None),
            P(None, None, "dp"),
        ),
        out_specs=(
            P(None, "section", "dp"),
            P("section", None, None, "dp"),
            P("section", None, "dp"),
            P("section", "dp", None),
        ),
        check_vma=False,
    )
```

profile of v0, /device:TPU:1, one launch (start us, length us, event | category | flops | bytes accessed | tf_op | source)
XLA Modules:
  0.0 814.2 jit_solution(366810827386209172)
XLA Ops:
  8.3 770.6 %while.24 = (s32[]{:T(128)}, bf16[64,384]{1,0:T(8,128)(2,1)S(1)}, bf16[4,32,512]{2,1,0:T(8,128)(2,1)S(1)}, bf16[4,32,6144]{2,1,0:T(8,128)(2,1)S(1)}, f32[384,8]{...) while((s32[]{:T(128)}, bf16[64,384]{1,0:T(8,128)(2,1)S(1)}, ...), condition=%wide.region_8.9_spmd.clone, body=%wide.region_0.8_spmd.clone.sunk | while | flops 205161344 | bytes 10185585 | solution.py:95
  9.8 21.1 %all_gather.11 = bf16[32,6144]{1,0:T(8,128)(2,1)S(1)} all-gather(bf16[32,384]{1,0:T(8,128)(2,1)S(1)} %convolution_convert_fusion.2), channel_id=1, replica_groups=mesh['section'=8,'dp'=16] {'dp'}, dimensions={1}, use_global_device_ids=true | all-gather | bytes 417792 | tf_op jit(solution)/shard_map/while/body/eval_jaxpr/all_gather | solution.py:59
  31.0 4.1 fusion.90
  35.0 31.4 %all-reduce.2 = (f32[64,8]{0,1:T(8,128)S(1)}, f32[32]{0:T(128)S(1)}) all-reduce(f32[64,8]{0,1:T(8,128)S(1)} %fusion.87, f32[32]{0:T(128)S(1)} %get-tuple-element.583), channel_id=1, replica_groups=mesh['section'=8,'dp'=16] {'dp'}, use_global_device_ids=true, to_apply=%region_1.1 | all-reduce | flops 544 | bytes 4352 | tf_op jit(solution)/shard_map/while/body/eval_jaxpr/psum | solution.py:58
  66.9 15.0 %collective-permute-start = (bf16[64,384]{1,0:T(8,128)(2,1)S(1)}, bf16[64,384]{1,0:T(8,128)(2,1)S(1)}, u32[]{:S(2)}, u32[]{:S(2)}) collective-permute-start(bf16[64,384]{1,0:T(8,128)(2,1)S(1)} %get-tuple-element.587), channel_id=1, source_target_pairs={{16,0},{32,16},{48,32},{64,48},{80,64},{96,80},{112,96},{17,1},{33... | collective-permute-start | bytes 147464 | tf_op jit(solution)/shard_map/while/body/eval_jaxpr/ppermute | solution.py:10
  86.3 15.7 %all_gather.11 = bf16[32,6144]{1,0:T(8,128)(2,1)S(1)} all-gather(bf16[32,384]{1,0:T(8,128)(2,1)S(1)} %convolution_convert_fusion.2), channel_id=1, replica_groups=mesh['section'=8,'dp'=16] {'dp'}, dimensions={1}, use_global_device_ids=true | all-gather | bytes 417792 | tf_op jit(solution)/shard_map/while/body/eval_jaxpr/all_gather | solution.py:59
  106.2 31.5 %all-reduce.2 = (f32[64,8]{0,1:T(8,128)S(1)}, f32[32]{0:T(128)S(1)}) all-reduce(f32[64,8]{0,1:T(8,128)S(1)} %fusion.87, f32[32]{0:T(128)S(1)} %get-tuple-element.583), channel_id=1, replica_groups=mesh['section'=8,'dp'=16] {'dp'}, use_global_device_ids=true, to_apply=%region_1.1 | all-reduce | flops 544 | bytes 4352 | tf_op jit(solution)/shard_map/while/body/eval_jaxpr/psum | solution.py:58
  138.1 12.6 %collective-permute-start = (bf16[64,384]{1,0:T(8,128)(2,1)S(1)}, bf16[64,384]{1,0:T(8,128)(2,1)S(1)}, u32[]{:S(2)}, u32[]{:S(2)}) collective-permute-start(bf16[64,384]{1,0:T(8,128)(2,1)S(1)} %get-tuple-element.587), channel_id=1, source_target_pairs={{16,0},{32,16},{48,32},{64,48},{80,64},{96,80},{112,96},{17,1},{33... | collective-permute-start | bytes 147464 | tf_op jit(solution)/shard_map/while/body/eval_jaxpr/ppermute | solution.py:10
  155.7 16.7 %all_gather.11 = bf16[32,6144]{1,0:T(8,128)(2,1)S(1)} all-gather(bf16[32,384]{1,0:T(8,128)(2,1)S(1)} %convolution_convert_fusion.2), channel_id=1, replica_groups=mesh['section'=8,'dp'=16] {'dp'}, dimensions={1}, use_global_device_ids=true | all-gather | bytes 417792 | tf_op jit(solution)/shard_map/while/body/eval_jaxpr/all_gather | solution.py:59
  172.5 4.1 fusion.90
  176.6 31.7 %all-reduce.2 = (f32[64,8]{0,1:T(8,128)S(1)}, f32[32]{0:T(128)S(1)}) all-reduce(f32[64,8]{0,1:T(8,128)S(1)} %fusion.87, f32[32]{0:T(128)S(1)} %get-tuple-element.583), channel_id=1, replica_groups=mesh['section'=8,'dp'=16] {'dp'}, use_global_device_ids=true, to_apply=%region_1.1 | all-reduce | flops 544 | bytes 4352 | tf_op jit(solution)/shard_map/while/body/eval_jaxpr/psum | solution.py:58
  208.7 10.9 %collective-permute-start = (bf16[64,384]{1,0:T(8,128)(2,1)S(1)}, bf16[64,384]{1,0:T(8,128)(2,1)S(1)}, u32[]{:S(2)}, u32[]{:S(2)}) collective-permute-start(bf16[64,384]{1,0:T(8,128)(2,1)S(1)} %get-tuple-element.587), channel_id=1, source_target_pairs={{16,0},{32,16},{48,32},{64,48},{80,64},{96,80},{112,96},{17,1},{33... | collective-permute-start | bytes 147464 | tf_op jit(solution)/shard_map/while/body/eval_jaxpr/ppermute | solution.py:10
  225.1 16.6 %all_gather.11 = bf16[32,6144]{1,0:T(8,128)(2,1)S(1)} all-gather(bf16[32,384]{1,0:T(8,128)(2,1)S(1)} %convolution_convert_fusion.2), channel_id=1, replica_groups=mesh['section'=8,'dp'=16] {'dp'}, dimensions={1}, use_global_device_ids=true | all-gather | bytes 417792 | tf_op jit(solution)/shard_map/while/body/eval_jaxpr/all_gather | solution.py:59
  245.9 31.5 %all-reduce.2 = (f32[64,8]{0,1:T(8,128)S(1)}, f32[32]{0:T(128)S(1)}) all-reduce(f32[64,8]{0,1:T(8,128)S(1)} %fusion.87, f32[32]{0:T(128)S(1)} %get-tuple-element.583), channel_id=1, replica_groups=mesh['section'=8,'dp'=16] {'dp'}, use_global_device_ids=true, to_apply=%region_1.1 | all-reduce | flops 544 | bytes 4352 | tf_op jit(solution)/shard_map/while/body/eval_jaxpr/psum | solution.py:58
  277.9 10.9 %collective-permute-start = (bf16[64,384]{1,0:T(8,128)(2,1)S(1)}, bf16[64,384]{1,0:T(8,128)(2,1)S(1)}, u32[]{:S(2)}, u32[]{:S(2)}) collective-permute-start(bf16[64,384]{1,0:T(8,128)(2,1)S(1)} %get-tuple-element.587), channel_id=1, source_target_pairs={{16,0},{32,16},{48,32},{64,48},{80,64},{96,80},{112,96},{17,1},{33... | collective-permute-start | bytes 147464 | tf_op jit(solution)/shard_map/while/body/eval_jaxpr/ppermute | solution.py:10
  294.6 16.7 %all_gather.11 = bf16[32,6144]{1,0:T(8,128)(2,1)S(1)} all-gather(bf16[32,384]{1,0:T(8,128)(2,1)S(1)} %convolution_convert_fusion.2), channel_id=1, replica_groups=mesh['section'=8,'dp'=16] {'dp'}, dimensions={1}, use_global_device_ids=true | all-gather | bytes 417792 | tf_op jit(solution)/shard_map/while/body/eval_jaxpr/all_gather | solution.py:59
  315.5 31.1 %all-reduce.2 = (f32[64,8]{0,1:T(8,128)S(1)}, f32[32]{0:T(128)S(1)}) all-reduce(f32[64,8]{0,1:T(8,128)S(1)} %fusion.87, f32[32]{0:T(128)S(1)} %get-tuple-element.583), channel_id=1, replica_groups=mesh['section'=8,'dp'=16] {'dp'}, use_global_device_ids=true, to_apply=%region_1.1 | all-reduce | flops 544 | bytes 4352 | tf_op jit(solution)/shard_map/while/body/eval_jaxpr/psum | solution.py:58
  347.0 10.8 %collective-permute-start = (bf16[64,384]{1,0:T(8,128)(2,1)S(1)}, bf16[64,384]{1,0:T(8,128)(2,1)S(1)}, u32[]{:S(2)}, u32[]{:S(2)}) collective-permute-start(bf16[64,384]{1,0:T(8,128)(2,1)S(1)} %get-tuple-element.587), channel_id=1, source_target_pairs={{16,0},{32,16},{48,32},{64,48},{80,64},{96,80},{112,96},{17,1},{33... | collective-permute-start | bytes 147464 | tf_op jit(solution)/shard_map/while/body/eval_jaxpr/ppermute | solution.py:10
  358.4 4.1 collective-permute-done
  364.0 16.1 %all_gather.11 = bf16[32,6144]{1,0:T(8,128)(2,1)S(1)} all-gather(bf16[32,384]{1,0:T(8,128)(2,1)S(1)} %convolution_convert_fusion.2), channel_id=1, replica_groups=mesh['section'=8,'dp'=16] {'dp'}, dimensions={1}, use_global_device_ids=true | all-gather | bytes 417792 | tf_op jit(solution)/shard_map/while/body/eval_jaxpr/all_gather | solution.py:59
  380.2 4.1 fusion.90
  384.3 31.4 %all-reduce.2 = (f32[64,8]{0,1:T(8,128)S(1)}, f32[32]{0:T(128)S(1)}) all-reduce(f32[64,8]{0,1:T(8,128)S(1)} %fusion.87, f32[32]{0:T(128)S(1)} %get-tuple-element.583), channel_id=1, replica_groups=mesh['section'=8,'dp'=16] {'dp'}, use_global_device_ids=true, to_apply=%region_1.1 | all-reduce | flops 544 | bytes 4352 | tf_op jit(solution)/shard_map/while/body/eval_jaxpr/psum | solution.py:58
  416.1 10.6 %collective-permute-start = (bf16[64,384]{1,0:T(8,128)(2,1)S(1)}, bf16[64,384]{1,0:T(8,128)(2,1)S(1)}, u32[]{:S(2)}, u32[]{:S(2)}) collective-permute-start(bf16[64,384]{1,0:T(8,128)(2,1)S(1)} %get-tuple-element.587), channel_id=1, source_target_pairs={{16,0},{32,16},{48,32},{64,48},{80,64},{96,80},{112,96},{17,1},{33... | collective-permute-start | bytes 147464 | tf_op jit(solution)/shard_map/while/body/eval_jaxpr/ppermute | solution.py:10
  427.3 4.5 collective-permute-done
  433.3 16.6 %all_gather.11 = bf16[32,6144]{1,0:T(8,128)(2,1)S(1)} all-gather(bf16[32,384]{1,0:T(8,128)(2,1)S(1)} %convolution_convert_fusion.2), channel_id=1, replica_groups=mesh['section'=8,'dp'=16] {'dp'}, dimensions={1}, use_global_device_ids=true | all-gather | bytes 417792 | tf_op jit(solution)/shard_map/while/body/eval_jaxpr/all_gather | solution.py:59
  450.1 4.1 fusion.90
  454.1 31.3 %all-reduce.2 = (f32[64,8]{0,1:T(8,128)S(1)}, f32[32]{0:T(128)S(1)}) all-reduce(f32[64,8]{0,1:T(8,128)S(1)} %fusion.87, f32[32]{0:T(128)S(1)} %get-tuple-element.583), channel_id=1, replica_groups=mesh['section'=8,'dp'=16] {'dp'}, use_global_device_ids=true, to_apply=%region_1.1 | all-reduce | flops 544 | bytes 4352 | tf_op jit(solution)/shard_map/while/body/eval_jaxpr/psum | solution.py:58
  486.0 9.8 %collective-permute-start = (bf16[64,384]{1,0:T(8,128)(2,1)S(1)}, bf16[64,384]{1,0:T(8,128)(2,1)S(1)}, u32[]{:S(2)}, u32[]{:S(2)}) collective-permute-start(bf16[64,384]{1,0:T(8,128)(2,1)S(1)} %get-tuple-element.587), channel_id=1, source_target_pairs={{16,0},{32,16},{48,32},{64,48},{80,64},{96,80},{112,96},{17,1},{33... | collective-permute-start | bytes 147464 | tf_op jit(solution)/shard_map/while/body/eval_jaxpr/ppermute | solution.py:10
  496.3 4.9 collective-permute-done
  502.7 16.1 %all_gather.11 = bf16[32,6144]{1,0:T(8,128)(2,1)S(1)} all-gather(bf16[32,384]{1,0:T(8,128)(2,1)S(1)} %convolution_convert_fusion.2), channel_id=1, replica_groups=mesh['section'=8,'dp'=16] {'dp'}, dimensions={1}, use_global_device_ids=true | all-gather | bytes 417792 | tf_op jit(solution)/shard_map/while/body/eval_jaxpr/all_gather | solution.py:59
  518.9 4.1 fusion.90
  523.0 31.4 %all-reduce.2 = (f32[64,8]{0,1:T(8,128)S(1)}, f32[32]{0:T(128)S(1)}) all-reduce(f32[64,8]{0,1:T(8,128)S(1)} %fusion.87, f32[32]{0:T(128)S(1)} %get-tuple-element.583), channel_id=1, replica_groups=mesh['section'=8,'dp'=16] {'dp'}, use_global_device_ids=true, to_apply=%region_1.1 | all-reduce | flops 544 | bytes 4352 | tf_op jit(solution)/shard_map/while/body/eval_jaxpr/psum | solution.py:58
  554.9 9.9 %collective-permute-start = (bf16[64,384]{1,0:T(8,128)(2,1)S(1)}, bf16[64,384]{1,0:T(8,128)(2,1)S(1)}, u32[]{:S(2)}, u32[]{:S(2)}) collective-permute-start(bf16[64,384]{1,0:T(8,128)(2,1)S(1)} %get-tuple-element.587), channel_id=1, source_target_pairs={{16,0},{32,16},{48,32},{64,48},{80,64},{96,80},{112,96},{17,1},{33... | collective-permute-start | bytes 147464 | tf_op jit(solution)/shard_map/while/body/eval_jaxpr/ppermute | solution.py:10
  565.3 5.4 collective-permute-done
  572.2 16.4 %all_gather.11 = bf16[32,6144]{1,0:T(8,128)(2,1)S(1)} all-gather(bf16[32,384]{1,0:T(8,128)(2,1)S(1)} %convolution_convert_fusion.2), channel_id=1, replica_groups=mesh['section'=8,'dp'=16] {'dp'}, dimensions={1}, use_global_device_ids=true | all-gather | bytes 417792 | tf_op jit(solution)/shard_map/while/body/eval_jaxpr/all_gather | solution.py:59
  592.8 31.5 %all-reduce.2 = (f32[64,8]{0,1:T(8,128)S(1)}, f32[32]{0:T(128)S(1)}) all-reduce(f32[64,8]{0,1:T(8,128)S(1)} %fusion.87, f32[32]{0:T(128)S(1)} %get-tuple-element.583), channel_id=1, replica_groups=mesh['section'=8,'dp'=16] {'dp'}, use_global_device_ids=true, to_apply=%region_1.1 | all-reduce | flops 544 | bytes 4352 | tf_op jit(solution)/shard_map/while/body/eval_jaxpr/psum | solution.py:58
  624.8 9.2 %collective-permute-start = (bf16[64,384]{1,0:T(8,128)(2,1)S(1)}, bf16[64,384]{1,0:T(8,128)(2,1)S(1)}, u32[]{:S(2)}, u32[]{:S(2)}) collective-permute-start(bf16[64,384]{1,0:T(8,128)(2,1)S(1)} %get-tuple-element.587), channel_id=1, source_target_pairs={{16,0},{32,16},{48,32},{64,48},{80,64},{96,80},{112,96},{17,1},{33... | collective-permute-start | bytes 147464 | tf_op jit(solution)/shard_map/while/body/eval_jaxpr/ppermute | solution.py:10
  634.5 5.5 collective-permute-done
  641.5 16.3 %all_gather.11 = bf16[32,6144]{1,0:T(8,128)(2,1)S(1)} all-gather(bf16[32,384]{1,0:T(8,128)(2,1)S(1)} %convolution_convert_fusion.2), channel_id=1, replica_groups=mesh['section'=8,'dp'=16] {'dp'}, dimensions={1}, use_global_device_ids=true | all-gather | bytes 417792 | tf_op jit(solution)/shard_map/while/body/eval_jaxpr/all_gather | solution.py:59
  662.0 31.4 %all-reduce.2 = (f32[64,8]{0,1:T(8,128)S(1)}, f32[32]{0:T(128)S(1)}) all-reduce(f32[64,8]{0,1:T(8,128)S(1)} %fusion.87, f32[32]{0:T(128)S(1)} %get-tuple-element.583), channel_id=1, replica_groups=mesh['section'=8,'dp'=16] {'dp'}, use_global_device_ids=true, to_apply=%region_1.1 | all-reduce | flops 544 | bytes 4352 | tf_op jit(solution)/shard_map/while/body/eval_jaxpr/psum | solution.py:58
  693.9 9.2 %collective-permute-start = (bf16[64,384]{1,0:T(8,128)(2,1)S(1)}, bf16[64,384]{1,0:T(8,128)(2,1)S(1)}, u32[]{:S(2)}, u32[]{:S(2)}) collective-permute-start(bf16[64,384]{1,0:T(8,128)(2,1)S(1)} %get-tuple-element.587), channel_id=1, source_target_pairs={{16,0},{32,16},{48,32},{64,48},{80,64},{96,80},{112,96},{17,1},{33... | collective-permute-start | bytes 147464 | tf_op jit(solution)/shard_map/while/body/eval_jaxpr/ppermute | solution.py:10
  703.6 5.8 collective-permute-done
  710.9 16.0 %all_gather.11 = bf16[32,6144]{1,0:T(8,128)(2,1)S(1)} all-gather(bf16[32,384]{1,0:T(8,128)(2,1)S(1)} %convolution_convert_fusion.2), channel_id=1, replica_groups=mesh['section'=8,'dp'=16] {'dp'}, dimensions={1}, use_global_device_ids=true | all-gather | bytes 417792 | tf_op jit(solution)/shard_map/while/body/eval_jaxpr/all_gather | solution.py:59
  731.1 31.4 %all-reduce.2 = (f32[64,8]{0,1:T(8,128)S(1)}, f32[32]{0:T(128)S(1)}) all-reduce(f32[64,8]{0,1:T(8,128)S(1)} %fusion.87, f32[32]{0:T(128)S(1)} %get-tuple-element.583), channel_id=1, replica_groups=mesh['section'=8,'dp'=16] {'dp'}, use_global_device_ids=true, to_apply=%region_1.1 | all-reduce | flops 544 | bytes 4352 | tf_op jit(solution)/shard_map/while/body/eval_jaxpr/psum | solution.py:58
  762.9 9.1 %collective-permute-start = (bf16[64,384]{1,0:T(8,128)(2,1)S(1)}, bf16[64,384]{1,0:T(8,128)(2,1)S(1)}, u32[]{:S(2)}, u32[]{:S(2)}) collective-permute-start(bf16[64,384]{1,0:T(8,128)(2,1)S(1)} %get-tuple-element.587), channel_id=1, source_target_pairs={{16,0},{32,16},{48,32},{64,48},{80,64},{96,80},{112,96},{17,1},{33... | collective-permute-start | bytes 147464 | tf_op jit(solution)/shard_map/while/body/eval_jaxpr/ppermute | solution.py:10
  772.5 6.3 collective-permute-done
  779.8 4.5 fusion.51
  784.3 21.7 %reduce-scatter.4.cloned.1.call-done = bf16[8,1536]{1,0:T(8,128)(2,1)} async-done(((bf16[64,1536]{1,0:T(8,128)(2,1)}), bf16[8,1536]{1,0:T(8,128)(2,1)}) %reduce-scatter.4.cloned.1.call-update) | async-done | bytes 24592
  (275 shorter events, 68.1 us)
Async XLA Ops:
  7.2 0.9 copy-start.5
  7.2 1.0 copy-start.1
  7.2 1.0 copy-start.3
  7.2 1.1 copy-start
  7.2 798.8 %reduce-scatter.4.cloned.1.call-start = ((), (), s32[]{:S(2)}) async-start(), calls=%async_computation.1 | async-start | bytes 221184
  66.9 17.9 %collective-permute-start = (bf16[64,384]{1,0:T(8,128)(2,1)S(1)}, bf16[64,384]{1,0:T(8,128)(2,1)S(1)}, u32[]{:S(2)}, u32[]{:S(2)}) collective-permute-start(bf16[64,384]{1,0:T(8,128)(2,1)S(1)} %get-tuple-element.587), channel_id=1, source_target_pairs={{16,0},{32,16},{48,32},{64,48},{80,64},{96,80},{112,96},{17,1},{33... | collective-permute-start | bytes 147464 | tf_op jit(solution)/shard_map/while/body/eval_jaxpr/ppermute | solution.py:10
  138.1 16.1 %collective-permute-start = (bf16[64,384]{1,0:T(8,128)(2,1)S(1)}, bf16[64,384]{1,0:T(8,128)(2,1)S(1)}, u32[]{:S(2)}, u32[]{:S(2)}) collective-permute-start(bf16[64,384]{1,0:T(8,128)(2,1)S(1)} %get-tuple-element.587), channel_id=1, source_target_pairs={{16,0},{32,16},{48,32},{64,48},{80,64},{96,80},{112,96},{17,1},{33... | collective-permute-start | bytes 147464 | tf_op jit(solution)/shard_map/while/body/eval_jaxpr/ppermute | solution.py:10
  208.7 14.9 %collective-permute-start = (bf16[64,384]{1,0:T(8,128)(2,1)S(1)}, bf16[64,384]{1,0:T(8,128)(2,1)S(1)}, u32[]{:S(2)}, u32[]{:S(2)}) collective-permute-start(bf16[64,384]{1,0:T(8,128)(2,1)S(1)} %get-tuple-element.587), channel_id=1, source_target_pairs={{16,0},{32,16},{48,32},{64,48},{80,64},{96,80},{112,96},{17,1},{33... | collective-permute-start | bytes 147464 | tf_op jit(solution)/shard_map/while/body/eval_jaxpr/ppermute | solution.py:10
  277.9 15.2 %collective-permute-start = (bf16[64,384]{1,0:T(8,128)(2,1)S(1)}, bf16[64,384]{1,0:T(8,128)(2,1)S(1)}, u32[]{:S(2)}, u32[]{:S(2)}) collective-permute-start(bf16[64,384]{1,0:T(8,128)(2,1)S(1)} %get-tuple-element.587), channel_id=1, source_target_pairs={{16,0},{32,16},{48,32},{64,48},{80,64},{96,80},{112,96},{17,1},{33... | collective-permute-start | bytes 147464 | tf_op jit(solution)/shard_map/while/body/eval_jaxpr/ppermute | solution.py:10
  347.0 15.4 %collective-permute-start = (bf16[64,384]{1,0:T(8,128)(2,1)S(1)}, bf16[64,384]{1,0:T(8,128)(2,1)S(1)}, u32[]{:S(2)}, u32[]{:S(2)}) collective-permute-start(bf16[64,384]{1,0:T(8,128)(2,1)S(1)} %get-tuple-element.587), channel_id=1, source_target_pairs={{16,0},{32,16},{48,32},{64,48},{80,64},{96,80},{112,96},{17,1},{33... | collective-permute-start | bytes 147464 | tf_op jit(solution)/shard_map/while/body/eval_jaxpr/ppermute | solution.py:10
  416.1 15.7 %collective-permute-start = (bf16[64,384]{1,0:T(8,128)(2,1)S(1)}, bf16[64,384]{1,0:T(8,128)(2,1)S(1)}, u32[]{:S(2)}, u32[]{:S(2)}) collective-permute-start(bf16[64,384]{1,0:T(8,128)(2,1)S(1)} %get-tuple-element.587), channel_id=1, source_target_pairs={{16,0},{32,16},{48,32},{64,48},{80,64},{96,80},{112,96},{17,1},{33... | collective-permute-start | bytes 147464 | tf_op jit(solution)/shard_map/while/body/eval_jaxpr/ppermute | solution.py:10
  486.0 15.2 %collective-permute-start = (bf16[64,384]{1,0:T(8,128)(2,1)S(1)}, bf16[64,384]{1,0:T(8,128)(2,1)S(1)}, u32[]{:S(2)}, u32[]{:S(2)}) collective-permute-start(bf16[64,384]{1,0:T(8,128)(2,1)S(1)} %get-tuple-element.587), channel_id=1, source_target_pairs={{16,0},{32,16},{48,32},{64,48},{80,64},{96,80},{112,96},{17,1},{33... | collective-permute-start | bytes 147464 | tf_op jit(solution)/shard_map/while/body/eval_jaxpr/ppermute | solution.py:10
  554.9 15.8 %collective-permute-start = (bf16[64,384]{1,0:T(8,128)(2,1)S(1)}, bf16[64,384]{1,0:T(8,128)(2,1)S(1)}, u32[]{:S(2)}, u32[]{:S(2)}) collective-permute-start(bf16[64,384]{1,0:T(8,128)(2,1)S(1)} %get-tuple-element.587), channel_id=1, source_target_pairs={{16,0},{32,16},{48,32},{64,48},{80,64},{96,80},{112,96},{17,1},{33... | collective-permute-start | bytes 147464 | tf_op jit(solution)/shard_map/while/body/eval_jaxpr/ppermute | solution.py:10
  624.8 15.3 %collective-permute-start = (bf16[64,384]{1,0:T(8,128)(2,1)S(1)}, bf16[64,384]{1,0:T(8,128)(2,1)S(1)}, u32[]{:S(2)}, u32[]{:S(2)}) collective-permute-start(bf16[64,384]{1,0:T(8,128)(2,1)S(1)} %get-tuple-element.587), channel_id=1, source_target_pairs={{16,0},{32,16},{48,32},{64,48},{80,64},{96,80},{112,96},{17,1},{33... | collective-permute-start | bytes 147464 | tf_op jit(solution)/shard_map/while/body/eval_jaxpr/ppermute | solution.py:10
  693.9 15.5 %collective-permute-start = (bf16[64,384]{1,0:T(8,128)(2,1)S(1)}, bf16[64,384]{1,0:T(8,128)(2,1)S(1)}, u32[]{:S(2)}, u32[]{:S(2)}) collective-permute-start(bf16[64,384]{1,0:T(8,128)(2,1)S(1)} %get-tuple-element.587), channel_id=1, source_target_pairs={{16,0},{32,16},{48,32},{64,48},{80,64},{96,80},{112,96},{17,1},{33... | collective-permute-start | bytes 147464 | tf_op jit(solution)/shard_map/while/body/eval_jaxpr/ppermute | solution.py:10
  762.9 15.9 %collective-permute-start = (bf16[64,384]{1,0:T(8,128)(2,1)S(1)}, bf16[64,384]{1,0:T(8,128)(2,1)S(1)}, u32[]{:S(2)}, u32[]{:S(2)}) collective-permute-start(bf16[64,384]{1,0:T(8,128)(2,1)S(1)} %get-tuple-element.587), channel_id=1, source_target_pairs={{16,0},{32,16},{48,32},{64,48},{80,64},{96,80},{112,96},{17,1},{33... | collective-permute-start | bytes 147464 | tf_op jit(solution)/shard_map/while/body/eval_jaxpr/ppermute | solution.py:10
  778.9 5.4 copy-start.2
  778.9 5.4 copy-start.4
Sparse Core Ops, SparseCore 0:
  779.9 26.1 reduce-scatter.3
where the time goes:
time: 818 us; the launch traced here: 814 us
  blocking collectives  530 us (65%)
  starting transfers between devices  118 us (14%)
  waiting for transfers between devices  70.8 us (9%)
  matrix products  57.5 us (7%)
  between operations  14.1 us (2%)
  local copies, waits for them, and re-layouts  13.6 us (2%)
  other arithmetic  9.5 us (1%)
    psum x11, blocking collectives, turn(): logits = lax.psum(logit_part, 'dp')  345 us
    all_gather x11, blocking collectives, turn(): rows = lax.all_gather(local_rows, 'dp', axis=1, tiled=True)  184 us
    ppermute x11, starting transfers between devices, from_behind(): lax.ppermute(value, axis, [(source, source + steps) for source in range(i...  118 us
    ppermute x11, waiting for transfers between devices, from_behind(): lax.ppermute(value, axis, [(source, source + steps) for source in range(i...  49 us
    dot_general x11, matrix products, turn(): product = jnp.dot(rows, weights, preferred_element_type=jnp.float32)  44.9 us
    unnamed x2, waiting for transfers between devices  21.8 us
  transfers between devices with their start and end apart: 12, of which 12 were waited for; matrix products, arithmetic and copies ran while one was open for 1% of the time, Pallas kernels for 0%

commit v1 on v0

v1 whole, which is shorter than its diff:
```python
import jax
import jax.numpy as jnp
from jax import lax
from jax.sharding import PartitionSpec as P

F32 = jnp.float32
BF16 = jnp.bfloat16


def nt(a, b):
    return lax.dot_general(a, b, (((1,), (1,)), ((), ())), preferred_element_type=F32)


def tn(a, b):
    return lax.dot_general(a, b, (((0,), (0,)), ((), ())), preferred_element_type=F32)


def nn(a, b):
    return jnp.dot(a, b, preferred_element_type=F32)


def to_all(value, axes, count):
    copies = jnp.broadcast_to(value[None], (count,) + value.shape)
    return lax.all_to_all(copies, axes, 0, 0, tiled=True)


def pieces(value):
    first = lax.reduce_precision(value, 8, 7)
    rest = value - first
    second = lax.reduce_precision(rest, 8, 7)
    return [first.astype(BF16), second.astype(BF16), (rest - second).astype(BF16)]


def slot_picks(codes, micro, tok, cap):
    tokens = micro * tok
    row = lax.broadcasted_iota(jnp.int32, (tokens, tokens), 0)
    col = lax.broadcasted_iota(jnp.int32, (tokens, tokens), 1)
    before = ((row < col) & (row // tok == col // tok)).astype(BF16)
    member = codes > 0.0
    rank = nn(member.astype(BF16), before).astype(jnp.int32)
    base = (lax.broadcasted_iota(jnp.int32, (1, tokens), 1) // tok) * cap
    slot = jnp.where(member, rank + base, -1)
    slots = lax.broadcasted_iota(jnp.int32, (1, micro * cap, 1), 1)
    return (slot[:, None, :] == slots).astype(BF16)


def per_device(layer_inputs, expert_ids, hidden, down_weight, router_weight, grad_out):
    sections, ways = lax.axis_size("section"), lax.axis_size("dp")
    me = lax.axis_index("section")
    micro, tok, width = grad_out.shape
    cap, units = hidden.shape[2:]
    experts = router_weight.shape[2]
    tokens, slots = micro * tok, micro * cap
    x = layer_inputs[0].reshape(tokens, width)
    ids = expert_ids[0].reshape(tokens, 2)
    hid = hidden[0].reshape(slots, units)
    weights = down_weight[0].reshape(ways, width, units)
    router = router_weight[0].T
    grads = grad_out.reshape(tokens, width)

    other = jnp.where(ids[:, 0] == 0, ids[:, 1], ids[:, 0])
    member = (ids[:, 0] == 0) | (ids[:, 1] == 0)
    code = jnp.where(member, other, 0).astype(F32)
    code_row = jnp.pad(code.astype(BF16), (0, width - tokens))[None]
    got = to_all(jnp.concatenate([router, code_row]), "section", sections)
    routers = got[:, :experts]
    codes = got[:, experts, :tokens].astype(F32)
    picks = slot_picks(codes, micro, tok, cap)
    pick = slot_picks(code[None], micro, tok, cap)[0]

    expert_col = jnp.arange(experts, dtype=F32)[:, None]
    sign_own = (expert_col == 0).astype(F32) - (expert_col == code[None]).astype(F32)
    apart = -jnp.sum(sign_own * nt(router, x), axis=0)
    parts = jnp.stack(pieces(apart))
    parts = jnp.pad(nt(parts, pick).astype(BF16), ((0, experts - 3), (0, width - slots)))
    rows = nn(pick, grads).astype(BF16)
    block = jnp.concatenate([rows, routers[1:].reshape(-1, width), parts])
    got = to_all(block, "dp", ways)

    both = jnp.einsum("pkd,pdf->kf", got, weights, preferred_element_type=F32)
    product, mixed = both[:slots], both[slots:-experts]
    apart = jnp.sum(got[:, -experts:, :slots].astype(F32), axis=(0, 1))
    filled = jnp.sum(pick.astype(F32), axis=1)
    gate = filled / (1.0 + jnp.exp(apart))
    base = jnp.sum(hid.astype(F32) * product, axis=1)
    cross = nt(mixed.astype(BF16), hid).reshape(sections - 1, experts, slots)
    code_slot = nt(codes.astype(BF16), pick)
    signs = (expert_col == 0).astype(F32)[None] - (
        expert_col[None] == code_slot[:, None, :]
    ).astype(F32)
    above = jnp.arange(sections) > me
    signs = jnp.where(above[:, None, None], signs, 0.0)[1:]
    coefs = jnp.sum(signs * cross, axis=1)
    table = jnp.concatenate([base[None], coefs]) * (gate * (1.0 - gate))[None]
    got_table = to_all(table, ("section", "dp"), sections * ways)
    table = jnp.sum(got_table.reshape(sections, ways, sections, slots), axis=1)

    table = jnp.einsum(
        "skc,sct->skt", table, picks.astype(F32), precision=lax.Precision.HIGHEST
    )
    deltas = [None] * sections
    for layer in range(sections - 1, -1, -1):
        value = table[layer, 0]
        for upper in range(layer + 1, sections):
            value = value + deltas[upper] * table[layer, upper]
        deltas[layer] = lax.reduce_precision(value, 8, 7)
    deltas = jnp.stack(deltas)

    delta_slot = nt(deltas.astype(BF16), pick)
    lift = (signs * delta_slot[1:, None, :]).reshape(-1, slots).astype(BF16)
    scaled = (gate[:, None] * hid.astype(F32)).astype(BF16)
    right = jnp.concatenate([scaled, nn(lift, scaled).astype(BF16)])
    down_grad = jnp.einsum(
        "pkd,kf->pdf", got[:, :-experts], right, preferred_element_type=F32
    ).astype(BF16)
    hidden_grad = (gate[:, None] * (product + tn(lift, mixed.astype(BF16)))).astype(BF16)

    delta_own = lax.dynamic_index_in_dim(deltas, me, 0, keepdims=True)
    router_grad = nt(x.T, (sign_own * delta_own).astype(BF16))
    mine = tok // sections
    tokens_own = lambda a: lax.dynamic_slice_in_dim(
        a.reshape(a.shape[:-1] + (micro, tok)), me * mine, mine, axis=a.ndim
    )
    code_mine = tokens_own(codes).reshape(sections, 1, micro * mine)
    sign_mine = (expert_col == 0).astype(F32)[None] - (expert_col[None] == code_mine).astype(F32)
    logit_grads = sign_mine * tokens_own(deltas).reshape(sections, 1, micro * mine)
    step = tn(
        logit_grads.reshape(sections * experts, -1).astype(BF16),
        routers.reshape(sections * experts, width),
    )
    grads_mine = lax.dynamic_slice_in_dim(grad_out, me * mine, mine, axis=1)
    input_grad = (grads_mine.astype(F32) + step.reshape(micro, mine, width)).astype(BF16)
    return (
        input_grad,
        hidden_grad.reshape(1, micro, cap, units),
        down_grad.reshape(1, ways * width, units),
        router_grad[None],
    )


def solution(mesh):
    return jax.shard_map(
        per_device,
        mesh=mesh,
        in_specs=(
            P("section", None, None, "dp"),
            P("section", None, None, None),
            P("section", None, None, "dp"),
            P("section", None, "dp"),
            P("section", "dp", None),
            P(None, None, "dp"),
        ),
        out_specs=(
            P(None, "section", "dp"),
            P("section", None, None, "dp"),
            P("section", None, "dp"),
            P("section", "dp", None),
        ),
        check_vma=False,
    )
```

time: 818 us -> 98.4 us (0.12)
  blocking collectives: 530 us -> 0 us
  starting transfers between devices: 118 us -> 19.8 us
  matrix products: 57.5 us -> 17.8 us
  waiting for transfers between devices: 70.8 us -> 49.3 us
  between operations: 14.1 us -> 0.89 us
    psum x11 -> x0, blocking collectives: 345 us -> none  [turn(): logits = lax.psum(logit_part, 'dp')]
    all_gather x11 -> x0, blocking collectives: 184 us -> none  [turn(): rows = lax.all_gather(local_rows, 'dp', axis=1, tiled=True)]
    ppermute x11 -> x0, starting transfers between devices: 118 us -> none  [from_behind(): lax.ppermute(value, axis, [(source, source + steps) for source in range(i...]
    all_to_all x0 -> x3, waiting for transfers between devices: none -> 49.3 us  [to_all(): return lax.all_to_all(copies, axes, 0, 0, tiled=True)]
    ppermute x11 -> x0, waiting for transfers between devices: 49 us -> none  [from_behind(): lax.ppermute(value, axis, [(source, source + steps) for source in range(i...]
    dot_general x56 -> x15, matrix products: 57.5 us -> 17.8 us  [the longest x1 5.61 us: per_device(): jnp.einsum('pkd,kf->pdf', got[:, :-experts], right, preferred_element_typ...]
    unnamed x2 -> x0, waiting for transfers between devices: 21.8 us -> none
    all_to_all x0 -> x3, starting transfers between devices: none -> 19.8 us  [to_all(): return lax.all_to_all(copies, axes, 0, 0, tiled=True)]
  transfers between devices with their start and end apart: 12 -> 3, of which waited for: 12 -> 3; matrix products, arithmetic and copies ran while one was open for 1% -> 4% of each run, Pallas kernels for 0% -> 0%
where the time goes in v1:
time: 98.4 us; the launch traced here: 97.9 us
  waiting for transfers between devices  49.3 us (50%)
  starting transfers between devices  19.8 us (20%)
  matrix products  17.8 us (18%)
  local copies, waits for them, and re-layouts  7.89 us (8%)
  other arithmetic  2.12 us (2%)
    all_to_all x3, waiting for transfers between devices, to_all(): return lax.all_to_all(copies, axes, 0, 0, tiled=True)  49.3 us
    all_to_all x3, starting transfers between devices, to_all(): return lax.all_to_all(copies, axes, 0, 0, tiled=True)  19.8 us
    dot_general x1, matrix products, per_device(): jnp.einsum('pkd,kf->pdf', got[:, :-experts], right, preferred_element_typ...  5.61 us
    dot_general x1, matrix products, per_device(): both = jnp.einsum('pkd,pdf->kf', got, weights, preferred_element_type=F32)  4.21 us
    dot_general x2, matrix products, tn(): lax.dot_general(a, b, (((0,), (0,)), ((), ())), preferred_element_type=F32)  3.45 us
    broadcast_in_dim x3, local copies, waits for them, and re-layouts, to_all(): copies = jnp.broadcast_to(value[None], (count,) + value.shape)  3.19 us
    dot_general x6, matrix products, nt(): lax.dot_general(a, b, (((1,), (1,)), ((), ())), preferred_element_type=F32)  2.27 us
    squeeze x28, local copies, waits for them, and re-layouts, per_device(): value = value + deltas[upper] * table[layer, upper]  2.27 us
  transfers between devices with their start and end apart: 3, of which 3 were waited for; matrix products, arithmetic and copies ran while one was open for 4% of the time, Pallas kernels for 0%

profile of v1, /device:TPU:1, one launch (start us, length us, event | category | flops | bytes accessed | tf_op | source)
XLA Modules:
  0.0 97.9 jit_solution(3809524448361395000)
XLA Ops:
  0.6 0.7 copy.21
  1.4 0.1 reshape_squeeze.12
  1.5 0.7 pad_maximum_fusion
  2.2 0.7 broadcast_in_dim.31
  2.9 5.8 %all-to-all-start = ((bf16[8,9,384]{2,1,0:T(8,128)(2,1)}), bf16[8,9,384]{2,1,0:T(8,128)(2,1)S(1)}, u32[]{:S(2)}, u32[]{:S(2)}) async-start(bf16[8,9,384]{2,1,0:T(8,128)(2,1)} %broadcast_in_dim.31), calls=%async_computation | async-start | bytes 196608 | tf_op jit(solution)/shard_map/all_to_all | solution.py:24
  8.7 0.3 fusion.21
  9.0 0.9 fusion.7
  9.9 1.1 %convolution_convert_fusion.1 = bf16[128,384]{1,0:T(8,128)(2,1)S(1)} fusion(bf16[256,384]{1,0:T(8,128)(2,1)} %bitcast.319, s32[256]{0:T(256)S(1)} %add_select_fusion), kind=kOutput, calls=%fused_computation.6 | convolution fusion | flops 25247744 | bytes 295936 | tf_op jit(solution)/shard_map/dot_general | solution.py:19
  11.0 0.1 convolution_convert_fusion.4
  11.2 2.4 %all-to-all-done = bf16[8,9,384]{2,1,0:T(8,128)(2,1)S(1)} async-done(((bf16[8,9,384]{2,1,0:T(8,128)(2,1)}), bf16[8,9,384]{2,1,0:T(8,128)(2,1)S(1)}, u32[]{:S(2)}, u32[]{:S(2)}) %all-to-all-start) | async-done | bytes 55328 | tf_op jit(solution)/shard_map/all_to_all | solution.py:24
  13.7 1.7 %broadcast_in_dim.32 = bf16[16,192,384]{2,1,0:T(8,128)(2,1)} broadcast(bf16[192,384]{1,0:T(8,128)(2,1)S(1)} %fusion.16), dimensions={1,2} | broadcast | bytes 2506752 | tf_op jit(solution)/shard_map/broadcast_in_dim | solution.py:23
  15.4 7.8 %all-to-all-start.1 = ((bf16[16,192,384]{2,1,0:T(8,128)(2,1)}), bf16[16,192,384]{2,1,0:T(8,128)(2,1)S(1)}, u32[]{:S(2)}, u32[]{:S(2)}) async-start(bf16[16,192,384]{2,1,0:T(8,128)(2,1)} %broadcast_in_dim.32), calls=%async_computation.1 | async-start | bytes 4718592 | tf_op jit(solution)/shard_map/all_to_all | solution.py:24
  23.3 0.1 eq.126
  23.3 0.1 sub.87
  23.4 0.1 convert_reduce_fusion
  23.6 0.1 fusion.19
  23.7 33.4 %all-to-all-done.1 = bf16[16,192,384]{2,1,0:T(8,128)(2,1)S(1)} async-done(((bf16[16,192,384]{2,1,0:T(8,128)(2,1)}), bf16[16,192,384]{2,1,0:T(8,128)(2,1)S(1)}, u32[]{:S(2)}, u32[]{:S(2)}) %all-to-all-start.1) | async-done | bytes 2359328 | tf_op jit(solution)/shard_map/all_to_all | solution.py:24
  57.1 4.2 %convolution_bitcast_fusion = f32[192,512]{1,0:T(8,128)S(1)} fusion(bf16[16,192,384]{2,1,0:T(8,128)(2,1)S(1)} %all-to-all-done.1, bf16[16,384,512]{2,1,0:T(8,128)(2,1)} %bitcast.328), kind=kOutput, calls=%fused_computation.2 | convolution fusion | flops 1207959552 | bytes 9043968 | tf_op jit(solution)/shard_map/pkd,pdf->kf/dot_general | solution.py:80
  61.4 0.8 fusion.12
  62.2 0.2 fusion.4
  62.3 0.8 broadcast_in_dim.35
  63.2 6.2 %all-to-all-start.2 = ((f32[128,8,128]{2,1,0:T(8,128)}), f32[128,8,128]{2,1,0:T(8,128)S(1)}, u32[]{:S(2)}, u32[]{:S(2)}) async-start(f32[128,8,128]{2,1,0:T(8,128)} %broadcast_in_dim.35), calls=%async_computation.2 | async-start | bytes 1048576 | tf_op jit(solution)/shard_map/all_to_all | solution.py:24
  69.5 0.3 fusion.6
  69.8 0.1 div.46
  69.9 0.1 multiply_convert_fusion
  70.0 13.5 %all-to-all-done.2 = f32[128,8,128]{2,1,0:T(8,128)S(1)} async-done(((f32[128,8,128]{2,1,0:T(8,128)}), f32[128,8,128]{2,1,0:T(8,128)S(1)}, u32[]{:S(2)}, u32[]{:S(2)}) %all-to-all-start.2) | async-done | bytes 524320 | tf_op jit(solution)/shard_map/all_to_all | solution.py:24
  83.5 0.4 fusion.8
  84.2 0.1 reduce_precision.415
  84.2 0.1 squeeze.230
  84.3 0.1 squeeze.229
  84.4 0.1 squeeze.228
  84.5 0.1 squeeze.227
  84.6 0.1 squeeze.226
  84.6 0.1 squeeze.225
  84.7 0.1 squeeze.196
  85.4 0.1 squeeze.218
  85.5 0.1 squeeze.217
  85.5 0.1 squeeze.216
  87.2 0.1 constant_dynamic-slice_fusion.1
  87.3 0.1 mul.1110
  87.4 0.1 eq.130
  87.5 0.1 fusion.29
  87.7 0.1 fusion.17
  87.8 2.0 %fusion.2 = bf16[128,512]{1,0:T(8,128)(2,1)} fusion(f32[192,512]{1,0:T(8,128)} %copy-done.2, f32[128]{0:T(128)S(1)} %get-tuple-element.55, f32[8]{0:T(128)S(1)} %compare_convert_fusion, f32[7,128]{1,0:T(8,128)S(1)} %slice.199, f32[7,128]{1,0:T(8,128)S(1)} %fusion.17, pred[7]{0:T(512)(128)(4,1)S(1)} %slice.200), kind=kOutput, calls=%fused_computation.5 | convolution fusion | flops 7608320 | bytes 515623 | tf_op jit(solution)/shard_map/dot_general | solution.py:15
  89.8 0.2 convolution_convert_fusion.2
  90.0 0.8 convolution_bitcast_fusion.1
  90.8 1.5 %fusion.3 = bf16[4,8,384]{2,1,0:T(8,128)(2,1)} fusion(bf16[8,9,384]{2,1,0:T(8,128)(2,1)S(1)} %all-to-all-done, bf16[4,64,384]{2,1,0:T(8,128)(2,1)} %param.11, s32[]{:T(128)S(6)} %select_n.69, bf16[32,64]{1,0:T(8,128)(2,1)S(1)} %copy.23), kind=kOutput, calls=%fused_computation.9 | convolution fusion | flops 1609728 | bytes 106500 | tf_op jit(solution)/shard_map/dot_general | solution.py:15
  92.3 5.6 %convolution_convert_fusion = bf16[16,384,512]{2,1,0:T(8,128)(2,1)} fusion(bf16[16,192,384]{2,1,0:T(8,128)(2,1)S(1)} %all-to-all-done.1, bf16[56,512]{1,0:T(8,128)(2,1)S(1)} %convolution_convert_fusion.2, bf16[128,512]{1,0:T(8,128)(2,1)} %get-tuple-element.58), kind=kOutput, calls=%fused_computation | convolution fusion | flops 1161150464 | bytes 8740864 | tf_op jit(solution)/shard_map/pkd,kf->pdf/dot_general | solution.py:113
  (74 shorter events, 2.9 us)
Async XLA Ops:
  0.6 8.4 %copy-start = (bf16[1,4,64,384]{3,2,1,0:T(8,128)(2,1)S(1)}, bf16[1,4,64,384]{3,2,1,0:T(8,128)(2,1)}, u32[]{:S(2)}) copy-start(bf16[1,4,64,384]{3,2,1,0:T(8,128)(2,1)} %param.6) | copy-start | bytes 589828
  2.9 10.8 %all-to-all-start = ((bf16[8,9,384]{2,1,0:T(8,128)(2,1)}), bf16[8,9,384]{2,1,0:T(8,128)(2,1)S(1)}, u32[]{:S(2)}, u32[]{:S(2)}) async-start(bf16[8,9,384]{2,1,0:T(8,128)(2,1)} %broadcast_in_dim.31), calls=%async_computation | async-start | bytes 196608 | tf_op jit(solution)/shard_map/all_to_all | solution.py:24
  15.4 41.7 %all-to-all-start.1 = ((bf16[16,192,384]{2,1,0:T(8,128)(2,1)}), bf16[16,192,384]{2,1,0:T(8,128)(2,1)S(1)}, u32[]{:S(2)}, u32[]{:S(2)}) async-start(bf16[16,192,384]{2,1,0:T(8,128)(2,1)} %broadcast_in_dim.32), calls=%async_computation.1 | async-start | bytes 4718592 | tf_op jit(solution)/shard_map/all_to_all | solution.py:24
  57.1 4.2 %copy-start.1 = (bf16[1,4,32,512]{3,2,1,0:T(8,128)(2,1)S(1)}, bf16[1,4,32,512]{3,2,1,0:T(8,128)(2,1)}, u32[]{:S(2)}) copy-start(bf16[1,4,32,512]{3,2,1,0:T(8,128)(2,1)} %param.8) | copy-start | bytes 393220
  61.4 0.8 copy-start.2
  63.2 20.3 %all-to-all-start.2 = ((f32[128,8,128]{2,1,0:T(8,128)}), f32[128,8,128]{2,1,0:T(8,128)S(1)}, u32[]{:S(2)}, u32[]{:S(2)}) async-start(f32[128,8,128]{2,1,0:T(8,128)} %broadcast_in_dim.35), calls=%async_computation.2 | async-start | bytes 1048576 | tf_op jit(solution)/shard_map/all_to_all | solution.py:24

commit v2 on v1

v2 whole, which is shorter than its diff:
```python
import jax
import jax.numpy as jnp
from jax import lax
from jax.experimental import pallas as pl
from jax.experimental.pallas import tpu as pltpu
from jax.sharding import PartitionSpec as P

F32 = jnp.float32
BF16 = jnp.bfloat16
VMEM = pl.BlockSpec(memory_space=pltpu.VMEM)
SMEM = pl.BlockSpec(memory_space=pltpu.SMEM)
ANY = pl.BlockSpec(memory_space=pl.ANY)
CHUNKS = 8


def nt(a, b):
    return lax.dot_general(a, b, (((1,), (1,)), ((), ())), preferred_element_type=F32)


def tn(a, b):
    return lax.dot_general(a, b, (((0,), (0,)), ((), ())), preferred_element_type=F32)


def nn(a, b):
    return jnp.dot(a, b, preferred_element_type=F32)


def to_all(value, axes, count):
    copies = jnp.broadcast_to(value[None], (count,) + value.shape)
    return lax.all_to_all(copies, axes, 0, 0, tiled=True)


def swaps(value, axis, distances):
    count = lax.axis_size(axis)
    return [value] + [
        lax.ppermute(value, axis, [(i, i ^ d) for i in range(count)]) for d in distances
    ]


def pieces(value):
    first = lax.reduce_precision(value, 8, 7)
    rest = value - first
    second = lax.reduce_precision(rest, 8, 7)
    return [first.astype(BF16), second.astype(BF16), (rest - second).astype(BF16)]


def iota(shape, dim):
    return lax.broadcasted_iota(jnp.int32, shape, dim)


def slot_of(codes, tok, cap):
    tokens = codes.shape[1]
    row, col = iota((tokens, tokens), 0), iota((tokens, tokens), 1)
    before = ((row < col) & (row // tok == col // tok)).astype(F32).astype(BF16)
    member = codes > 0.0
    rank = nn(member.astype(F32).astype(BF16), before).astype(jnp.int32)
    return jnp.where(member, rank + (iota(codes.shape, 1) // tok) * cap, -1)


def expert_signs(codes):
    experts = iota((codes.shape[0], 8, codes.shape[1]), 1).astype(F32)
    return (experts == 0.0).astype(F32) - (experts == codes[:, None, :]).astype(F32)


def diagonal(size):
    return (iota((size, size), 0) == iota((size, size), 1)).astype(F32)


def mid_kernel(me_ref, got_ref, rt_ref, hid_ref, codes_ref, pick_ref, w_ref,
               table_ref, product_ref, mixed_ref, signs_ref, gate_ref, wbuf, sems):
    ways, slots = got_ref.shape[0], hid_ref.shape[0]
    per = ways // CHUNKS
    depth = per * got_ref.shape[2]
    copies = [
        pltpu.make_async_copy(w_ref.at[pl.ds(q * depth, depth)], wbuf.at[q], sems.at[q])
        for q in range(CHUNKS)
    ]
    for copy in copies:
        copy.start()
    me = me_ref[0]
    pick = pick_ref[...]
    code_slot = nt(codes_ref[...].astype(BF16), pick)
    layers = code_slot.shape[0]
    signs = expert_signs(code_slot)
    above = (iota(signs.shape, 0) ^ me) > me
    signs = jnp.where(above, signs, 0.0)
    signs_ref[...] = signs
    filled = nt(jnp.ones((8, pick.shape[1]), BF16), pick)
    apart = jnp.zeros((8, slots), F32)
    for p in range(ways):
        apart += got_ref[p, slots:slots + 8, :slots].astype(F32)
    gate = filled / (1.0 + jnp.exp(jnp.sum(apart, axis=0, keepdims=True)))
    gate_ref[...] = gate
    total = jnp.zeros((slots + rt_ref.shape[1], hid_ref.shape[1]), F32)
    for q in range(CHUNKS):
        copies[q].wait()
        ps = range(q * per, (q + 1) * per)
        left = jnp.concatenate([
            jnp.concatenate([got_ref[p, :slots] for p in ps], axis=1),
            jnp.concatenate([rt_ref[p] for p in ps], axis=1),
        ], axis=0)
        total += nn(left, wbuf[q])
    product, mixed = total[:slots], total[slots:].astype(BF16)
    product_ref[...] = product
    mixed_ref[...] = mixed
    hid = hid_ref[...]
    base = jnp.sum(hid.astype(F32) * product, axis=1, keepdims=True)
    base = jnp.sum(diagonal(slots) * base, axis=0, keepdims=True)
    cross = nt(mixed, hid).reshape(signs.shape)
    coefs = jnp.sum(signs * cross, axis=1)
    table = jnp.where(iota((layers, slots), 0) == 0, base, coefs) * (gate * (1.0 - gate))
    table_ref[...] = jnp.broadcast_to(table[None], table_ref.shape)


def side_kernel(me_ref, got_ref, rt_ref, hid_ref, codes_ref, gate_ref,
                left_ref, picks_ref, scaled_ref, *, tok, cap):
    ways, slots = got_ref.shape[0], hid_ref.shape[0]
    width = got_ref.shape[2]
    me = me_ref[0]
    layers = codes_ref.shape[0]
    slot = slot_of(codes_ref[...], tok, cap)
    for j in range(layers):
        pick = (iota((slots, slot.shape[1]), 0) == slot[j:j + 1]).astype(F32).astype(BF16)
        picks_ref[me ^ j] = pick
    gate_col = jnp.sum(diagonal(slots) * gate_ref[0:1], axis=1, keepdims=True)
    scaled_ref[...] = (gate_col * hid_ref[...].astype(F32)).astype(BF16)
    for p in range(ways):
        left_ref[pl.ds(p * width, width), :] = jnp.concatenate(
            [got_ref[p, :slots], rt_ref[p]], axis=0
        ).T


def tail_kernel(me_ref, got_ref, picks_ref, codes_ref, pick_ref, signs_ref, gate_ref,
                product_ref, mixed_ref, scaled_ref, left_ref, x_ref, here_ref, grads_ref,
                input_ref, hidden_ref, down_ref, router_ref,
                delta_ref, step_ref, obuf, sems):
    layers, slots = codes_ref.shape[0], gate_ref.shape[1]
    tokens = codes_ref.shape[1]
    ways = got_ref.shape[0] // layers
    me = me_ref[0]
    rows = []
    for s in range(layers):
        table = got_ref[s * ways]
        for p in range(1, ways):
            table += got_ref[s * ways + p]
        first = table.astype(BF16)
        rest = table - first.astype(F32)
        second = rest.astype(BF16)
        third = (rest - second.astype(F32)).astype(BF16)
        parts = nn(jnp.concatenate([first, second, third], axis=0), picks_ref[s])
        rows.append(parts[:8] + parts[8:16] + parts[16:])
    deltas = [None] * layers
    for layer in range(layers - 1, -1, -1):
        value = rows[layer][0:1]
        for upper in range(layer + 1, layers):
            value += deltas[upper] * rows[layer][layer ^ upper:(layer ^ upper) + 1]
        deltas[layer] = value.astype(BF16).astype(F32)
        delta_ref[layer:layer + 1, :] = deltas[layer]
    mine = jnp.concatenate([delta_ref[pl.ds(me ^ j, 1), :] for j in range(layers)], axis=0)
    delta_slot = nt(mine.astype(BF16), pick_ref[...])
    lift = (signs_ref[...] * delta_slot[:, None, :]).reshape(layers * 8, slots).astype(BF16)
    scaled = scaled_ref[...]
    right = jnp.concatenate([scaled, nn(lift, scaled).astype(BF16)], axis=0)
    depth = obuf.shape[1]
    copies = []
    for q in range(CHUNKS):
        obuf[q] = nn(left_ref[pl.ds(q * depth, depth), :], right).astype(BF16)
        copies.append(
            pltpu.make_async_copy(obuf.at[q], down_ref.at[pl.ds(q * depth, depth)], sems.at[q])
        )
        copies[-1].start()
    gate_col = jnp.sum(diagonal(slots) * gate_ref[0:1], axis=1, keepdims=True)
    hidden_ref[...] = (gate_col * (product_ref[...] + tn(lift, mixed_ref[...]))).astype(BF16)
    logit_grads = expert_signs(codes_ref[...]) * mine[:, None, :]
    router_ref[...] = nn(logit_grads[0].astype(BF16), x_ref[...])
    step_ref[...] = tn(logit_grads.reshape(layers * 8, tokens).astype(BF16), here_ref[...])
    count = grads_ref.shape[0]
    tok = tokens // count
    own = grads_ref.shape[1]
    for m in range(count):
        step = step_ref[pl.ds(pl.multiple_of(m * tok + me * own, 8), own), :]
        input_ref[m] = (grads_ref[m].astype(F32) + step).astype(BF16)
    for copy in copies:
        copy.wait()


def call(kernel, outs, in_specs, scratch, limit, out_specs=None, flops=0, moved=0):
    return pl.pallas_call(
        kernel,
        out_shape=[jax.ShapeDtypeStruct(*o) for o in outs],
        in_specs=in_specs,
        out_specs=out_specs or [VMEM] * len(outs),
        scratch_shapes=scratch,
        compiler_params=pltpu.CompilerParams(vmem_limit_bytes=limit << 20),
        cost_estimate=pl.CostEstimate(flops=flops, bytes_accessed=moved, transcendentals=0),
    )


def per_device(layer_inputs, expert_ids, hidden, down_weight, router_weight, grad_out):
    sections, ways = lax.axis_size("section"), lax.axis_size("dp")
    me, at = lax.axis_index("section"), lax.axis_index("dp")
    micro, tok, width = grad_out.shape
    cap, units = hidden.shape[2:]
    experts = router_weight.shape[2]
    tokens, slots = micro * tok, micro * cap
    full = ways * width
    x = layer_inputs[0].reshape(tokens, width)
    ids = expert_ids[0].reshape(tokens, 2)
    hid = hidden[0].reshape(slots, units)
    router = router_weight[0].T
    grads = grad_out.reshape(tokens, width)

    got_router = to_all(router, "dp", ways)

    other = jnp.where(ids[:, 0] == 0, ids[:, 1], ids[:, 0])
    member = (ids[:, 0] == 0) | (ids[:, 1] == 0)
    code = jnp.where(member, other, 0).astype(F32)
    code_block = jnp.zeros((1, experts, width), BF16).at[0, 0, :tokens].set(code.astype(BF16))
    slot = slot_of(code[None], tok, cap)
    pick = (slot == iota((slots, 1), 0)).astype(BF16)
    apart = -jnp.sum(expert_signs(code[None])[0] * nt(router, x), axis=0)
    parts = jnp.stack(pieces(apart))
    parts = jnp.pad(nt(parts, pick).astype(BF16), ((0, 16 - 3), (0, width - slots)))
    rows = nn(pick, grads).astype(BF16)
    block = jnp.concatenate([rows, parts])

    block, got_router = lax.optimization_barrier((block, got_router))
    got = to_all(block, "dp", ways)
    layer_blocks = swaps(
        jnp.concatenate([got_router, code_block]), "section", range(1, sections)
    )
    routers = jnp.concatenate([b[:ways] for b in layer_blocks], axis=1)
    codes = jnp.stack([b[ways, 0, :tokens] for b in layer_blocks]).astype(F32)
    here = lax.dynamic_index_in_dim(routers, at, 0, keepdims=False)
    own = tok // sections
    grads_mine = lax.dynamic_slice_in_dim(grad_out, me * own, own, axis=1)
    me_arr = me.astype(jnp.int32).reshape(1)

    depth = full // CHUNKS
    table, product, mixed, signs, gate = call(
        mid_kernel,
        [
            ((sections * ways, sections, slots), F32),
            ((slots, units), F32),
            ((sections * experts, units), BF16),
            ((sections, experts, slots), F32),
            ((8, slots), F32),
        ],
        [SMEM] + [VMEM] * 5 + [ANY],
        [pltpu.VMEM((CHUNKS, depth, units), BF16), pltpu.SemaphoreType.DMA((CHUNKS,))],
        24,
        flops=2 * 192 * full * units,
        moved=full * units * 2,
    )(me_arr, got, routers, hid, codes, pick, down_weight[0])

    got_table = lax.all_to_all(table, ("section", "dp"), 0, 0, tiled=True)

    left, picks, scaled = call(
        lambda *refs: side_kernel(*refs, tok=tok, cap=cap),
        [
            ((full, slots + sections * experts), BF16),
            ((sections, slots, tokens), BF16),
            ((slots, units), BF16),
        ],
        [SMEM] + [VMEM] * 5,
        [],
        24,
        flops=10**9,
        moved=4 * full * 192,
    )(me_arr, got, routers, hid, codes, gate)

    input_grad, hidden_grad, down_grad, router_grad = call(
        tail_kernel,
        [
            ((micro, own, width), BF16),
            ((slots, units), BF16),
            ((full, units), BF16),
            ((experts, width), F32),
        ],
        [SMEM] + [VMEM] * 13,
        [
            pltpu.VMEM((sections, tokens), F32),
            pltpu.VMEM((tokens, width), F32),
            pltpu.VMEM((CHUNKS, depth, units), BF16),
            pltpu.SemaphoreType.DMA((CHUNKS,)),
        ],
        24,
        out_specs=[VMEM, VMEM, ANY, VMEM],
        flops=2 * 192 * full * units,
        moved=full * units * 2,
    )(
        me_arr, got_table, picks, codes, pick, signs, gate,
        product, mixed, scaled, left, x, here, grads_mine,
    )
    return (
        input_grad,
        hidden_grad.reshape(1, micro, cap, units),
        down_grad[None],
        router_grad.T[None],
    )


def solution(mesh):
    return jax.shard_map(
        per_device,
        mesh=mesh,
        in_specs=(
            P("section", None, None, "dp"),
            P("section", None, None, None),
            P("section", None, None, "dp"),
            P("section", None, "dp"),
            P("section", "dp", None),
            P(None, None, "dp"),
        ),
        out_specs=(
            P(None, "section", "dp"),
            P("section", None, None, "dp"),
            P("section", None, "dp"),
            P("section", "dp", None),
        ),
        check_vma=False,
    )
```

time: 98.4 us -> 100 us (1.016)
  local copies, waits for them, and re-layouts: 7.89 us -> 27.3 us
  matrix products: 17.8 us -> 1.75 us
  waiting for transfers between devices: 49.3 us -> 34 us
  Pallas kernels: 0 us -> 7.91 us
  starting transfers between devices: 19.8 us -> 27.3 us
  other arithmetic: 2.12 us -> 0.12 us
    all_to_all x3 -> x2, waiting for transfers between devices: 49.3 us -> 23.4 us  [to_all(): return lax.all_to_all(copies, axes, 0, 0, tiled=True)]
    unnamed x13 -> x48, local copies, waits for them, and re-layouts: 0.8 us -> 21.7 us
    dot_general x5 -> x0, matrix products: 13.7 us -> none  [the longest x1 5.61 us: per_device(): jnp.einsum('pkd,kf->pdf', got[:, :-experts], right, preferred_element_typ...]
    ppermute x0 -> x7, starting transfers between devices: none -> 10.1 us  [swaps(): lax.ppermute(value, axis, [(i, i ^ d) for i in range(count)])]
    all_to_all x0 -> x1, waiting for transfers between devices: none -> 9.19 us  [per_device(): got_table = lax.all_to_all(table, ('section', 'dp'), 0, 0, tiled=True)]
    pallas_call x0 -> x3, Pallas kernels: none -> 7.91 us  [the longest x1 4.29 us: per_device(): call(tail_kernel, [((micro, own, width), BF16), ((slots, units), BF16), (...]
    all_to_all x3 -> x2, starting transfers between devices: 19.8 us -> 12.3 us  [to_all(): return lax.all_to_all(copies, axes, 0, 0, tiled=True)]
    all_to_all x0 -> x1, starting transfers between devices: none -> 4.97 us  [per_device(): got_table = lax.all_to_all(table, ('section', 'dp'), 0, 0, tiled=True)]
  transfers between devices with their start and end apart: 3 -> 10, of which waited for: 3 -> 4; matrix products, arithmetic and copies ran while one was open for 4% -> 11% of each run, Pallas kernels for 0% -> 1%
where the time goes in v2:
time: 100 us; the launch traced here: 99.3 us
  waiting for transfers between devices  34 us (34%)
  local copies, waits for them, and re-layouts  27.3 us (27%)
  starting transfers between devices  27.3 us (27%)
  Pallas kernels  7.91 us (8%)
  matrix products  1.75 us (2%)
    all_to_all x2, waiting for transfers between devices, to_all(): return lax.all_to_all(copies, axes, 0, 0, tiled=True)  23.4 us
    unnamed x48, local copies, waits for them, and re-layouts  21.7 us
    all_to_all x2, starting transfers between devices, to_all(): return lax.all_to_all(copies, axes, 0, 0, tiled=True)  12.3 us
    ppermute x7, starting transfers between devices, swaps(): lax.ppermute(value, axis, [(i, i ^ d) for i in range(count)])  10.1 us
    all_to_all x1, waiting for transfers between devices, per_device(): got_table = lax.all_to_all(table, ('section', 'dp'), 0, 0, tiled=True)  9.19 us
    all_to_all x1, starting transfers between devices, per_device(): got_table = lax.all_to_all(table, ('section', 'dp'), 0, 0, tiled=True)  4.97 us
    pallas_call x1, Pallas kernels, per_device(): call(tail_kernel, [((micro, own, width), BF16), ((slots, units), BF16), (...  4.29 us
    another operation x8, local copies, waits for them, and re-layouts, per_device(): codes = jnp.stack([b[ways, 0, :tokens] for b in layer_blocks]).astype(F32)  2.77 us
  transfers between devices with their start and end apart: 10, of which 4 were waited for; matrix products, arithmetic and copies ran while one was open for 11% of the time, Pallas kernels for 1%

profile of v2, /device:TPU:1, one launch (start us, length us, event | category | flops | bytes accessed | tf_op | source)
XLA Modules:
  0.0 99.3 jit_solution(83981073285615730)
XLA Ops:
  0.6 1.4 %broadcast_in_dim.12 = bf16[16,8,384]{2,1,0:T(8,128)(2,1)} broadcast(bf16[8,384]{1,0:T(8,128)(2,1)} %bitcast.62), dimensions={1,2} | broadcast | bytes 104448 | tf_op jit(solution)/shard_map/broadcast_in_dim | solution.py:29
  2.0 8.6 %all-to-all-start = ((bf16[16,8,384]{2,1,0:T(8,128)(2,1)}), bf16[16,8,384]{2,1,0:T(8,128)(2,1)S(1)}, u32[]{:S(2)}, u32[]{:S(2)}) async-start(bf16[16,8,384]{2,1,0:T(8,128)(2,1)} %broadcast_in_dim.12), calls=%async_computation | async-start | bytes 196608 | tf_op jit(solution)/shard_map/all_to_all | solution.py:30
  10.7 0.7 copy.10
  11.5 1.1 %fusion = f32[256]{0:T(256)S(1)} fusion(bf16[256,384]{1,0:T(8,128)(2,1)} %bitcast.58, bf16[1,384,8]{1,2,0:T(8,128)(2,1)} %param.12, f32[256]{0:T(256)S(1)} %get-tuple-element.45, f32[8]{0:T(128)S(1)} %compare_convert_fusion, f32[8]{0:T(128)S(1)} %iota_convert_fusion), kind=kOutput, calls=%fused_computation.2 | convolution fusion | flops 1582848 | bytes 204864 | tf_op jit(solution)/shard_map/dot_general | solution.py:17
  12.7 0.3 fusion.5
  13.0 0.2 convolution_convert_fusion
  13.4 4.0 %all-to-all-done = bf16[16,8,384]{2,1,0:T(8,128)(2,1)S(1)} async-done(((bf16[16,8,384]{2,1,0:T(8,128)(2,1)}), bf16[16,8,384]{2,1,0:T(8,128)(2,1)S(1)}, u32[]{:S(2)}, u32[]{:S(2)}) %all-to-all-start) | async-done | bytes 98336 | tf_op jit(solution)/shard_map/all_to_all | solution.py:30
  17.4 4.5 %collective-permute-start.6 = (bf16[17,8,384]{2,1,0:T(8,128)(2,1)S(1)}, bf16[17,8,384]{2,1,0:T(8,128)(2,1)S(1)}, u32[]{:S(2)}, u32[]{:S(2)}) collective-permute-start(bf16[17,8,384]{2,1,0:T(8,128)(2,1)S(1)} %fusion.9), channel_id=1, source_target_pairs={{0,112},{16,96},{32,80},{48,64},{64,48},{80,32},{96,16},{112,0},{1... | collective-permute-start | bytes 313352 | tf_op jit(solution)/shard_map/ppermute | solution.py:36
  21.9 0.2 collective-permute-start.5
  22.1 0.7 collective-permute-start.4
  22.8 2.5 %collective-permute-start.3 = (bf16[17,8,384]{2,1,0:T(8,128)(2,1)S(1)}, bf16[17,8,384]{2,1,0:T(8,128)(2,1)}, u32[]{:S(2)}, u32[]{:S(2)}) collective-permute-start(bf16[17,8,384]{2,1,0:T(8,128)(2,1)S(1)} %fusion.9), channel_id=1, source_target_pairs={{0,64},{16,80},{32,96},{48,112},{64,0},{80,16},{96,32},{112,48},{1... | collective-permute-start | bytes 313352 | tf_op jit(solution)/shard_map/ppermute | solution.py:36
  25.2 0.4 collective-permute-start.2
  25.6 1.4 %broadcast_in_dim.13 = bf16[16,144,384]{2,1,0:T(8,128)(2,1)} broadcast(bf16[144,384]{1,0:T(8,128)(2,1)S(1)} %fusion.8), dimensions={1,2} | broadcast | bytes 1880064 | tf_op jit(solution)/shard_map/broadcast_in_dim | solution.py:29
  27.0 3.7 %all-to-all-start.1 = ((bf16[16,144,384]{2,1,0:T(8,128)(2,1)}), bf16[16,144,384]{2,1,0:T(8,128)(2,1)S(1)}, u32[]{:S(2)}, u32[]{:S(2)}) async-start(bf16[16,144,384]{2,1,0:T(8,128)(2,1)} %broadcast_in_dim.13), calls=%async_computation.1 | async-start | bytes 3538944 | tf_op jit(solution)/shard_map/all_to_all | solution.py:30
  30.7 1.5 %collective-permute-start.1 = (bf16[17,8,384]{2,1,0:T(8,128)(2,1)S(1)}, bf16[17,8,384]{2,1,0:T(8,128)(2,1)}, u32[]{:S(2)}, u32[]{:S(2)}) collective-permute-start(bf16[17,8,384]{2,1,0:T(8,128)(2,1)S(1)} %fusion.9), channel_id=1, source_target_pairs={{0,32},{16,48},{32,0},{48,16},{64,96},{80,112},{96,64},{112,80},{1... | collective-permute-start | bytes 313352 | tf_op jit(solution)/shard_map/ppermute | solution.py:36
  32.3 0.3 collective-permute-start
  32.6 0.7 slice_bitcast_fusion.3
  33.3 0.7 slice_bitcast_fusion.4
  33.9 1.4 %collective-permute-done.1 = bf16[17,8,384]{2,1,0:T(8,128)(2,1)} collective-permute-done((bf16[17,8,384]{2,1,0:T(8,128)(2,1)S(1)}, bf16[17,8,384]{2,1,0:T(8,128)(2,1)}, u32[]{:S(2)}, u32[]{:S(2)}) %collective-permute-start.1) | collective-permute-done | bytes 104480 | tf_op jit(solution)/shard_map/ppermute | solution.py:36
  35.3 0.7 slice_bitcast_fusion.5
  36.0 0.7 slice_bitcast_fusion.6
  36.7 0.9 slice_dynamic-update-slice_fusion.6
  37.6 0.9 slice_dynamic-update-slice_fusion.5
  38.5 0.9 slice_dynamic-update-slice_fusion.4
  39.5 0.9 slice_dynamic-update-slice_fusion.3
  40.5 19.4 %all-to-all-done.1.got_ref.refs_1_ = bf16[16,144,384]{2,1,0:T(8,128)(2,1)S(1)} async-done(((bf16[16,144,384]{2,1,0:T(8,128)(2,1)}), bf16[16,144,384]{2,1,0:T(8,128)(2,1)S(1)}, u32[]{:S(2)}, u32[]{:S(2)}) %all-to-all-start.1) | async-done | bytes 1769504 | tf_op jit(solution)/shard_map/all_to_all | solution.py:30
  59.9 2.8 %copy-done.1 = bf16[1,6144,512]{2,1,0:T(8,128)(2,1)S(1)} copy-done((bf16[1,6144,512]{2,1,0:T(8,128)(2,1)S(1)}, bf16[1,6144,512]{2,1,0:T(8,128)(2,1)}, u32[]{:S(2)}) %copy-start.1) | copy-done | bytes 6291480
  62.7 2.6 %shard_map.93 = (f32[128,8,128]{2,1,0:T(8,128)S(1)}, f32[128,512]{1,0:T(8,128)S(1)}, bf16[64,512]{1,0:T(8,128)(2,1)S(1)}, f32[8,8,128]{2,1,0:T(8,128)S(1)}, f32[8,128]{1,0:T(8,128)S(1)}) custom-call(s32[1]{0:T(128)} %bitcast.me_ref.refs_0_, bf16[16,144,384]{2,1,0:T(8,128)(2,1)S(1)} %all-to-all-done.1.got_ref.refs_1_, ...), custom_call_target="tpu_custom_call" | custom-call | flops 1207959552 | bytes 6291456 | tf_op jit(solution)/shard_map/pallas_call | solution.py:240
  65.3 0.8 copy-done.6
  66.1 0.7 copy-done.7
  66.8 0.6 copy-done.13
  67.4 0.6 copy-done.15
  68.0 5.0 %all-to-all-start.2 = ((f32[128,8,128]{2,1,0:T(8,128)}), f32[128,8,128]{2,1,0:T(8,128)S(1)}, u32[]{:S(2)}, u32[]{:S(2)}) async-start(f32[128,8,128]{2,1,0:T(8,128)} %copy-done.6), calls=%async_computation.2 | async-start | bytes 1048576 | tf_op jit(solution)/shard_map/all_to_all | solution.py:256
  73.0 0.7 copy-done.18
  73.7 1.0 %shard_map.94 = (bf16[6144,192]{1,0:T(8,128)(2,1)S(1)}, bf16[8,128,256]{2,1,0:T(8,128)(2,1)S(1)}, bf16[128,512]{1,0:T(8,128)(2,1)S(1)}) custom-call(s32[1]{0:T(128)} %bitcast.me_ref.refs_0_, bf16[16,144,384]{2,1,0:T(8,128)(2,1)S(1)} %all-to-all-done.1.got_ref.refs_1_, bf16[16,64,384]{2,1,0:T(8,128)(2,1)S(1)} %slice_dynamic-update-slice_fusion.rt_ref.refs_2_, ...), custom_call_target="tpu_custom_call" | custom-call | flops 1000000000 | bytes 4718592 | tf_op jit(solution)/shard_map/pallas_call | solution.py:258
  74.7 1.7 %copy-done.2 = bf16[6144,192]{1,0:T(8,128)(2,1)} copy-done((bf16[6144,192]{1,0:T(8,128)(2,1)}, bf16[6144,192]{1,0:T(8,128)(2,1)S(1)}, u32[]{:S(2)}) %copy-start.2) | copy-done | bytes 2359320
  76.4 0.8 copy-done.4
  77.2 0.7 copy-done.11
  77.9 9.2 %all-to-all-done.2.got_ref = f32[128,8,128]{2,1,0:T(8,128)S(1)} async-done(((f32[128,8,128]{2,1,0:T(8,128)}), f32[128,8,128]{2,1,0:T(8,128)S(1)}, u32[]{:S(2)}, u32[]{:S(2)}) %all-to-all-start.2) | async-done | bytes 524320 | tf_op jit(solution)/shard_map/all_to_all | solution.py:256
  87.0 1.9 %copy-done.3 = bf16[6144,192]{1,0:T(8,128)(2,1)S(1)} copy-done((bf16[6144,192]{1,0:T(8,128)(2,1)S(1)}, bf16[6144,192]{1,0:T(8,128)(2,1)}, u32[]{:S(2)}) %copy-start.3) | copy-done | bytes 2359320
  88.9 1.0 %copy-done.5 = bf16[8,128,256]{2,1,0:T(8,128)(2,1)S(1)} copy-done((bf16[8,128,256]{2,1,0:T(8,128)(2,1)S(1)}, bf16[8,128,256]{2,1,0:T(8,128)(2,1)}, u32[]{:S(2)}) %copy-start.5) | copy-done | bytes 524312
  90.0 0.9 copy-done.8
  90.9 0.9 copy-done.9
  91.9 0.9 copy-done.12
  92.8 0.8 copy-done.14
  93.6 0.8 copy-done.16
  94.4 0.7 copy-done.19
  95.0 4.3 %shard_map.95 = (bf16[4,8,384]{2,1,0:T(8,128)(2,1)}, bf16[128,512]{1,0:T(8,128)(2,1)}, bf16[6144,512]{1,0:T(8,128)(2,1)}, f32[8,384]{1,0:T(8,128)}) custom-call(s32[1]{0:T(128)} %bitcast.me_ref.refs_0_, f32[128,8,128]{2,1,0:T(8,128)S(1)} %all-to-all-done.2.got_ref, bf16[8,128,256]{2,1,0:T(8,128)(2,1)S(1)} %copy-done.5, ...), custom_call_target="tpu_custom_call" | custom-call | flops 1207959552 | bytes 6291456 | tf_op jit(solution)/shard_map/pallas_call | solution.py:272
  (57 shorter events, 0.6 us)
Async XLA Ops:
  0.6 12.4 %copy-start = (bf16[4,64,384]{2,1,0:T(8,128)(2,1)S(1)}, bf16[4,64,384]{2,1,0:T(8,128)(2,1)}, u32[]{:S(2)}) copy-start(bf16[4,64,384]{2,1,0:T(8,128)(2,1)} %param.13) | copy-start | bytes 589828
  2.0 15.3 %all-to-all-start = ((bf16[16,8,384]{2,1,0:T(8,128)(2,1)}), bf16[16,8,384]{2,1,0:T(8,128)(2,1)S(1)}, u32[]{:S(2)}, u32[]{:S(2)}) async-start(bf16[16,8,384]{2,1,0:T(8,128)(2,1)} %broadcast_in_dim.12), calls=%async_computation | async-start | bytes 196608 | tf_op jit(solution)/shard_map/all_to_all | solution.py:30
  17.4 42.5 %copy-start.10 = (bf16[1,4,32,512]{3,2,1,0:T(8,128)(2,1)S(1)}, bf16[1,4,32,512]{3,2,1,0:T(8,128)(2,1)}, u32[]{:S(2)}) copy-start(bf16[1,4,32,512]{3,2,1,0:T(8,128)(2,1)} %param.10) | copy-start | bytes 393220
  17.4 13.3 %collective-permute-start.6 = (bf16[17,8,384]{2,1,0:T(8,128)(2,1)S(1)}, bf16[17,8,384]{2,1,0:T(8,128)(2,1)S(1)}, u32[]{:S(2)}, u32[]{:S(2)}) collective-permute-start(bf16[17,8,384]{2,1,0:T(8,128)(2,1)S(1)} %fusion.9), channel_id=1, source_target_pairs={{0,112},{16,96},{32,80},{48,64},{64,48},{80,32},{96,16},{112,0},{1... | collective-permute-start | bytes 313352 | tf_op jit(solution)/shard_map/ppermute | solution.py:36
  21.9 10.4 %collective-permute-start.5 = (bf16[17,8,384]{2,1,0:T(8,128)(2,1)S(1)}, bf16[17,8,384]{2,1,0:T(8,128)(2,1)S(1)}, u32[]{:S(2)}, u32[]{:S(2)}) collective-permute-start(bf16[17,8,384]{2,1,0:T(8,128)(2,1)S(1)} %fusion.9), channel_id=1, source_target_pairs={{0,96},{16,112},{32,64},{48,80},{64,32},{80,48},{96,0},{112,16},{1... | collective-permute-start | bytes 313352 | tf_op jit(solution)/shard_map/ppermute | solution.py:36
  22.1 10.5 %collective-permute-start.4 = (bf16[17,8,384]{2,1,0:T(8,128)(2,1)S(1)}, bf16[17,8,384]{2,1,0:T(8,128)(2,1)S(1)}, u32[]{:S(2)}, u32[]{:S(2)}) collective-permute-start(bf16[17,8,384]{2,1,0:T(8,128)(2,1)S(1)} %fusion.9), channel_id=1, source_target_pairs={{0,80},{16,64},{32,112},{48,96},{64,16},{80,0},{96,48},{112,32},{1... | collective-permute-start | bytes 313352 | tf_op jit(solution)/shard_map/ppermute | solution.py:36
  22.8 9.8 %collective-permute-start.3 = (bf16[17,8,384]{2,1,0:T(8,128)(2,1)S(1)}, bf16[17,8,384]{2,1,0:T(8,128)(2,1)}, u32[]{:S(2)}, u32[]{:S(2)}) collective-permute-start(bf16[17,8,384]{2,1,0:T(8,128)(2,1)S(1)} %fusion.9), channel_id=1, source_target_pairs={{0,64},{16,80},{32,96},{48,112},{64,0},{80,16},{96,32},{112,48},{1... | collective-permute-start | bytes 313352 | tf_op jit(solution)/shard_map/ppermute | solution.py:36
  25.2 8.1 %collective-permute-start.2 = (bf16[17,8,384]{2,1,0:T(8,128)(2,1)S(1)}, bf16[17,8,384]{2,1,0:T(8,128)(2,1)}, u32[]{:S(2)}, u32[]{:S(2)}) collective-permute-start(bf16[17,8,384]{2,1,0:T(8,128)(2,1)S(1)} %fusion.9), channel_id=1, source_target_pairs={{0,48},{16,32},{32,16},{48,0},{64,112},{80,96},{96,80},{112,64},{1... | collective-permute-start | bytes 313352 | tf_op jit(solution)/shard_map/ppermute | solution.py:36
  27.0 32.9 %all-to-all-start.1 = ((bf16[16,144,384]{2,1,0:T(8,128)(2,1)}), bf16[16,144,384]{2,1,0:T(8,128)(2,1)S(1)}, u32[]{:S(2)}, u32[]{:S(2)}) async-start(bf16[16,144,384]{2,1,0:T(8,128)(2,1)} %broadcast_in_dim.13), calls=%async_computation.1 | async-start | bytes 3538944 | tf_op jit(solution)/shard_map/all_to_all | solution.py:30
  30.7 4.6 %collective-permute-start.1 = (bf16[17,8,384]{2,1,0:T(8,128)(2,1)S(1)}, bf16[17,8,384]{2,1,0:T(8,128)(2,1)}, u32[]{:S(2)}, u32[]{:S(2)}) collective-permute-start(bf16[17,8,384]{2,1,0:T(8,128)(2,1)S(1)} %fusion.9), channel_id=1, source_target_pairs={{0,32},{16,48},{32,0},{48,16},{64,96},{80,112},{96,64},{112,80},{1... | collective-permute-start | bytes 313352 | tf_op jit(solution)/shard_map/ppermute | solution.py:36
  32.3 3.7 %collective-permute-start = (bf16[17,8,384]{2,1,0:T(8,128)(2,1)S(1)}, bf16[17,8,384]{2,1,0:T(8,128)(2,1)}, u32[]{:S(2)}, u32[]{:S(2)}) collective-permute-start(bf16[17,8,384]{2,1,0:T(8,128)(2,1)S(1)} %fusion.9), channel_id=1, source_target_pairs={{0,16},{16,0},{32,48},{48,32},{64,80},{80,64},{96,112},{112,96},{1... | collective-permute-start | bytes 313352 | tf_op jit(solution)/shard_map/ppermute | solution.py:36
  59.9 2.8 %copy-start.1 = (bf16[1,6144,512]{2,1,0:T(8,128)(2,1)S(1)}, bf16[1,6144,512]{2,1,0:T(8,128)(2,1)}, u32[]{:S(2)}) copy-start(bf16[1,6144,512]{2,1,0:T(8,128)(2,1)} %param.11) | copy-start | bytes 18874372
  65.3 0.8 copy-start.6
  66.1 0.7 copy-start.7
  66.8 0.6 copy-start.13
  67.4 0.6 copy-start.15
  68.0 5.0 %copy-start.17 = (f32[8,128]{1,0:T(8,128)}, f32[8,128]{1,0:T(8,128)S(1)}, u32[]{:S(2)}) copy-start(f32[8,128]{1,0:T(8,128)S(1)} %get-tuple-element.33.refs_5_.gate_ref) | copy-start | bytes 12292
  68.0 19.1 %all-to-all-start.2 = ((f32[128,8,128]{2,1,0:T(8,128)}), f32[128,8,128]{2,1,0:T(8,128)S(1)}, u32[]{:S(2)}, u32[]{:S(2)}) async-start(f32[128,8,128]{2,1,0:T(8,128)} %copy-done.6), calls=%async_computation.2 | async-start | bytes 1048576 | tf_op jit(solution)/shard_map/all_to_all | solution.py:256
  73.0 0.7 copy-start.18
  74.7 1.7 %copy-start.2 = (bf16[6144,192]{1,0:T(8,128)(2,1)}, bf16[6144,192]{1,0:T(8,128)(2,1)S(1)}, u32[]{:S(2)}) copy-start(bf16[6144,192]{1,0:T(8,128)(2,1)S(1)} %get-tuple-element.39.left_ref) | copy-start | bytes 7077892
  76.4 0.8 copy-start.4
  77.2 0.7 copy-start.11
  87.0 1.9 %copy-start.3 = (bf16[6144,192]{1,0:T(8,128)(2,1)S(1)}, bf16[6144,192]{1,0:T(8,128)(2,1)}, u32[]{:S(2)}) copy-start(bf16[6144,192]{1,0:T(8,128)(2,1)} %copy-done.2) | copy-start | bytes 7077892
  88.9 1.0 %copy-start.5 = (bf16[8,128,256]{2,1,0:T(8,128)(2,1)S(1)}, bf16[8,128,256]{2,1,0:T(8,128)(2,1)}, u32[]{:S(2)}) copy-start(bf16[8,128,256]{2,1,0:T(8,128)(2,1)} %copy-done.4) | copy-start | bytes 1572868
  90.0 0.9 copy-start.8
  90.9 0.9 copy-start.9
  91.9 0.9 copy-start.12
  92.8 0.8 copy-start.14
  93.6 0.8 copy-start.16
  94.4 0.7 copy-start.19

commit v3 on v2

v3 whole, which is shorter than its diff:
```python
import jax
import jax.numpy as jnp
from jax import lax
from jax.experimental import pallas as pl
from jax.experimental.pallas import tpu as pltpu
from jax.sharding import PartitionSpec as P

F32 = jnp.float32
BF16 = jnp.bfloat16
VMEM = pl.BlockSpec(memory_space=pltpu.VMEM)
SMEM = pl.BlockSpec(memory_space=pltpu.SMEM)
HBM = pl.BlockSpec(memory_space=pltpu.HBM)
AUTO = pl.BlockSpec()
RING = (0, 1, 3, 2)
SECTION_STEPS = (2, 6, 4)
LAYER_ORDER = [d ^ core for core in (0, 1) for d in (0,) + SECTION_STEPS]


def nt(a, b):
    return lax.dot_general(a, b, (((1,), (1,)), ((), ())), preferred_element_type=F32)


def tn(a, b):
    return lax.dot_general(a, b, (((0,), (0,)), ((), ())), preferred_element_type=F32)


def nn(a, b):
    return jnp.dot(a, b, preferred_element_type=F32)


def to_all(value, axes, count):
    copies = jnp.broadcast_to(value[None], (count,) + value.shape)
    return lax.all_to_all(copies, axes, 0, 0, tiled=True)


def swap(value, axis, distance):
    count = lax.axis_size(axis)
    return lax.ppermute(value, axis, [(i, i ^ distance) for i in range(count)])


def turn(value, stage, step):
    sections, ways = lax.axis_size("section"), lax.axis_size("dp")
    pairs = []
    for s in range(sections):
        distance = RING[step] * (1 if s % 2 == stage else 4)
        pairs += [(s * ways + p, s * ways + (p ^ distance)) for p in range(ways)]
    return lax.ppermute(value, ("section", "dp"), pairs)


def pieces(value):
    first = lax.reduce_precision(value, 8, 7)
    rest = value - first
    second = lax.reduce_precision(rest, 8, 7)
    return [first.astype(BF16), second.astype(BF16), (rest - second).astype(BF16)]


def iota(shape, dim):
    return lax.broadcasted_iota(jnp.int32, shape, dim)


def slot_of(codes, tok, cap):
    tokens = codes.shape[1]
    row, col = iota((tokens, tokens), 0), iota((tokens, tokens), 1)
    before = ((row < col) & (row // tok == col // tok)).astype(F32).astype(BF16)
    member = codes > 0.0
    rank = nn(member.astype(F32).astype(BF16), before).astype(jnp.int32)
    return jnp.where(member, rank + (iota(codes.shape, 1) // tok) * cap, -1)


def expert_signs(codes):
    experts = iota((codes.shape[0], 8, codes.shape[1]), 1).astype(F32)
    return (experts == 0.0).astype(F32) - (experts == codes[:, None, :]).astype(F32)


def diagonal(size):
    return (iota((size, size), 0) == iota((size, size), 1)).astype(F32)


def block_way(at, odd, far, near):
    plain = RING[near] + 4 * RING[far]
    turned = 4 * RING[near] + RING[far]
    return at ^ jnp.where(odd, turned, plain)


def router_rows(left_ref, right_ref, way):
    return jnp.concatenate(
        [ref[k, way] for ref in (left_ref, right_ref) for k in range(4)], axis=0
    )


def mid_kernel(here_ref, a0, a1, a2, a3, near_ref, far_ref, hid_ref, pick_ref, w_ref,
               table_ref, product_ref, mixed_ref, signs_ref, gate_ref, wbuf, sems):
    slots, width = hid_ref.shape[0], a0.shape[2]
    me, at = here_ref[0], here_ref[1]
    ways = [block_way(at, (me & 1) == 1, far, k) for far in range(4) for k in range(4)]
    copies = [
        pltpu.make_async_copy(
            w_ref.at[pl.ds(pl.multiple_of(way * width, width), width)],
            wbuf.at[j // 2, pl.ds((j % 2) * width, width)],
            sems.at[j],
        )
        for j, way in enumerate(ways)
    ]
    for copy in copies:
        copy.start()
    pick = pick_ref[...]
    codes = jnp.concatenate(
        [ref[k, 16, 0:1, :pick.shape[1]].astype(F32) for ref in (near_ref, far_ref) for k in range(4)],
        axis=0,
    )
    code_slot = nt(codes.astype(BF16), pick)
    layers = code_slot.shape[0]
    signs = expert_signs(code_slot)
    layer = jnp.concatenate([jnp.full((1, 8, slots), d, jnp.int32) for d in LAYER_ORDER]) ^ me
    signs = jnp.where(layer > me, signs, 0.0)
    signs_ref[...] = signs
    filled = nt(jnp.ones((8, pick.shape[1]), BF16), pick)
    apart = jnp.zeros((8, slots), F32)
    for block in (a0, a1, a2, a3):
        for k in range(4):
            apart += block[k, slots:slots + 8, :slots].astype(F32)
    gate = filled / (1.0 + jnp.exp(jnp.sum(apart, axis=0, keepdims=True)))
    gate_ref[...] = gate
    total = jnp.zeros((slots + layers * 8, hid_ref.shape[1]), F32)
    for far, block in enumerate((a0, a1, a2, a3)):
        for half in range(2):
            j = 4 * far + 2 * half
            left = jnp.concatenate([
                jnp.concatenate([block[2 * half + i, :slots] for i in range(2)], axis=1),
                jnp.concatenate(
                    [router_rows(near_ref, far_ref, ways[j + i]) for i in range(2)], axis=1
                ),
            ], axis=0)
            copies[j].wait()
            copies[j + 1].wait()
            total += nn(left, wbuf[j // 2])
    product, mixed = total[:slots], total[slots:].astype(BF16)
    product_ref[...] = product
    mixed_ref[...] = mixed
    hid = hid_ref[...]
    base = jnp.sum(hid.astype(F32) * product, axis=1, keepdims=True)
    base = jnp.sum(diagonal(slots) * base, axis=0, keepdims=True)
    cross = nt(mixed, hid).reshape(signs.shape)
    coefs = jnp.sum(signs * cross, axis=1)
    table = jnp.where(iota((layers, slots), 0) == 0, base, coefs) * (gate * (1.0 - gate))
    table_ref[...] = jnp.broadcast_to(table.astype(BF16)[None], table_ref.shape)


def side_kernel(here_ref, a0, a1, a2, a3, near_ref, far_ref, hid_ref, gate_ref,
                left_ref, picks_ref, scaled_ref, local_ref, codes_ref, *, tok, cap):
    slots, width = hid_ref.shape[0], a0.shape[2]
    me, at = here_ref[0], here_ref[1]
    codes = jnp.concatenate(
        [ref[k, 16, 0:1, :codes_ref.shape[1]].astype(F32) for ref in (near_ref, far_ref) for k in range(4)],
        axis=0,
    )
    codes_ref[...] = codes
    slot = slot_of(codes, tok, cap)
    for i, d in enumerate(LAYER_ORDER):
        pick = (iota((slots, slot.shape[1]), 0) == slot[i:i + 1]).astype(F32).astype(BF16)
        picks_ref[me ^ d] = pick
    gate_col = jnp.sum(diagonal(slots) * gate_ref[0:1], axis=1, keepdims=True)
    scaled_ref[...] = (gate_col * hid_ref[...].astype(F32)).astype(BF16)
    local_ref[...] = router_rows(near_ref, far_ref, at)
    for far, block in enumerate((a0, a1, a2, a3)):
        for k in range(4):
            way = block_way(at, (me & 1) == 1, far, k)
            left_ref[pl.ds((4 * far + k) * width, width), :] = jnp.concatenate(
                [block[k, :slots], router_rows(near_ref, far_ref, way)], axis=0
            ).T


def tail_kernel(here_ref, got_ref, picks_ref, codes_ref, pick_ref, signs_ref, gate_ref,
                product_ref, mixed_ref, scaled_ref, left_ref, x_ref, local_ref, grads_ref,
                input_ref, hidden_ref, down_ref, router_ref,
                delta_ref, step_ref, ibuf, isems, obuf, sems):
    layers, slots = codes_ref.shape[0], gate_ref.shape[1]
    tokens, width = codes_ref.shape[1], x_ref.shape[1]
    ways = got_ref.shape[0] // layers
    loads = [
        pltpu.make_async_copy(left_ref.at[pl.ds(j * width, width)], ibuf.at[j], isems.at[j])
        for j in range(ways)
    ]
    for load in loads:
        load.start()
    me, at = here_ref[0], here_ref[1]
    rows = []
    for s in range(layers):
        table = got_ref[s * ways].astype(F32)
        for p in range(1, ways):
            table += got_ref[s * ways + p].astype(F32)
        first = table.astype(BF16)
        rest = table - first.astype(F32)
        second = rest.astype(BF16)
        third = (rest - second.astype(F32)).astype(BF16)
        parts = nn(jnp.concatenate([first, second, third], axis=0), picks_ref[s])
        rows.append(parts[:8] + parts[8:16] + parts[16:])
    deltas = [None] * layers
    for layer in range(layers - 1, -1, -1):
        value = rows[layer][0:1]
        for upper in range(layer + 1, layers):
            i = LAYER_ORDER.index(layer ^ upper)
            value += deltas[upper] * rows[layer][i:i + 1]
        deltas[layer] = value.astype(BF16).astype(F32)
        delta_ref[layer:layer + 1, :] = deltas[layer]
    mine = jnp.concatenate([delta_ref[pl.ds(me ^ d, 1), :] for d in LAYER_ORDER], axis=0)
    delta_slot = nt(mine.astype(BF16), pick_ref[...])
    lift = (signs_ref[...] * delta_slot[:, None, :]).reshape(layers * 8, slots).astype(BF16)
    scaled = scaled_ref[...]
    right = jnp.concatenate([scaled, nn(lift, scaled).astype(BF16)], axis=0)
    copies = []
    for j in range(ways):
        way = block_way(at, (me & 1) == 1, j // 4, j % 4)
        loads[j].wait()
        obuf[j] = nn(ibuf[j], right).astype(BF16)
        copies.append(
            pltpu.make_async_copy(
                obuf.at[j],
                down_ref.at[pl.ds(pl.multiple_of(way * width, width), width)],
                sems.at[j],
            )
        )
        copies[-1].start()
    gate_col = jnp.sum(diagonal(slots) * gate_ref[0:1], axis=1, keepdims=True)
    hidden_ref[...] = (gate_col * (product_ref[...] + tn(lift, mixed_ref[...]))).astype(BF16)
    logit_grads = expert_signs(codes_ref[...]) * mine[:, None, :]
    router_ref[...] = nn(logit_grads[0].astype(BF16), x_ref[...])
    step_ref[...] = tn(logit_grads.reshape(layers * 8, tokens).astype(BF16), local_ref[...])
    count = grads_ref.shape[0]
    tok = tokens // count
    own = grads_ref.shape[1]
    for m in range(count):
        step = step_ref[pl.ds(pl.multiple_of(m * tok + me * own, 8), own), :]
        input_ref[m] = (grads_ref[m].astype(F32) + step).astype(BF16)
    for copy in copies:
        copy.wait()


def call(kernel, outs, in_specs, scratch, limit, out_specs=None, flops=0, moved=0):
    return pl.pallas_call(
        kernel,
        out_shape=[jax.ShapeDtypeStruct(*o) for o in outs],
        in_specs=in_specs,
        out_specs=out_specs or [AUTO] * len(outs),
        scratch_shapes=scratch,
        compiler_params=pltpu.CompilerParams(vmem_limit_bytes=limit << 20),
        cost_estimate=pl.CostEstimate(flops=flops, bytes_accessed=moved, transcendentals=0),
    )


def per_device(layer_inputs, expert_ids, hidden, down_weight, router_weight, grad_out):
    sections, ways = lax.axis_size("section"), lax.axis_size("dp")
    me, at = lax.axis_index("section"), lax.axis_index("dp")
    micro, tok, width = grad_out.shape
    cap, units = hidden.shape[2:]
    experts = router_weight.shape[2]
    tokens, slots = micro * tok, micro * cap
    full = ways * width
    x = layer_inputs[0].reshape(tokens, width)
    ids = expert_ids[0].reshape(tokens, 2)
    hid = hidden[0].reshape(slots, units)
    router = router_weight[0].T
    grads = grad_out.reshape(tokens, width)

    got_router = to_all(router, "dp", ways)

    other = jnp.where(ids[:, 0] == 0, ids[:, 1], ids[:, 0])
    member = (ids[:, 0] == 0) | (ids[:, 1] == 0)
    code = jnp.where(member, other, 0).astype(F32)
    code_block = jnp.zeros((1, experts, width), BF16).at[0, 0, :tokens].set(code.astype(BF16))
    slot = slot_of(code[None], tok, cap)
    pick = (slot == iota((slots, 1), 0)).astype(BF16)
    apart = -jnp.sum(expert_signs(code[None])[0] * nt(router, x), axis=0)
    parts = jnp.stack(pieces(apart))
    parts = jnp.pad(nt(parts, pick).astype(BF16), ((0, 8 - 3), (0, width - slots)))
    rows = nn(pick, grads).astype(BF16)
    block = jnp.concatenate([rows, parts])

    group = jnp.stack([block] + [turn(block, 0, step) for step in (1, 2, 3)])
    blocks = [group] + [turn(group, 1, step) for step in (1, 2, 3)]
    mine = jnp.concatenate([got_router, code_block])
    near = jnp.stack([mine] + [swap(mine, "section", d) for d in SECTION_STEPS])
    far = swap(near, "section", 1)
    own = tok // sections
    grads_mine = lax.dynamic_slice_in_dim(grad_out, me * own, own, axis=1)
    place = jnp.stack([me, at]).astype(jnp.int32)

    table, product, mixed, signs, gate = call(
        mid_kernel,
        [
            ((sections * ways, sections, slots), BF16),
            ((slots, units), F32),
            ((sections * experts, units), BF16),
            ((sections, experts, slots), F32),
            ((8, slots), F32),
        ],
        [SMEM] + [AUTO] * 8 + [HBM],
        [pltpu.VMEM((ways // 2, 2 * width, units), BF16), pltpu.SemaphoreType.DMA((ways,))],
        60,
        flops=2 * 192 * full * units,
        moved=full * units * 2,
    )(place, *blocks, near, far, hid, pick, down_weight[0])

    got_table = lax.all_to_all(table, ("section", "dp"), 0, 0, tiled=True)

    left, picks, scaled, local, codes = call(
        lambda *refs: side_kernel(*refs, tok=tok, cap=cap),
        [
            ((full, slots + sections * experts), BF16),
            ((sections, slots, tokens), BF16),
            ((slots, units), BF16),
            ((sections * experts, width), BF16),
            ((sections, tokens), F32),
        ],
        [SMEM] + [AUTO] * 8,
        [],
        60,
        flops=10**9,
        moved=4 * full * 192,
    )(place, *blocks, near, far, hid, gate)

    input_grad, hidden_grad, down_grad, router_grad = call(
        tail_kernel,
        [
            ((micro, own, width), BF16),
            ((slots, units), BF16),
            ((full, units), BF16),
            ((experts, width), F32),
        ],
        [SMEM] + [AUTO] * 9 + [HBM] + [AUTO] * 3,
        [
            pltpu.VMEM((sections, tokens), F32),
            pltpu.VMEM((tokens, width), F32),
            pltpu.VMEM((ways, width, slots + sections * experts), BF16),
            pltpu.SemaphoreType.DMA((ways,)),
            pltpu.VMEM((ways, width, units), BF16),
            pltpu.SemaphoreType.DMA((ways,)),
        ],
        60,
        out_specs=[AUTO, AUTO, HBM, AUTO],
        flops=2 * 192 * full * units,
        moved=full * units * 2,
    )(
        place, got_table, picks, codes, pick, signs, gate,
        product, mixed, scaled, left, x, local, grads_mine,
    )
    return (
        input_grad,
        hidden_grad.reshape(1, micro, cap, units),
        down_grad[None],
        router_grad.T[None],
    )


def solution(mesh):
    return jax.shard_map(
        per_device,
        mesh=mesh,
        in_specs=(
            P("section", None, None, "dp"),
            P("section", None, None, None),
            P("section", None, None, "dp"),
            P("section", None, "dp"),
            P("section", "dp", None),
            P(None, None, "dp"),
        ),
        out_specs=(
            P(None, "section", "dp"),
            P("section", None, None, "dp"),
            P("section", None, "dp"),
            P("section", "dp", None),
        ),
        check_vma=False,
    )
```

time: 100 us -> 78.3 us (0.78)
  local copies, waits for them, and re-layouts: 27.3 us -> 4.48 us
  waiting for transfers between devices: 34 us -> 17.7 us
  Pallas kernels: 7.91 us -> 18.5 us
  starting transfers between devices: 27.3 us -> 33.1 us
  other arithmetic: 0.12 us -> 1.44 us
    unnamed x48 -> x17, local copies, waits for them, and re-layouts: 21.7 us -> 2.44 us
    all_to_all x2 -> x1, waiting for transfers between devices: 23.4 us -> 6.65 us  [to_all(): return lax.all_to_all(copies, axes, 0, 0, tiled=True)]
    ppermute x7 -> x10, starting transfers between devices: 10.1 us -> 17.1 us  [the longest x6 8.7 us: turn(): return lax.ppermute(value, ('section', 'dp'), pairs)]
    all_to_all x2 -> x1, starting transfers between devices: 12.3 us -> 6.59 us  [to_all(): return lax.all_to_all(copies, axes, 0, 0, tiled=True)]
    all_to_all x1, starting transfers between devices: 4.97 us -> 9.46 us  [per_device(): got_table = lax.all_to_all(table, ('section', 'dp'), 0, 0, tiled=True)]
    pallas_call x1, Pallas kernels: 4.29 us -> 8.06 us  [per_device(): call(tail_kernel, [((micro, own, width), BF16), ((slots, units), BF16), (...]
    pallas_call x1, Pallas kernels: 1.01 us -> 4.54 us  [per_device(): call(lambda *refs: side_kernel(*refs, tok=tok, cap=cap), [((full, slots +...]
    ppermute x7 -> x10, waiting for transfers between devices: 1.38 us -> 4.79 us  [the longest x6 3.91 us: turn(): return lax.ppermute(value, ('section', 'dp'), pairs)]
  transfers between devices with their start and end apart: 10 -> 12, of which waited for: 4 -> 4; matrix products, arithmetic and copies ran while one was open for 11% -> 4% of each run, Pallas kernels for 1% -> 6%
where the time goes in v3:
time: 78.3 us; the launch traced here: 77.9 us
  starting transfers between devices  33.1 us (42%)
  Pallas kernels  18.5 us (24%)
  waiting for transfers between devices  17.7 us (23%)
  local copies, waits for them, and re-layouts  4.48 us (6%)
  matrix products  1.75 us (2%)
  other arithmetic  1.44 us (2%)
  between operations  0.83 us (1%)
    all_to_all x1, starting transfers between devices, per_device(): got_table = lax.all_to_all(table, ('section', 'dp'), 0, 0, tiled=True)  9.46 us
    ppermute x6, starting transfers between devices, turn(): return lax.ppermute(value, ('section', 'dp'), pairs)  8.7 us
    ppermute x4, starting transfers between devices, swap(): return lax.ppermute(value, axis, [(i, i ^ distance) for i in range(count)])  8.36 us
    pallas_call x1, Pallas kernels, per_device(): call(tail_kernel, [((micro, own, width), BF16), ((slots, units), BF16), (...  8.06 us
    all_to_all x1, waiting for transfers between devices, to_all(): return lax.all_to_all(copies, axes, 0, 0, tiled=True)  6.65 us
    all_to_all x1, starting transfers between devices, to_all(): return lax.all_to_all(copies, axes, 0, 0, tiled=True)  6.59 us
    all_to_all x1, waiting for transfers between devices, per_device(): got_table = lax.all_to_all(table, ('section', 'dp'), 0, 0, tiled=True)  6.29 us
    pallas_call x1, Pallas kernels, per_device(): call(mid_kernel, [((sections * ways, sections, slots), BF16), ((slots, un...  5.93 us
  transfers between devices with their start and end apart: 12, of which 4 were waited for; matrix products, arithmetic and copies ran while one was open for 4% of the time, Pallas kernels for 6%

profile of v3, /device:TPU:1, one launch (start us, length us, event | category | flops | bytes accessed | tf_op | source)
XLA Modules:
  0.0 77.9 jit_solution(16018017653697606314)
XLA Ops:
  0.6 0.0 copy-start
  0.7 0.7 copy.10
  1.4 0.1 reshape_squeeze.9
  1.5 1.1 %fusion = f32[256]{0:T(256)S(1)} fusion(bf16[256,384]{1,0:T(8,128)(2,1)} %bitcast.45, bf16[1,384,8]{1,2,0:T(8,128)(2,1)} %param.12, f32[256]{0:T(256)S(1)} %get-tuple-element.45, f32[8]{0:T(128)S(1)} %compare_convert_fusion, f32[8]{0:T(128)S(1)} %iota_convert_fusion), kind=kOutput, calls=%fused_computation.2 | convolution fusion | flops 1582848 | bytes 204864 | tf_op jit(solution)/shard_map/dot_general | solution.py:20
  2.7 0.3 fusion.5
  3.0 0.0 copy-done
  3.0 0.2 convolution_convert_fusion
  3.2 0.1 convolution_convert_fusion.1
  3.4 4.7 %collective-permute-start.1 = (bf16[136,384]{1,0:T(8,128)(2,1)S(1)}, bf16[136,384]{1,0:T(8,128)(2,1)S(1)}, u32[]{:S(2)}, u32[]{:S(2)}) collective-permute-start(bf16[136,384]{1,0:T(8,128)(2,1)S(1)} %get-tuple-element.49), channel_id=1, source_target_pairs={{0,3},{1,2},{2,1},{3,0},{4,7},{5,6},{6,5},{7,4},{8,11},{9,10},{10,... | collective-permute-start | bytes 313352 | tf_op jit(solution)/shard_map/ppermute | solution.py:47
  8.0 0.0 collective-permute-start
  8.0 1.3 %collective-permute-start.2 = (bf16[136,384]{1,0:T(8,128)(2,1)S(1)}, bf16[136,384]{1,0:T(8,128)(2,1)S(1)}, u32[]{:S(2)}, u32[]{:S(2)}) collective-permute-start(bf16[136,384]{1,0:T(8,128)(2,1)S(1)} %get-tuple-element.49), channel_id=1, source_target_pairs={{0,2},{1,3},{2,0},{3,1},{4,6},{5,7},{6,4},{7,5},{8,10},{9,11},{10,... | collective-permute-start | bytes 313352 | tf_op jit(solution)/shard_map/ppermute | solution.py:47
  9.3 1.3 %broadcast_in_dim.10 = bf16[16,8,384]{2,1,0:T(8,128)(2,1)} broadcast(bf16[8,384]{1,0:T(8,128)(2,1)} %bitcast.55), dimensions={1,2} | broadcast | bytes 104448 | tf_op jit(solution)/shard_map/broadcast_in_dim | solution.py:32
  10.7 6.6 %all-to-all-start = ((bf16[16,8,384]{2,1,0:T(8,128)(2,1)}), bf16[16,8,384]{2,1,0:T(8,128)(2,1)S(1)}, u32[]{:S(2)}, u32[]{:S(2)}) async-start(bf16[16,8,384]{2,1,0:T(8,128)(2,1)} %broadcast_in_dim.10), calls=%async_computation | async-start | bytes 196608 | tf_op jit(solution)/shard_map/all_to_all | solution.py:33
  17.3 6.7 %all-to-all-done = bf16[16,8,384]{2,1,0:T(8,128)(2,1)S(1)} async-done(((bf16[16,8,384]{2,1,0:T(8,128)(2,1)}), bf16[16,8,384]{2,1,0:T(8,128)(2,1)S(1)}, u32[]{:S(2)}, u32[]{:S(2)}) %all-to-all-start) | async-done | bytes 98336 | tf_op jit(solution)/shard_map/all_to_all | solution.py:33
  23.9 2.6 %collective-permute-start.7 = (bf16[17,8,384]{2,1,0:T(8,128)(2,1)S(1)}, bf16[17,8,384]{2,1,0:T(8,128)(2,1)S(1)}, u32[]{:S(2)}, u32[]{:S(2)}) collective-permute-start(bf16[17,8,384]{2,1,0:T(8,128)(2,1)S(1)} %get-tuple-element.47), channel_id=1, source_target_pairs={{0,96},{16,112},{32,64},{48,80},{64,32},{80,48},{96,0},{112,16},{1... | collective-permute-start | bytes 313352 | tf_op jit(solution)/shard_map/ppermute | solution.py:38
  26.5 0.0 collective-permute-start.6
  26.5 0.0 collective-permute-done.1
  26.5 1.4 %collective-permute-start.8 = (bf16[17,8,384]{2,1,0:T(8,128)(2,1)S(1)}, bf16[17,8,384]{2,1,0:T(8,128)(2,1)S(1)}, u32[]{:S(2)}, u32[]{:S(2)}) collective-permute-start(bf16[17,8,384]{2,1,0:T(8,128)(2,1)S(1)} %get-tuple-element.47), channel_id=1, source_target_pairs={{0,64},{16,80},{32,96},{48,112},{64,0},{80,16},{96,32},{112,48},{1... | collective-permute-start | bytes 313352 | tf_op jit(solution)/shard_map/ppermute | solution.py:38
  27.9 0.0 collective-permute-done
  27.9 0.0 collective-permute-done.2
  27.9 0.1 pad_maximum_fusion.a0.refs_1_
  28.0 0.0 copy-start.1
  28.0 1.1 %collective-permute-start.5 = (bf16[4,136,384]{2,1,0:T(8,128)(2,1)S(1)}, bf16[4,136,384]{2,1,0:T(8,128)(2,1)S(1)}, u32[]{:S(2)}, u32[]{:S(2)}) collective-permute-start(bf16[4,136,384]{2,1,0:T(8,128)(2,1)S(1)} %pad_maximum_fusion.a0.refs_1_), channel_id=1, source_target_pairs={{0,8},{1,9},{2,10},{3,11},{4,12},{5,13},{6,14},{7,15},{8,0},{9,1},... | collective-permute-start | bytes 1253384 | tf_op jit(solution)/shard_map/ppermute | solution.py:47
  29.0 1.7 %collective-permute-start.4 = (bf16[4,136,384]{2,1,0:T(8,128)(2,1)S(1)}, bf16[4,136,384]{2,1,0:T(8,128)(2,1)S(1)}, u32[]{:S(2)}, u32[]{:S(2)}) collective-permute-start(bf16[4,136,384]{2,1,0:T(8,128)(2,1)S(1)} %pad_maximum_fusion.a0.refs_1_), channel_id=1, source_target_pairs={{0,12},{1,13},{2,14},{3,15},{4,8},{5,9},{6,10},{7,11},{8,4},{9,5},... | collective-permute-start | bytes 1253384 | tf_op jit(solution)/shard_map/ppermute | solution.py:47
  30.7 0.0 collective-permute-done.7
  30.7 0.0 collective-permute-start.3
  30.7 0.0 collective-permute-done.6
  30.7 0.9 %collective-permute-done.8 = bf16[17,8,384]{2,1,0:T(8,128)(2,1)S(1)} collective-permute-done((bf16[17,8,384]{2,1,0:T(8,128)(2,1)S(1)}, bf16[17,8,384]{2,1,0:T(8,128)(2,1)S(1)}, u32[]{:S(2)}, u32[]{:S(2)}) %collective-permute-start.8) | collective-permute-done | bytes 104480 | tf_op jit(solution)/shard_map/ppermute | solution.py:38
  31.6 0.1 pad_maximum_fusion.1.near_ref.refs_5_
  31.7 0.0 copy-start.2
  31.7 4.4 %collective-permute-start.9 = (bf16[4,17,8,384]{3,2,1,0:T(8,128)(2,1)S(1)}, bf16[4,17,8,384]{3,2,1,0:T(8,128)(2,1)S(1)}, u32[]{:S(2)}, u32[]{:S(2)}) collective-permute-start(bf16[4,17,8,384]{3,2,1,0:T(8,128)(2,1)S(1)} %pad_maximum_fusion.1.near_ref.refs_5_), channel_id=1, source_target_pairs={{0,16},{16,0},{32,48},{48,32},{64,80},{80,64},{96,112},{112,96},{1... | collective-permute-start | bytes 1253384 | tf_op jit(solution)/shard_map/ppermute | solution.py:38
  36.1 0.6 pad_add_fusion.here_ref.refs_0_
  36.7 0.6 fusion.4.pick_ref
  37.3 0.0 collective-permute-done.5.a3.refs_4_
  37.3 3.9 %collective-permute-done.4.a2.refs_3_ = bf16[4,136,384]{2,1,0:T(8,128)(2,1)S(1)} collective-permute-done((bf16[4,136,384]{2,1,0:T(8,128)(2,1)S(1)}, bf16[4,136,384]{2,1,0:T(8,128)(2,1)S(1)}, u32[]{:S(2)}, u32[]{:S(2)}) %collective-permute-start.4) | collective-permute-done | bytes 417824 | tf_op jit(solution)/shard_map/ppermute | solution.py:47
  41.2 0.0 collective-permute-done.3.a1.refs_2_
  41.2 0.0 collective-permute-done.9.far_ref.refs_6_
  41.2 0.0 copy-start.7
  41.3 0.7 copy-done.5
  42.0 0.2 copy-done.6
  42.1 0.2 copy-done.7
  42.3 5.9 %shard_map.93 = (bf16[128,8,128]{2,1,0:T(8,128)(2,1)}, f32[128,512]{1,0:T(8,128)}, bf16[64,512]{1,0:T(8,128)(2,1)}, f32[8,8,128]{2,1,0:T(8,128)}, f32[8,128]{1,0:T(8,128)}) custom-call(s32[2]{0:T(128)} %pad_add_fusion.here_ref.refs_0_, bf16[4,136,384]{2,1,0:T(8,128)(2,1)} %copy-done.1, bf16[4,136,384]{2,1,0:T(8,128)(2,1)} %copy-done.6, ...), custom_call_target="tpu_custom_call" | custom-call | flops 1207959552 | bytes 6291456 | tf_op jit(solution)/shard_map/pallas_call | solution.py:288
  48.2 9.5 %all-to-all-start.1 = ((bf16[128,8,128]{2,1,0:T(8,128)(2,1)}), bf16[128,8,128]{2,1,0:T(8,128)(2,1)S(1)}, u32[]{:S(2)}, u32[]{:S(2)}) async-start(bf16[128,8,128]{2,1,0:T(8,128)(2,1)} %get-tuple-element.30), calls=%async_computation.1 | async-start | bytes 524288 | tf_op jit(solution)/shard_map/all_to_all | solution.py:304
  57.7 0.6 constant_dynamic-slice_fusion.grads_ref
  58.3 4.5 %shard_map.94 = (bf16[6144,192]{1,0:T(8,128)(2,1)}, bf16[8,128,256]{2,1,0:T(8,128)(2,1)}, bf16[128,512]{1,0:T(8,128)(2,1)}, bf16[64,384]{1,0:T(8,128)(2,1)}, f32[8,256]{1,0:T(8,128)}) custom-call(s32[2]{0:T(128)} %pad_add_fusion.here_ref.refs_0_, bf16[4,136,384]{2,1,0:T(8,128)(2,1)} %copy-done.1, bf16[4,136,384]{2,1,0:T(8,128)(2,1)} %copy-done.6, ...), custom_call_target="tpu_custom_call" | custom-call | flops 1000000000 | bytes 4718592 | tf_op jit(solution)/shard_map/pallas_call | solution.py:306
  62.8 6.3 %all-to-all-done.1.got_ref = bf16[128,8,128]{2,1,0:T(8,128)(2,1)S(1)} async-done(((bf16[128,8,128]{2,1,0:T(8,128)(2,1)}), bf16[128,8,128]{2,1,0:T(8,128)(2,1)S(1)}, u32[]{:S(2)}, u32[]{:S(2)}) %all-to-all-start.1) | async-done | bytes 262176 | tf_op jit(solution)/shard_map/all_to_all | solution.py:304
  69.1 0.7 copy-done.3
  69.8 8.1 %shard_map.95 = (bf16[4,8,384]{2,1,0:T(8,128)(2,1)}, bf16[128,512]{1,0:T(8,128)(2,1)}, bf16[6144,512]{1,0:T(8,128)(2,1)}, f32[8,384]{1,0:T(8,128)}) custom-call(s32[2]{0:T(128)} %pad_add_fusion.here_ref.refs_0_, bf16[128,8,128]{2,1,0:T(8,128)(2,1)} %copy-done.3, bf16[8,128,256]{2,1,0:T(8,128)(2,1)} %get-tuple-element.32.picks_ref, ...), custom_call_target="tpu_custom_call" | custom-call | flops 1207959552 | bytes 6291456 | tf_op jit(solution)/shard_map/pallas_call | solution.py:322
  (20 shorter events, 0.1 us)
Async XLA Ops:
  0.6 2.4 %copy-start = (bf16[4,64,384]{2,1,0:T(8,128)(2,1)S(1)}, bf16[4,64,384]{2,1,0:T(8,128)(2,1)}, u32[]{:S(2)}) copy-start(bf16[4,64,384]{2,1,0:T(8,128)(2,1)} %param.13) | copy-start | bytes 589828
  3.4 23.1 %collective-permute-start.1 = (bf16[136,384]{1,0:T(8,128)(2,1)S(1)}, bf16[136,384]{1,0:T(8,128)(2,1)S(1)}, u32[]{:S(2)}, u32[]{:S(2)}) collective-permute-start(bf16[136,384]{1,0:T(8,128)(2,1)S(1)} %get-tuple-element.49), channel_id=1, source_target_pairs={{0,3},{1,2},{2,1},{3,0},{4,7},{5,6},{6,5},{7,4},{8,11},{9,10},{10,... | collective-permute-start | bytes 313352 | tf_op jit(solution)/shard_map/ppermute | solution.py:47
  8.0 19.9 %collective-permute-start = (bf16[136,384]{1,0:T(8,128)(2,1)S(1)}, bf16[136,384]{1,0:T(8,128)(2,1)S(1)}, u32[]{:S(2)}, u32[]{:S(2)}) collective-permute-start(bf16[136,384]{1,0:T(8,128)(2,1)S(1)} %get-tuple-element.49), channel_id=1, source_target_pairs={{0,1},{1,0},{2,3},{3,2},{4,5},{5,4},{6,7},{7,6},{8,9},{9,8},{10,11... | collective-permute-start | bytes 313352 | tf_op jit(solution)/shard_map/ppermute | solution.py:47
  8.0 19.9 %collective-permute-start.2 = (bf16[136,384]{1,0:T(8,128)(2,1)S(1)}, bf16[136,384]{1,0:T(8,128)(2,1)S(1)}, u32[]{:S(2)}, u32[]{:S(2)}) collective-permute-start(bf16[136,384]{1,0:T(8,128)(2,1)S(1)} %get-tuple-element.49), channel_id=1, source_target_pairs={{0,2},{1,3},{2,0},{3,1},{4,6},{5,7},{6,4},{7,5},{8,10},{9,11},{10,... | collective-permute-start | bytes 313352 | tf_op jit(solution)/shard_map/ppermute | solution.py:47
  10.7 13.3 %all-to-all-start = ((bf16[16,8,384]{2,1,0:T(8,128)(2,1)}), bf16[16,8,384]{2,1,0:T(8,128)(2,1)S(1)}, u32[]{:S(2)}, u32[]{:S(2)}) async-start(bf16[16,8,384]{2,1,0:T(8,128)(2,1)} %broadcast_in_dim.10), calls=%async_computation | async-start | bytes 196608 | tf_op jit(solution)/shard_map/all_to_all | solution.py:33
  23.9 6.8 %collective-permute-start.7 = (bf16[17,8,384]{2,1,0:T(8,128)(2,1)S(1)}, bf16[17,8,384]{2,1,0:T(8,128)(2,1)S(1)}, u32[]{:S(2)}, u32[]{:S(2)}) collective-permute-start(bf16[17,8,384]{2,1,0:T(8,128)(2,1)S(1)} %get-tuple-element.47), channel_id=1, source_target_pairs={{0,96},{16,112},{32,64},{48,80},{64,32},{80,48},{96,0},{112,16},{1... | collective-permute-start | bytes 313352 | tf_op jit(solution)/shard_map/ppermute | solution.py:38
  26.5 4.2 %collective-permute-start.6 = (bf16[17,8,384]{2,1,0:T(8,128)(2,1)S(1)}, bf16[17,8,384]{2,1,0:T(8,128)(2,1)S(1)}, u32[]{:S(2)}, u32[]{:S(2)}) collective-permute-start(bf16[17,8,384]{2,1,0:T(8,128)(2,1)S(1)} %get-tuple-element.47), channel_id=1, source_target_pairs={{0,32},{16,48},{32,0},{48,16},{64,96},{80,112},{96,64},{112,80},{1... | collective-permute-start | bytes 313352 | tf_op jit(solution)/shard_map/ppermute | solution.py:38
  26.5 5.1 %collective-permute-start.8 = (bf16[17,8,384]{2,1,0:T(8,128)(2,1)S(1)}, bf16[17,8,384]{2,1,0:T(8,128)(2,1)S(1)}, u32[]{:S(2)}, u32[]{:S(2)}) collective-permute-start(bf16[17,8,384]{2,1,0:T(8,128)(2,1)S(1)} %get-tuple-element.47), channel_id=1, source_target_pairs={{0,64},{16,80},{32,96},{48,112},{64,0},{80,16},{96,32},{112,48},{1... | collective-permute-start | bytes 313352 | tf_op jit(solution)/shard_map/ppermute | solution.py:38
  28.0 13.3 %copy-start.1 = (bf16[4,136,384]{2,1,0:T(8,128)(2,1)}, bf16[4,136,384]{2,1,0:T(8,128)(2,1)S(1)}, u32[]{:S(2)}) copy-start(bf16[4,136,384]{2,1,0:T(8,128)(2,1)S(1)} %pad_maximum_fusion.a0.refs_1_) | copy-start | bytes 1253380
  28.0 9.3 %collective-permute-start.5 = (bf16[4,136,384]{2,1,0:T(8,128)(2,1)S(1)}, bf16[4,136,384]{2,1,0:T(8,128)(2,1)S(1)}, u32[]{:S(2)}, u32[]{:S(2)}) collective-permute-start(bf16[4,136,384]{2,1,0:T(8,128)(2,1)S(1)} %pad_maximum_fusion.a0.refs_1_), channel_id=1, source_target_pairs={{0,8},{1,9},{2,10},{3,11},{4,12},{5,13},{6,14},{7,15},{8,0},{9,1},... | collective-permute-start | bytes 1253384 | tf_op jit(solution)/shard_map/ppermute | solution.py:47
  29.0 12.2 %collective-permute-start.4 = (bf16[4,136,384]{2,1,0:T(8,128)(2,1)S(1)}, bf16[4,136,384]{2,1,0:T(8,128)(2,1)S(1)}, u32[]{:S(2)}, u32[]{:S(2)}) collective-permute-start(bf16[4,136,384]{2,1,0:T(8,128)(2,1)S(1)} %pad_maximum_fusion.a0.refs_1_), channel_id=1, source_target_pairs={{0,12},{1,13},{2,14},{3,15},{4,8},{5,9},{6,10},{7,11},{8,4},{9,5},... | collective-permute-start | bytes 1253384 | tf_op jit(solution)/shard_map/ppermute | solution.py:47
  30.7 10.5 %collective-permute-start.3 = (bf16[4,136,384]{2,1,0:T(8,128)(2,1)S(1)}, bf16[4,136,384]{2,1,0:T(8,128)(2,1)S(1)}, u32[]{:S(2)}, u32[]{:S(2)}) collective-permute-start(bf16[4,136,384]{2,1,0:T(8,128)(2,1)S(1)} %pad_maximum_fusion.a0.refs_1_), channel_id=1, source_target_pairs={{0,4},{1,5},{2,6},{3,7},{4,0},{5,1},{6,2},{7,3},{8,12},{9,13},{10,... | collective-permute-start | bytes 1253384 | tf_op jit(solution)/shard_map/ppermute | solution.py:47
  31.7 9.6 %copy-start.2 = (bf16[4,17,8,384]{3,2,1,0:T(8,128)(2,1)}, bf16[4,17,8,384]{3,2,1,0:T(8,128)(2,1)S(1)}, u32[]{:S(2)}) copy-start(bf16[4,17,8,384]{3,2,1,0:T(8,128)(2,1)S(1)} %pad_maximum_fusion.1.near_ref.refs_5_) | copy-start | bytes 1253380
  31.7 9.5 %collective-permute-start.9 = (bf16[4,17,8,384]{3,2,1,0:T(8,128)(2,1)S(1)}, bf16[4,17,8,384]{3,2,1,0:T(8,128)(2,1)S(1)}, u32[]{:S(2)}, u32[]{:S(2)}) collective-permute-start(bf16[4,17,8,384]{3,2,1,0:T(8,128)(2,1)S(1)} %pad_maximum_fusion.1.near_ref.refs_5_), channel_id=1, source_target_pairs={{0,16},{16,0},{32,48},{48,32},{64,80},{80,64},{96,112},{112,96},{1... | collective-permute-start | bytes 1253384 | tf_op jit(solution)/shard_map/ppermute | solution.py:38
  37.3 3.9 %copy-start.4 = (bf16[4,136,384]{2,1,0:T(8,128)(2,1)}, bf16[4,136,384]{2,1,0:T(8,128)(2,1)S(1)}, u32[]{:S(2)}) copy-start(bf16[4,136,384]{2,1,0:T(8,128)(2,1)S(1)} %collective-permute-done.5.a3.refs_4_) | copy-start | bytes 1253380
  41.2 0.7 copy-start.5
  41.2 0.9 %copy-start.6 = (bf16[4,136,384]{2,1,0:T(8,128)(2,1)}, bf16[4,136,384]{2,1,0:T(8,128)(2,1)S(1)}, u32[]{:S(2)}) copy-start(bf16[4,136,384]{2,1,0:T(8,128)(2,1)S(1)} %collective-permute-done.3.a1.refs_2_) | copy-start | bytes 1253380
  41.2 1.0 %copy-start.7 = (bf16[4,17,8,384]{3,2,1,0:T(8,128)(2,1)}, bf16[4,17,8,384]{3,2,1,0:T(8,128)(2,1)S(1)}, u32[]{:S(2)}) copy-start(bf16[4,17,8,384]{3,2,1,0:T(8,128)(2,1)S(1)} %collective-permute-done.9.far_ref.refs_6_) | copy-start | bytes 1253380
  48.2 20.9 %all-to-all-start.1 = ((bf16[128,8,128]{2,1,0:T(8,128)(2,1)}), bf16[128,8,128]{2,1,0:T(8,128)(2,1)S(1)}, u32[]{:S(2)}, u32[]{:S(2)}) async-start(bf16[128,8,128]{2,1,0:T(8,128)(2,1)} %get-tuple-element.30), calls=%async_computation.1 | async-start | bytes 524288 | tf_op jit(solution)/shard_map/all_to_all | solution.py:304
  69.1 0.7 copy-start.3

commit v4 on v1

v4 whole, which is shorter than its diff:
```python
import jax
import jax.numpy as jnp
from jax import lax
from jax.experimental import pallas as pl
from jax.experimental.pallas import tpu as pltpu
from jax.sharding import PartitionSpec as P

F32 = jnp.float32
BF16 = jnp.bfloat16
HBM = pl.BlockSpec(memory_space=pltpu.HBM)
GRANT = 62 << 20
RING = (0, 1, 3, 2)
SECTION_STEPS = (2, 6, 4)
LAYER_ORDER = [d ^ core for core in (0, 1) for d in (0,) + SECTION_STEPS]


def nt(a, b):
    return lax.dot_general(a, b, (((1,), (1,)), ((), ())), preferred_element_type=F32)


def tn(a, b):
    return lax.dot_general(a, b, (((0,), (0,)), ((), ())), preferred_element_type=F32)


def nn(a, b):
    return jnp.dot(a, b, preferred_element_type=F32)


def swap(value, axis, distance):
    count = lax.axis_size(axis)
    return lax.ppermute(value, axis, [(i, i ^ distance) for i in range(count)])


def turn(value, stage, step):
    sections, ways = lax.axis_size("section"), lax.axis_size("dp")
    pairs = []
    for s in range(sections):
        distance = RING[step] * (1 if s % 2 == stage else 4)
        pairs += [(s * ways + p, s * ways + (p ^ distance)) for p in range(ways)]
    return lax.ppermute(value, ("section", "dp"), pairs)


def iota(shape, dim):
    return lax.broadcasted_iota(jnp.int32, shape, dim)


def slot_of(codes, tok, cap):
    tokens = codes.shape[1]
    row, col = iota((tokens, tokens), 0), iota((tokens, tokens), 1)
    before = ((row < col) & (row // tok == col // tok)).astype(F32).astype(BF16)
    member = codes > 0.0
    rank = nn(member.astype(F32).astype(BF16), before).astype(jnp.int32)
    return jnp.where(member, rank + (iota(codes.shape, 1) // tok) * cap, -1)


def expert_signs(codes):
    experts = iota((codes.shape[0], 8, codes.shape[1]), 1).astype(F32)
    return (experts == 0.0).astype(F32) - (experts == codes[:, None, :]).astype(F32)


def diagonal(size):
    return (iota((size, size), 0) == iota((size, size), 1)).astype(F32)


def block_of(at, odd, way):
    apart = at ^ way
    low, high = apart & 3, apart >> 2
    low, high = low ^ (low >> 1), high ^ (high >> 1)
    return jnp.where(odd, 4 * low + high, 4 * high + low)


def left_block(rows, near, far, j, slots):
    turned = 4 * (j & 3) + (j >> 2)
    size = slots + 16
    members = rows[pl.ds(pl.multiple_of(j * size, 16), slots), :]
    routers = [near[17 * k + j] for k in range(4)] + [far[17 * k + turned] for k in range(4)]
    return jnp.concatenate([members] + routers, axis=0)


def layer_codes(near, far, tokens):
    return jnp.concatenate(
        [ref[17 * k + 16, 0:1, :tokens].astype(F32) for ref in (near, far) for k in range(4)],
        axis=0,
    )


def split(value):
    first = value.astype(BF16)
    rest = value - first.astype(F32)
    second = rest.astype(BF16)
    return [first, second, (rest - second.astype(F32)).astype(BF16)]


def pre_kernel(ins, raws, outs, raw_outs, *, cap):
    ids, grads, x, router = ins
    block, pick_out, code_out, mine_out = outs
    slots, tokens = pick_out.ref.shape
    tok = ids.ref.shape[1]
    micro = tokens // tok
    left = jnp.concatenate([ids.ref[2 * m:2 * m + 1, :] for m in range(micro)], axis=1)
    right = jnp.concatenate([ids.ref[2 * m + 1:2 * m + 2, :] for m in range(micro)], axis=1)
    code = jnp.where(left == 0, right, jnp.where(right == 0, left, 0)).astype(F32)
    code = jnp.broadcast_to(code, (16, tokens))
    code_out.ref[...] = jnp.zeros(code_out.ref.shape, BF16)
    code_out.ref[:, :tokens] = code.astype(BF16)
    code_out.flush()
    slot = slot_of(code[:8], tok, cap)[0:1]
    pick = (iota((slots, tokens), 0) == slot).astype(F32).astype(BF16)
    pick_out.ref[...] = pick
    pick_out.flush()
    block.ref[:slots, :] = nn(pick, grads.ref[...]).astype(BF16)
    me, _, _ = place()
    count = mine_out.ref.shape[0]
    own = count // micro
    wanted = iota((count, 1), 0)
    wanted = (wanted // own) * tok + me * own + wanted % own
    choose = (iota((count, tokens), 1) == wanted).astype(F32).astype(BF16)
    mine_out.ref[...] = nn(choose, grads.ref[...]).astype(BF16)
    mine_out.flush()
    logits = nt(router.ref[...], x.ref[...])
    apart = -jnp.sum(expert_signs(code[0:1])[0] * logits, axis=0, keepdims=True)
    parts = jnp.concatenate(split(apart) + [jnp.zeros((5, tokens), BF16)], axis=0)
    parts = jnp.concatenate(
        [nt(parts, pick), jnp.zeros((8, block.ref.shape[1] - slots), F32)], axis=1
    )
    both = jnp.concatenate([router.ref[...].astype(F32), parts], axis=0)
    block.ref[slots:, :] = both.astype(BF16)


def logit_parts(rows, slots, ways):
    apart = jnp.zeros((8, slots), F32)
    for j in range(ways):
        at = j * (slots + 16) + slots
        apart += rows[at:at + 16, :slots].astype(F32)[8:]
    return apart


def mid_kernel(ins, raws, outs, raw_outs, rows, wbuf, sems):
    hid, pick, near, far = ins
    blocks, w_ref = raws[:4], raws[4]
    table_out, product_out, mixed_out, signs_out, gate_out = outs
    slots, width = hid.buffer.shape[0], near.buffer.shape[2]
    size = blocks[0].shape[0]
    ways = wbuf.shape[0] // width
    loads = [
        pltpu.make_async_copy(block, rows.at[pl.ds(n * size, size)], sems.at[n])
        for n, block in enumerate(blocks)
    ]
    depth = wbuf.shape[0] // 4
    loads += [
        pltpu.make_async_copy(
            w_ref.at[pl.ds(q * depth, depth)], wbuf.at[pl.ds(q * depth, depth)], sems.at[4 + q]
        )
        for q in range(4)
    ]
    for load in loads:
        load.start()
    me, at, odd = place()
    codes = layer_codes(near.ref, far.ref, pick.ref.shape[1])
    signs = expert_signs(nt(codes.astype(BF16), pick.ref[...]))
    layer = jnp.concatenate([jnp.full((1, 8, slots), d, jnp.int32) for d in LAYER_ORDER]) ^ me
    signs = jnp.where(layer > me, signs, 0.0)
    signs_out.ref[...] = signs
    filled = nt(jnp.ones((8, pick.buffer.shape[1]), BF16), pick.ref[...])
    for load in loads[:4]:
        load.wait()
    apart = jnp.sum(logit_parts(rows, slots, ways), axis=0, keepdims=True)
    gate = filled / (1.0 + jnp.exp(apart))
    gate_out.ref[...] = gate
    slope = gate * (1.0 - gate)
    total = jnp.zeros((slots + mixed_out.ref.shape[0], mixed_out.ref.shape[1]), F32)
    for way in range(0, ways, 2):
        left = jnp.concatenate([
            left_block(rows, near.ref, far.ref, block_of(at, odd, way + i), slots)
            for i in range(2)
        ], axis=1)
        if way % 4 == 0:
            loads[4 + way // 4].wait()
        total += nn(left, wbuf[way * width:(way + 2) * width])
    product, mixed = total[:slots], total[slots:].astype(BF16)
    base = jnp.sum(hid.ref[...].astype(F32) * product, axis=1, keepdims=True)
    base = jnp.sum(diagonal(slots) * base, axis=0, keepdims=True)
    cross = nt(mixed, hid.ref[...]).reshape(signs.shape)
    coefs = jnp.sum(signs * cross, axis=1)
    table = jnp.where(iota(coefs.shape, 0) == 0, base, coefs) * slope
    table = jnp.concatenate([table.astype(BF16)] * 2, axis=0)
    table_out.ref[...] = jnp.broadcast_to(table[None], table_out.ref.shape)
    table_out.flush()
    product_out.ref[...] = product
    mixed_out.ref[...] = mixed


def side_kernel(ins, raws, outs, raw_outs, *, tok, cap):
    near, far, hid, gate = ins
    picks_out, scaled_out, codes_out = outs
    slots = hid.buffer.shape[0]
    me, _, _ = place()
    codes = layer_codes(near.ref, far.ref, codes_out.ref.shape[1])
    codes_out.ref[...] = codes
    slot = slot_of(codes, tok, cap)
    for i, d in enumerate(LAYER_ORDER):
        pick = (iota((slots, slot.shape[1]), 0) == slot[i:i + 1]).astype(F32).astype(BF16)
        picks_out.ref[me ^ d] = pick
    gate_col = jnp.sum(diagonal(slots) * gate.ref[0:1], axis=1, keepdims=True)
    scaled_out.ref[...] = (gate_col * hid.ref[...].astype(F32)).astype(BF16)


def tail_kernel(ins, raws, outs, raw_outs, delta_ref, step_ref, rows, lsems, obuf, sems):
    got, picks, codes, signs, pick, scaled_in, near, far, product, mixed, gate, x, grads = ins
    blocks, down_ref = raws, raw_outs[0]
    input_out, hidden_out, router_out = outs
    layers, slots = codes.buffer.shape[0], gate.buffer.shape[1]
    tokens, width = codes.buffer.shape[1], x.buffer.shape[1]
    ways = obuf.shape[0] // width
    size = blocks[0].shape[0]
    loads = [
        pltpu.make_async_copy(block, rows.at[pl.ds(n * size, size)], lsems.at[n])
        for n, block in enumerate(blocks)
    ]
    for load in loads:
        load.start()
    me, at, odd = place()
    parts_of = []
    for s in range(layers):
        n = s * ways * 8
        table = jnp.sum(
            got.ref[n:n + ways * 8].astype(F32).reshape(ways, 8, slots), axis=0
        )
        parts = nn(jnp.concatenate(split(table), axis=0), picks.ref[s])
        parts_of.append(parts[:8] + parts[8:16] + parts[16:])
    deltas = [None] * layers
    for layer in range(layers - 1, -1, -1):
        value = parts_of[layer][0:1]
        for upper in range(layer + 1, layers):
            i = LAYER_ORDER.index(layer ^ upper)
            value += deltas[upper] * parts_of[layer][i:i + 1]
        deltas[layer] = value.astype(BF16).astype(F32)
        delta_ref[layer:layer + 1, :] = deltas[layer]
    mine = jnp.concatenate([delta_ref[pl.ds(me ^ d, 1), :] for d in LAYER_ORDER], axis=0)
    delta_slot = nt(mine.astype(BF16), pick.ref[...])
    lift = (signs.ref[...] * delta_slot[:, None, :]).reshape(layers * 8, slots).astype(BF16)
    scaled = scaled_in.ref[...]
    right = jnp.concatenate([scaled, nn(lift, scaled).astype(BF16)], axis=0)
    for load in loads:
        load.wait()
    copies = []
    for way in range(ways):
        left = left_block(rows, near.ref, far.ref, block_of(at, odd, way), slots)
        obuf[way * width:(way + 1) * width] = tn(left, right).astype(BF16)
        if way % 2 == 1:
            done = pl.ds((way - 1) * width, 2 * width)
            copies.append(
                pltpu.make_async_copy(obuf.at[done], down_ref.at[done], sems.at[way // 2])
            )
            copies[-1].start()
    gate_col = jnp.sum(diagonal(slots) * gate.ref[0:1], axis=1, keepdims=True)
    hidden = product.ref[...] + tn(lift, mixed.ref[...])
    hidden_out.ref[...] = (gate_col * hidden).astype(BF16)
    hidden_out.flush()
    logit_grads = expert_signs(codes.ref[...]) * mine[:, None, :]
    router_out.ref[...] = nn(logit_grads[0].astype(BF16), x.ref[...])
    router_out.flush()
    local = jnp.concatenate([ref[17 * k] for ref in (near.ref, far.ref) for k in range(4)], axis=0)
    step_ref[...] = tn(logit_grads.reshape(layers * 8, tokens).astype(BF16), local)
    count = 4
    own, tok = grads.buffer.shape[0] // count, tokens // count
    steps = jnp.concatenate([
        step_ref[pl.ds(pl.multiple_of(m * tok + me * own, 8), own), :] for m in range(count)
    ], axis=0)
    input_out.ref[...] = (grads.ref[...].astype(F32) + steps).astype(BF16)
    input_out.flush()
    for copy in copies:
        copy.wait()


class Staged:
    def __init__(self, source, buffer, semaphore):
        self.copy = pltpu.make_async_copy(source, buffer, semaphore)
        self.copy.start()
        self.buffer, self.waited = buffer, False

    @property
    def ref(self):
        if not self.waited:
            self.copy.wait()
            self.waited = True
        return self.buffer


class Result:
    def __init__(self, buffer, target, semaphore):
        self.ref, self.copy, self.sent = buffer, None, False
        self.parts = (buffer, target, semaphore)

    def flush(self):
        if not self.sent:
            self.copy = pltpu.make_async_copy(*self.parts)
            self.copy.start()
            self.sent = True


def call(kernel, staged, raw, results, raw_results=(), scratch=(), flops=0, moved=0):
    counts = (len(staged), len(raw), len(results), len(raw_results))

    def body(*refs):
        groups, at = [], 0
        for count in counts + (counts[0], counts[2]):
            groups.append(refs[at:at + count])
            at += count
        sources, raws, targets, raw_targets, ibufs, obufs = groups
        sems, rest = refs[at], refs[at + 1:]
        ins = [Staged(r, v, sems.at[n]) for n, (r, v) in enumerate(zip(sources, ibufs))]
        outs = [
            Result(v, r, sems.at[counts[0] + n]) for n, (r, v) in enumerate(zip(targets, obufs))
        ]
        kernel(ins, raws, outs, raw_targets, *rest)
        for item in ins:
            item.ref
        for item in outs:
            item.flush()
        for item in outs:
            item.copy.wait()

    shapes = [jax.ShapeDtypeStruct(*o) for o in results] + [
        jax.ShapeDtypeStruct(*o) for o in raw_results
    ]
    return pl.pallas_call(
        body,
        out_shape=shapes,
        in_specs=[HBM] * (counts[0] + counts[1]),
        out_specs=[HBM] * len(shapes),
        scratch_shapes=[pltpu.VMEM(v.shape, v.dtype) for v in staged]
        + [pltpu.VMEM(*o) for o in results]
        + [pltpu.SemaphoreType.DMA((counts[0] + counts[2],))]
        + list(scratch),
        compiler_params=pltpu.CompilerParams(vmem_limit_bytes=GRANT),
        cost_estimate=pl.CostEstimate(flops=flops, bytes_accessed=moved, transcendentals=0),
    )(*staged, *raw)


def place():
    me, at = lax.axis_index("section"), lax.axis_index("dp")
    return me, at, (me & 1) == 1


def per_device(layer_inputs, expert_ids, hidden, down_weight, router_weight, grad_out):
    sections, ways = lax.axis_size("section"), lax.axis_size("dp")
    micro, tok, width = grad_out.shape
    cap, units = hidden.shape[2:]
    experts = router_weight.shape[2]
    tokens, slots = micro * tok, micro * cap
    full = ways * width
    x = layer_inputs[0].reshape(tokens, width)
    hid = hidden[0].reshape(slots, units)
    router = router_weight[0].T
    grads = grad_out.reshape(tokens, width)

    own = tok // sections
    block, pick, code, grads_mine = call(
        lambda *refs: pre_kernel(*refs, cap=cap),
        [expert_ids[0].transpose(0, 2, 1).reshape(2 * micro, tok), grads, x, router],
        [],
        [((slots + 16, width), BF16), ((slots, tokens), BF16), ((16, width), BF16),
         ((micro * own, width), BF16)],
    )

    group = jnp.stack([block] + [turn(block, 0, step) for step in (1, 2, 3)])
    routers = group[:, slots:slots + experts]
    routers = [routers] + [turn(routers, 1, step) for step in (1, 2, 3)]
    blocks = [group] + [turn(group, 1, step) for step in (1, 2, 3)]
    blocks = [b.reshape(4 * (slots + 16), width) for b in blocks]
    mine = jnp.concatenate(routers + [code[None, :experts]])
    weights = down_weight[0]
    near = jnp.concatenate([mine] + [swap(mine, "section", d) for d in SECTION_STEPS])
    far = swap(near, "section", 1)

    rows_buffer = pltpu.VMEM((ways * (slots + 16), width), BF16)
    table, product, mixed, signs, gate = call(
        mid_kernel,
        [hid, pick, near, far],
        blocks + [weights],
        [
            ((sections * ways // 2, 2 * sections, slots), BF16),
            ((slots, units), F32),
            ((sections * experts, units), BF16),
            ((sections, experts, slots), F32),
            ((8, slots), F32),
        ],
        scratch=[rows_buffer, pltpu.VMEM((full, units), BF16), pltpu.SemaphoreType.DMA((8,))],
    )
    table = table.reshape(sections * ways, sections, slots)
    got_table = lax.all_to_all(table, ("section", "dp"), 0, 0, tiled=True)

    picks, scaled, codes = call(
        lambda *refs: side_kernel(*refs, tok=tok, cap=cap),
        [near, far, hid, gate],
        [],
        [
            ((sections, slots, tokens), BF16),
            ((slots, units), BF16),
            ((sections, tokens), F32),
        ],
        flops=10**9,
        moved=10**7,
    )
    input_grad, hidden_grad, router_grad, down_grad = call(
        tail_kernel,
        [
            got_table.reshape(-1, slots), picks, codes, signs, pick, scaled, near, far,
            product, mixed, gate, x, grads_mine,
        ],
        blocks,
        [
            ((micro * own, width), BF16),
            ((slots, units), BF16),
            ((experts, width), F32),
        ],
        raw_results=[((full, units), BF16)],
        scratch=[
            pltpu.VMEM((sections, tokens), F32),
            pltpu.VMEM((tokens, width), F32),
            rows_buffer,
            pltpu.SemaphoreType.DMA((4,)),
            pltpu.VMEM((full, units), BF16),
            pltpu.SemaphoreType.DMA((ways // 2,)),
        ],
        flops=2 * 192 * full * units,
        moved=full * units * 2,
    )
    return (
        input_grad.reshape(micro, own, width),
        hidden_grad.reshape(1, micro, cap, units),
        down_grad[None],
        router_grad.T[None],
    )


def solution(mesh):
    return jax.shard_map(
        per_device,
        mesh=mesh,
        in_specs=(
            P("section", None, None, "dp"),
            P("section", None, None, None),
            P("section", None, None, "dp"),
            P("section", None, "dp"),
            P("section", "dp", None),
            P(None, None, "dp"),
        ),
        out_specs=(
            P(None, "section", "dp"),
            P("section", None, None, "dp"),
            P("section", None, "dp"),
            P("section", "dp", None),
        ),
        check_vma=False,
    )
```

time: 98.4 us -> 73 us (0.74)
  waiting for transfers between devices: 49.3 us -> 23.4 us
  matrix products: 17.8 us -> 0 us
  Pallas kernels: 0 us -> 16.3 us
  starting transfers between devices: 19.8 us -> 28.9 us
  local copies, waits for them, and re-layouts: 7.89 us -> 2.3 us
  other arithmetic: 2.12 us -> 0.97 us
    all_to_all x3 -> x1, waiting for transfers between devices: 49.3 us -> 9.01 us  [per_device(): got_table = lax.all_to_all(table, ('section', 'dp'), 0, 0, tiled=True)]
    ppermute x0 -> x13, starting transfers between devices: none -> 22.2 us  [the longest x9 11.8 us: turn(): return lax.ppermute(value, ('section', 'dp'), pairs)]
    dot_general x15 -> x0, matrix products: 17.8 us -> none  [the longest x1 5.61 us: per_device(): jnp.einsum('pkd,kf->pdf', got[:, :-experts], right, preferred_element_typ...]
    pallas_call x0 -> x4, Pallas kernels: none -> 16.3 us  [call(): pl.pallas_call(body, out_shape=shapes, in_specs=[HBM] * (counts[0] + coun...]
    ppermute x0 -> x13, waiting for transfers between devices: none -> 14.4 us  [the longest x9 8.23 us: turn(): return lax.ppermute(value, ('section', 'dp'), pairs)]
    all_to_all x3 -> x1, starting transfers between devices: 19.8 us -> 6.76 us  [per_device(): got_table = lax.all_to_all(table, ('section', 'dp'), 0, 0, tiled=True)]
    broadcast_in_dim x4 -> x0, local copies, waits for them, and re-layouts: 3.2 us -> none  [the longest x3 3.19 us: to_all(): copies = jnp.broadcast_to(value[None], (count,) + value.shape)]
    squeeze x35 -> x0, local copies, waits for them, and re-layouts: 2.84 us -> none  [the longest x28 2.27 us: per_device(): value = value + deltas[upper] * table[layer, upper]]
  transfers between devices with their start and end apart: 3 -> 14, of which waited for: 3 -> 6; matrix products, arithmetic and copies ran while one was open for 4% -> 0% of each run, Pallas kernels for 0% -> 3%
where the time goes in v4:
time: 73 us; the launch traced here: 72.7 us
  starting transfers between devices  28.9 us (40%)
  waiting for transfers between devices  23.4 us (32%)
  Pallas kernels  16.3 us (22%)
  local copies, waits for them, and re-layouts  2.3 us (3%)
  other arithmetic  0.97 us (1%)
  between operations  0.77 us (1%)
    pallas_call x4, Pallas kernels, call(): pl.pallas_call(body, out_shape=shapes, in_specs=[HBM] * (counts[0] + coun...  16.3 us
    ppermute x9, starting transfers between devices, turn(): return lax.ppermute(value, ('section', 'dp'), pairs)  11.8 us
    ppermute x4, starting transfers between devices, swap(): return lax.ppermute(value, axis, [(i, i ^ distance) for i in range(count)])  10.3 us
    all_to_all x1, waiting for transfers between devices, per_device(): got_table = lax.all_to_all(table, ('section', 'dp'), 0, 0, tiled=True)  9.01 us
    ppermute x9, waiting for transfers between devices, turn(): return lax.ppermute(value, ('section', 'dp'), pairs)  8.23 us
    all_to_all x1, starting transfers between devices, per_device(): got_table = lax.all_to_all(table, ('section', 'dp'), 0, 0, tiled=True)  6.76 us
    ppermute x4, waiting for transfers between devices, swap(): return lax.ppermute(value, axis, [(i, i ^ distance) for i in range(count)])  6.17 us
    unnamed x20, local copies, waits for them, and re-layouts  1.58 us
  transfers between devices with their start and end apart: 14, of which 6 were waited for; matrix products, arithmetic and copies ran while one was open for 0% of the time, Pallas kernels for 3%

profile of v4, /device:TPU:1, one launch (start us, length us, event | category | flops | bytes accessed | tf_op | source)
XLA Modules:
  0.0 72.7 jit_solution(2293581468211339102)
XLA Ops:
  0.6 2.2 %shard_map.93 = (bf16[144,384]{1,0:T(8,128)(2,1)}, bf16[128,256]{1,0:T(8,128)(2,1)}, bf16[16,384]{1,0:T(8,128)(2,1)}, bf16[32,384]{1,0:T(8,128)(2,1)}) custom-call(s32[8,64]{1,0:T(8,128)} %bitcast.52, bf16[256,384]{1,0:T(8,128)(2,1)} %bitcast.42, bf16[256,384]{1,0:T(8,128)(2,1)} %bitcast.43, bf16[8,384]{1,0:T(8,128)(2,1)} %bitcast.51), custom_call_target="tpu_custom_call" | custom-call | tf_op jit(solution)/shard_map/pallas_call | solution.py:327
  2.9 4.5 %collective-permute-start.2 = (bf16[144,384]{1,0:T(8,128)(2,1)}, bf16[144,384]{1,0:T(8,128)(2,1)S(1)}, u32[]{:S(2)}, u32[]{:S(2)}) collective-permute-start(bf16[144,384]{1,0:T(8,128)(2,1)} %get-tuple-element.21), channel_id=1, source_target_pairs={{0,2},{1,3},{2,0},{3,1},{4,6},{5,7},{6,4},{7,5},{8,10},{9,11},{10,... | collective-permute-start | bytes 331784 | tf_op jit(solution)/shard_map/ppermute | solution.py:40
  7.4 0.4 collective-permute-start.1
  7.8 0.3 collective-permute-start
  8.1 1.9 %collective-permute-done.2 = bf16[144,384]{1,0:T(8,128)(2,1)S(1)} collective-permute-done((bf16[144,384]{1,0:T(8,128)(2,1)}, bf16[144,384]{1,0:T(8,128)(2,1)S(1)}, u32[]{:S(2)}, u32[]{:S(2)}) %collective-permute-start.2) | collective-permute-done | bytes 110624 | tf_op jit(solution)/shard_map/ppermute | solution.py:40
  10.0 2.7 %collective-permute-done.1 = bf16[144,384]{1,0:T(8,128)(2,1)S(1)} collective-permute-done((bf16[144,384]{1,0:T(8,128)(2,1)}, bf16[144,384]{1,0:T(8,128)(2,1)S(1)}, u32[]{:S(2)}, u32[]{:S(2)}) %collective-permute-start.1) | collective-permute-done | bytes 110624 | tf_op jit(solution)/shard_map/ppermute | solution.py:40
  12.7 0.0 collective-permute-done
  12.7 1.0 %pad_maximum_fusion = bf16[4,144,384]{2,1,0:T(8,128)(2,1)S(1)} fusion(bf16[1,144,384]{2,1,0:T(8,128)(2,1)S(1)} %bitcast.48, bf16[1,144,384]{2,1,0:T(8,128)(2,1)S(1)} %bitcast.49, bf16[1,144,384]{2,1,0:T(8,128)(2,1)S(1)} %bitcast.50, bf16[1,144,384]{2,1,0:T(8,128)(2,1)} %bitcast.47), kind=kLoop, calls=%fused_computation | loop fusion | flops 663552 | bytes 884736 | tf_op jit(solution)/shard_map/stack | solution.py:367
  13.7 0.0 copy-start
  13.7 1.1 %collective-permute-start.3 = (bf16[4,8,384]{2,1,0:T(8,128)(2,1)S(1)}, bf16[4,8,384]{2,1,0:T(8,128)(2,1)S(1)}, u32[]{:S(2)}, u32[]{:S(2)}) collective-permute-start(bf16[4,8,384]{2,1,0:T(8,128)(2,1)S(1)} %get-tuple-element.38), channel_id=1, source_target_pairs={{0,4},{1,5},{2,6},{3,7},{4,0},{5,1},{6,2},{7,3},{8,12},{9,13},{10,... | collective-permute-start | bytes 73736 | tf_op jit(solution)/shard_map/ppermute | solution.py:40
  14.8 2.6 %collective-permute-start.5 = (bf16[4,8,384]{2,1,0:T(8,128)(2,1)S(1)}, bf16[4,8,384]{2,1,0:T(8,128)(2,1)S(1)}, u32[]{:S(2)}, u32[]{:S(2)}) collective-permute-start(bf16[4,8,384]{2,1,0:T(8,128)(2,1)S(1)} %get-tuple-element.38), channel_id=1, source_target_pairs={{0,8},{1,9},{2,10},{3,11},{4,12},{5,13},{6,14},{7,15},{8,0},{9,1},... | collective-permute-start | bytes 73736 | tf_op jit(solution)/shard_map/ppermute | solution.py:40
  17.4 0.2 collective-permute-start.4
  17.6 0.0 collective-permute-done.3
  17.6 3.6 %collective-permute-done.4 = bf16[4,8,384]{2,1,0:T(8,128)(2,1)S(1)} collective-permute-done((bf16[4,8,384]{2,1,0:T(8,128)(2,1)S(1)}, bf16[4,8,384]{2,1,0:T(8,128)(2,1)S(1)}, u32[]{:S(2)}, u32[]{:S(2)}) %collective-permute-start.4) | collective-permute-done | bytes 24608 | tf_op jit(solution)/shard_map/ppermute | solution.py:40
  21.3 0.0 collective-permute-done.5
  21.3 0.7 constant_dynamic-update-slice_fusion
  22.0 1.2 %collective-permute-start.6 = (bf16[17,8,384]{2,1,0:T(8,128)(2,1)S(1)}, bf16[17,8,384]{2,1,0:T(8,128)(2,1)S(1)}, u32[]{:S(2)}, u32[]{:S(2)}) collective-permute-start(bf16[17,8,384]{2,1,0:T(8,128)(2,1)S(1)} %get-tuple-element.45), channel_id=1, source_target_pairs={{0,32},{16,48},{32,0},{48,16},{64,96},{80,112},{96,64},{112,80},{1... | collective-permute-start | bytes 313352 | tf_op jit(solution)/shard_map/ppermute | solution.py:31
  23.2 0.3 collective-permute-start.12
  23.5 0.8 %collective-permute-start.11 = (bf16[4,144,384]{2,1,0:T(8,128)(2,1)S(1)}, bf16[4,144,384]{2,1,0:T(8,128)(2,1)S(1)}, u32[]{:S(2)}, u32[]{:S(2)}) collective-permute-start(bf16[4,144,384]{2,1,0:T(8,128)(2,1)S(1)} %pad_maximum_fusion), channel_id=1, source_target_pairs={{0,12},{1,13},{2,14},{3,15},{4,8},{5,9},{6,10},{7,11},{8,4},{9,5},... | collective-permute-start | bytes 1327112 | tf_op jit(solution)/shard_map/ppermute | solution.py:40
  24.3 1.6 %collective-permute-start.10 = (bf16[4,144,384]{2,1,0:T(8,128)(2,1)S(1)}, bf16[4,144,384]{2,1,0:T(8,128)(2,1)S(1)}, u32[]{:S(2)}, u32[]{:S(2)}) collective-permute-start(bf16[4,144,384]{2,1,0:T(8,128)(2,1)S(1)} %pad_maximum_fusion), channel_id=1, source_target_pairs={{0,4},{1,5},{2,6},{3,7},{4,0},{5,1},{6,2},{7,3},{8,12},{9,13},{10,... | collective-permute-start | bytes 1327112 | tf_op jit(solution)/shard_map/ppermute | solution.py:40
  25.9 2.4 %collective-permute-start.8 = (bf16[17,8,384]{2,1,0:T(8,128)(2,1)S(1)}, bf16[17,8,384]{2,1,0:T(8,128)(2,1)S(1)}, u32[]{:S(2)}, u32[]{:S(2)}) collective-permute-start(bf16[17,8,384]{2,1,0:T(8,128)(2,1)S(1)} %get-tuple-element.45), channel_id=1, source_target_pairs={{0,64},{16,80},{32,96},{48,112},{64,0},{80,16},{96,32},{112,48},{1... | collective-permute-start | bytes 313352 | tf_op jit(solution)/shard_map/ppermute | solution.py:31
  28.3 0.0 collective-permute-done.6
  28.3 0.2 collective-permute-start.7
  28.5 4.8 %collective-permute-done.7 = bf16[17,8,384]{2,1,0:T(8,128)(2,1)S(1)} collective-permute-done((bf16[17,8,384]{2,1,0:T(8,128)(2,1)S(1)}, bf16[17,8,384]{2,1,0:T(8,128)(2,1)S(1)}, u32[]{:S(2)}, u32[]{:S(2)}) %collective-permute-start.7) | collective-permute-done | bytes 104480 | tf_op jit(solution)/shard_map/ppermute | solution.py:31
  33.4 0.0 collective-permute-done.8
  33.4 0.0 copy-start.1
  33.4 6.5 %collective-permute-start.9 = (bf16[68,8,384]{2,1,0:T(8,128)(2,1)S(1)}, bf16[68,8,384]{2,1,0:T(8,128)(2,1)S(1)}, u32[]{:S(2)}, u32[]{:S(2)}) collective-permute-start(bf16[68,8,384]{2,1,0:T(8,128)(2,1)S(1)} %constant_dynamic-update-slice_fusion.5.refs_2_.refs_0_.refs_6_), channel_id=1, source_target_pairs={{0,16},{16,0},{32,48},{48,32},{64,80},{80,64},{96,112},{112,96},{1... | collective-permute-start | bytes 1253384 | tf_op jit(solution)/shard_map/ppermute | solution.py:31
  39.9 0.0 collective-permute-done.12
  39.9 0.0 copy-start.2
  39.9 0.0 collective-permute-done.11
  39.9 0.0 copy-start.3
  39.9 0.0 collective-permute-done.10
  40.0 0.0 copy-start.4
  40.0 1.3 %collective-permute-done.9.refs_3_.refs_1_.refs_7_ = bf16[68,8,384]{2,1,0:T(8,128)(2,1)S(1)} collective-permute-done((bf16[68,8,384]{2,1,0:T(8,128)(2,1)S(1)}, bf16[68,8,384]{2,1,0:T(8,128)(2,1)S(1)}, u32[]{:S(2)}, u32[]{:S(2)}) %collective-permute-start.9) | collective-permute-done | bytes 417824 | tf_op jit(solution)/shard_map/ppermute | solution.py:31
  41.3 0.0 copy-done.4
  41.3 0.0 copy-start.5
  41.3 0.7 %copy-done.5 = bf16[68,8,384]{2,1,0:T(8,128)(2,1)} copy-done((bf16[68,8,384]{2,1,0:T(8,128)(2,1)}, bf16[68,8,384]{2,1,0:T(8,128)(2,1)S(1)}, u32[]{:S(2)}) %copy-start.5) | copy-done | bytes 417816
  42.1 0.0 copy-done
  42.1 0.0 copy-done.1
  42.1 0.0 copy-done.2
  42.1 0.0 copy-done.3
  42.1 6.2 %shard_map.94 = (bf16[64,16,128]{2,1,0:T(8,128)(2,1)}, f32[128,512]{1,0:T(8,128)}, bf16[64,512]{1,0:T(8,128)(2,1)}, f32[8,8,128]{2,1,0:T(8,128)}, f32[8,128]{1,0:T(8,128)}) custom-call(bf16[128,512]{1,0:T(8,128)(2,1)} %bitcast.45, bf16[128,256]{1,0:T(8,128)(2,1)} %get-tuple-element.20.refs_1_.refs_4_, bf16[68,8,384]{2,1,0:T(8,128)(2,1)} %copy-done.1, ...), custom_call_target="tpu_custom_call" | custom-call | tf_op jit(solution)/shard_map/pallas_call | solution.py:327
  48.2 6.8 %all-to-all-start = ((bf16[128,8,128]{2,1,0:T(8,128)(2,1)}), bf16[128,8,128]{2,1,0:T(8,128)(2,1)S(1)}, u32[]{:S(2)}, u32[]{:S(2)}) async-start(bf16[128,8,128]{2,1,0:T(8,128)(2,1)} %bitcast.41), calls=%async_computation | async-start | bytes 524288 | tf_op jit(solution)/shard_map/all_to_all | solution.py:392
  55.0 2.4 %shard_map.95 = (bf16[8,128,256]{2,1,0:T(8,128)(2,1)}, bf16[128,512]{1,0:T(8,128)(2,1)}, f32[8,256]{1,0:T(8,128)}) custom-call(bf16[68,8,384]{2,1,0:T(8,128)(2,1)} %copy-done.1, bf16[68,8,384]{2,1,0:T(8,128)(2,1)} %copy-done.5, bf16[128,512]{1,0:T(8,128)(2,1)} %bitcast.46, f32[8,128]{1,0:T(8,128)} %get-tuple-element.24.refs_3_.refs_10_), custom_call_target="tpu_custom_call" | custom-call | flops 1000000000 | bytes 10000000 | tf_op jit(solution)/shard_map/pallas_call | solution.py:327
  57.5 9.0 %all-to-all-done = bf16[128,8,128]{2,1,0:T(8,128)(2,1)S(1)} async-done(((bf16[128,8,128]{2,1,0:T(8,128)(2,1)}), bf16[128,8,128]{2,1,0:T(8,128)(2,1)S(1)}, u32[]{:S(2)}, u32[]{:S(2)}) %all-to-all-start) | async-done | bytes 262176 | tf_op jit(solution)/shard_map/all_to_all | solution.py:392
  66.5 0.0 copy-start.6
  66.5 0.7 %copy-done.6 = bf16[128,8,128]{2,1,0:T(8,128)(2,1)} copy-done((bf16[128,8,128]{2,1,0:T(8,128)(2,1)}, bf16[128,8,128]{2,1,0:T(8,128)(2,1)S(1)}, u32[]{:S(2)}) %copy-start.6) | copy-done | bytes 262168
  67.2 5.5 %shard_map.96 = (bf16[32,384]{1,0:T(8,128)(2,1)}, bf16[128,512]{1,0:T(8,128)(2,1)}, f32[8,384]{1,0:T(8,128)}, bf16[6144,512]{1,0:T(8,128)(2,1)}) custom-call(bf16[1024,128]{1,0:T(8,128)(2,1)} %bitcast.40, bf16[8,128,256]{2,1,0:T(8,128)(2,1)} %get-tuple-element.25.refs_1_, f32[8,256]{1,0:T(8,128)} %get-tuple-element.26.refs_2_, ...), custom_call_target="tpu_custom_call" | custom-call | flops 1207959552 | bytes 6291456 | tf_op jit(solution)/shard_map/pallas_call | solution.py:327
  (7 shorter events, 0.1 us)
Async XLA Ops:
  2.9 7.2 %collective-permute-start.2 = (bf16[144,384]{1,0:T(8,128)(2,1)}, bf16[144,384]{1,0:T(8,128)(2,1)S(1)}, u32[]{:S(2)}, u32[]{:S(2)}) collective-permute-start(bf16[144,384]{1,0:T(8,128)(2,1)} %get-tuple-element.21), channel_id=1, source_target_pairs={{0,2},{1,3},{2,0},{3,1},{4,6},{5,7},{6,4},{7,5},{8,10},{9,11},{10,... | collective-permute-start | bytes 331784 | tf_op jit(solution)/shard_map/ppermute | solution.py:40
  7.4 5.3 %collective-permute-start.1 = (bf16[144,384]{1,0:T(8,128)(2,1)}, bf16[144,384]{1,0:T(8,128)(2,1)S(1)}, u32[]{:S(2)}, u32[]{:S(2)}) collective-permute-start(bf16[144,384]{1,0:T(8,128)(2,1)} %get-tuple-element.21), channel_id=1, source_target_pairs={{0,3},{1,2},{2,1},{3,0},{4,7},{5,6},{6,5},{7,4},{8,11},{9,10},{10,... | collective-permute-start | bytes 331784 | tf_op jit(solution)/shard_map/ppermute | solution.py:40
  7.8 4.9 %collective-permute-start = (bf16[144,384]{1,0:T(8,128)(2,1)}, bf16[144,384]{1,0:T(8,128)(2,1)S(1)}, u32[]{:S(2)}, u32[]{:S(2)}) collective-permute-start(bf16[144,384]{1,0:T(8,128)(2,1)} %get-tuple-element.21), channel_id=1, source_target_pairs={{0,1},{1,0},{2,3},{3,2},{4,5},{5,4},{6,7},{7,6},{8,9},{9,8},{10,11... | collective-permute-start | bytes 331784 | tf_op jit(solution)/shard_map/ppermute | solution.py:40
  13.7 28.4 %copy-start = (bf16[4,144,384]{2,1,0:T(8,128)(2,1)}, bf16[4,144,384]{2,1,0:T(8,128)(2,1)S(1)}, u32[]{:S(2)}) copy-start(bf16[4,144,384]{2,1,0:T(8,128)(2,1)S(1)} %pad_maximum_fusion) | copy-start | bytes 1327108
  13.7 3.9 %collective-permute-start.3 = (bf16[4,8,384]{2,1,0:T(8,128)(2,1)S(1)}, bf16[4,8,384]{2,1,0:T(8,128)(2,1)S(1)}, u32[]{:S(2)}, u32[]{:S(2)}) collective-permute-start(bf16[4,8,384]{2,1,0:T(8,128)(2,1)S(1)} %get-tuple-element.38), channel_id=1, source_target_pairs={{0,4},{1,5},{2,6},{3,7},{4,0},{5,1},{6,2},{7,3},{8,12},{9,13},{10,... | collective-permute-start | bytes 73736 | tf_op jit(solution)/shard_map/ppermute | solution.py:40
  14.8 6.5 %collective-permute-start.5 = (bf16[4,8,384]{2,1,0:T(8,128)(2,1)S(1)}, bf16[4,8,384]{2,1,0:T(8,128)(2,1)S(1)}, u32[]{:S(2)}, u32[]{:S(2)}) collective-permute-start(bf16[4,8,384]{2,1,0:T(8,128)(2,1)S(1)} %get-tuple-element.38), channel_id=1, source_target_pairs={{0,8},{1,9},{2,10},{3,11},{4,12},{5,13},{6,14},{7,15},{8,0},{9,1},... | collective-permute-start | bytes 73736 | tf_op jit(solution)/shard_map/ppermute | solution.py:40
  17.4 3.9 %collective-permute-start.4 = (bf16[4,8,384]{2,1,0:T(8,128)(2,1)S(1)}, bf16[4,8,384]{2,1,0:T(8,128)(2,1)S(1)}, u32[]{:S(2)}, u32[]{:S(2)}) collective-permute-start(bf16[4,8,384]{2,1,0:T(8,128)(2,1)S(1)} %get-tuple-element.38), channel_id=1, source_target_pairs={{0,12},{1,13},{2,14},{3,15},{4,8},{5,9},{6,10},{7,11},{8,4},{9,5},... | collective-permute-start | bytes 73736 | tf_op jit(solution)/shard_map/ppermute | solution.py:40
  22.0 6.3 %collective-permute-start.6 = (bf16[17,8,384]{2,1,0:T(8,128)(2,1)S(1)}, bf16[17,8,384]{2,1,0:T(8,128)(2,1)S(1)}, u32[]{:S(2)}, u32[]{:S(2)}) collective-permute-start(bf16[17,8,384]{2,1,0:T(8,128)(2,1)S(1)} %get-tuple-element.45), channel_id=1, source_target_pairs={{0,32},{16,48},{32,0},{48,16},{64,96},{80,112},{96,64},{112,80},{1... | collective-permute-start | bytes 313352 | tf_op jit(solution)/shard_map/ppermute | solution.py:31
  23.2 16.7 %collective-permute-start.12 = (bf16[4,144,384]{2,1,0:T(8,128)(2,1)S(1)}, bf16[4,144,384]{2,1,0:T(8,128)(2,1)S(1)}, u32[]{:S(2)}, u32[]{:S(2)}) collective-permute-start(bf16[4,144,384]{2,1,0:T(8,128)(2,1)S(1)} %pad_maximum_fusion), channel_id=1, source_target_pairs={{0,8},{1,9},{2,10},{3,11},{4,12},{5,13},{6,14},{7,15},{8,0},{9,1},... | collective-permute-start | bytes 1327112 | tf_op jit(solution)/shard_map/ppermute | solution.py:40
  23.5 16.4 %collective-permute-start.11 = (bf16[4,144,384]{2,1,0:T(8,128)(2,1)S(1)}, bf16[4,144,384]{2,1,0:T(8,128)(2,1)S(1)}, u32[]{:S(2)}, u32[]{:S(2)}) collective-permute-start(bf16[4,144,384]{2,1,0:T(8,128)(2,1)S(1)} %pad_maximum_fusion), channel_id=1, source_target_pairs={{0,12},{1,13},{2,14},{3,15},{4,8},{5,9},{6,10},{7,11},{8,4},{9,5},... | collective-permute-start | bytes 1327112 | tf_op jit(solution)/shard_map/ppermute | solution.py:40
  24.3 15.7 %collective-permute-start.10 = (bf16[4,144,384]{2,1,0:T(8,128)(2,1)S(1)}, bf16[4,144,384]{2,1,0:T(8,128)(2,1)S(1)}, u32[]{:S(2)}, u32[]{:S(2)}) collective-permute-start(bf16[4,144,384]{2,1,0:T(8,128)(2,1)S(1)} %pad_maximum_fusion), channel_id=1, source_target_pairs={{0,4},{1,5},{2,6},{3,7},{4,0},{5,1},{6,2},{7,3},{8,12},{9,13},{10,... | collective-permute-start | bytes 1327112 | tf_op jit(solution)/shard_map/ppermute | solution.py:40
  25.9 7.5 %collective-permute-start.8 = (bf16[17,8,384]{2,1,0:T(8,128)(2,1)S(1)}, bf16[17,8,384]{2,1,0:T(8,128)(2,1)S(1)}, u32[]{:S(2)}, u32[]{:S(2)}) collective-permute-start(bf16[17,8,384]{2,1,0:T(8,128)(2,1)S(1)} %get-tuple-element.45), channel_id=1, source_target_pairs={{0,64},{16,80},{32,96},{48,112},{64,0},{80,16},{96,32},{112,48},{1... | collective-permute-start | bytes 313352 | tf_op jit(solution)/shard_map/ppermute | solution.py:31
  28.3 5.0 %collective-permute-start.7 = (bf16[17,8,384]{2,1,0:T(8,128)(2,1)S(1)}, bf16[17,8,384]{2,1,0:T(8,128)(2,1)S(1)}, u32[]{:S(2)}, u32[]{:S(2)}) collective-permute-start(bf16[17,8,384]{2,1,0:T(8,128)(2,1)S(1)} %get-tuple-element.45), channel_id=1, source_target_pairs={{0,96},{16,112},{32,64},{48,80},{64,32},{80,48},{96,0},{112,16},{1... | collective-permute-start | bytes 313352 | tf_op jit(solution)/shard_map/ppermute | solution.py:31
  33.4 8.6 %copy-start.1 = (bf16[68,8,384]{2,1,0:T(8,128)(2,1)}, bf16[68,8,384]{2,1,0:T(8,128)(2,1)S(1)}, u32[]{:S(2)}) copy-start(bf16[68,8,384]{2,1,0:T(8,128)(2,1)S(1)} %constant_dynamic-update-slice_fusion.5.refs_2_.refs_0_.refs_6_) | copy-start | bytes 1253380
  33.4 7.9 %collective-permute-start.9 = (bf16[68,8,384]{2,1,0:T(8,128)(2,1)S(1)}, bf16[68,8,384]{2,1,0:T(8,128)(2,1)S(1)}, u32[]{:S(2)}, u32[]{:S(2)}) collective-permute-start(bf16[68,8,384]{2,1,0:T(8,128)(2,1)S(1)} %constant_dynamic-update-slice_fusion.5.refs_2_.refs_0_.refs_6_), channel_id=1, source_target_pairs={{0,16},{16,0},{32,48},{48,32},{64,80},{80,64},{96,112},{112,96},{1... | collective-permute-start | bytes 1253384 | tf_op jit(solution)/shard_map/ppermute | solution.py:31
  39.9 2.1 %copy-start.2 = (bf16[4,144,384]{2,1,0:T(8,128)(2,1)}, bf16[4,144,384]{2,1,0:T(8,128)(2,1)S(1)}, u32[]{:S(2)}) copy-start(bf16[4,144,384]{2,1,0:T(8,128)(2,1)S(1)} %collective-permute-done.12) | copy-start | bytes 1327108
  39.9 2.1 %copy-start.3 = (bf16[4,144,384]{2,1,0:T(8,128)(2,1)}, bf16[4,144,384]{2,1,0:T(8,128)(2,1)S(1)}, u32[]{:S(2)}) copy-start(bf16[4,144,384]{2,1,0:T(8,128)(2,1)S(1)} %collective-permute-done.11) | copy-start | bytes 1327108
  40.0 1.4 %copy-start.4 = (bf16[4,144,384]{2,1,0:T(8,128)(2,1)}, bf16[4,144,384]{2,1,0:T(8,128)(2,1)S(1)}, u32[]{:S(2)}) copy-start(bf16[4,144,384]{2,1,0:T(8,128)(2,1)S(1)} %collective-permute-done.10) | copy-start | bytes 1327108
  41.3 0.7 %copy-start.5 = (bf16[68,8,384]{2,1,0:T(8,128)(2,1)}, bf16[68,8,384]{2,1,0:T(8,128)(2,1)S(1)}, u32[]{:S(2)}) copy-start(bf16[68,8,384]{2,1,0:T(8,128)(2,1)S(1)} %collective-permute-done.9.refs_3_.refs_1_.refs_7_) | copy-start | bytes 1253380
  48.2 18.2 %all-to-all-start = ((bf16[128,8,128]{2,1,0:T(8,128)(2,1)}), bf16[128,8,128]{2,1,0:T(8,128)(2,1)S(1)}, u32[]{:S(2)}, u32[]{:S(2)}) async-start(bf16[128,8,128]{2,1,0:T(8,128)(2,1)} %bitcast.41), calls=%async_computation | async-start | bytes 524288 | tf_op jit(solution)/shard_map/all_to_all | solution.py:392
  66.5 0.7 %copy-start.6 = (bf16[128,8,128]{2,1,0:T(8,128)(2,1)}, bf16[128,8,128]{2,1,0:T(8,128)(2,1)S(1)}, u32[]{:S(2)}) copy-start(bf16[128,8,128]{2,1,0:T(8,128)(2,1)S(1)} %all-to-all-done) | copy-start | bytes 786436

commit v5 on v4

--- a/solution.py
+++ b/solution.py
@@ -135,26 +135,48 @@
     return apart
 
 
-def mid_kernel(ins, raws, outs, raw_outs, rows, wbuf, sems):
-    hid, pick, near, far = ins
-    blocks, w_ref = raws[:4], raws[4]
-    table_out, product_out, mixed_out, signs_out, gate_out = outs
-    slots, width = hid.buffer.shape[0], near.buffer.shape[2]
+def load_weights(w_ref, wbuf, sems, first):
+    count = sems.shape[0]
+    depth = wbuf.shape[0] // count
+    copies = [
+        pltpu.make_async_copy(
+            w_ref.at[pl.ds(first + q * depth, depth)], wbuf.at[pl.ds(q * depth, depth)], sems.at[q]
+        )
+        for q in range(count)
+    ]
+    for copy in copies:
+        copy.start()
+    return copies
+
+
+def load_rows(blocks, rows, sems):
     size = blocks[0].shape[0]
-    ways = wbuf.shape[0] // width
     loads = [
         pltpu.make_async_copy(block, rows.at[pl.ds(n * size, size)], sems.at[n])
         for n, block in enumerate(blocks)
     ]
-    depth = wbuf.shape[0] // 4
-    loads += [
-        pltpu.make_async_copy(
-            w_ref.at[pl.ds(q * depth, depth)], wbuf.at[pl.ds(q * depth, depth)], sems.at[4 + q]
-        )
-        for q in range(4)
-    ]
     for load in loads:
         load.start()
+    return loads
+
+
+def back_kernel(ins, raws, outs, raw_outs, wbuf, sems, *, first):
+    hid, back = ins[0], outs[0]
+    copies = load_weights(raws[0], wbuf, sems, first)
+    depth = wbuf.shape[0] // len(copies)
+    hidden = hid.ref[...].T
+    for q, copy in enumerate(copies):
+        copy.wait()
+        for part in range(4):
+            rows = pl.ds(q * depth + part * (depth // 4), depth // 4)
+            back.ref[rows, :] = nn(wbuf[rows, :], hidden).astype(BF16)
+
+
+def mid_kernel(ins, raws, outs, raw_outs, rows, sems):
+    pick, near, far, low, high = ins
+    table_out, signs_out, gate_out = outs
+    slots, width = pick.buffer.shape[0], near.buffer.shape[2]
+    loads = load_rows(raws, rows, sems)
     me, at, odd = place()
     codes = layer_codes(near.ref, far.ref, pick.ref.shape[1])
     signs = expert_signs(nt(codes.astype(BF16), pick.ref[...]))
@@ -162,47 +184,62 @@
     signs = jnp.where(layer > me, signs, 0.0)
     signs_out.ref[...] = signs
     filled = nt(jnp.ones((8, pick.buffer.shape[1]), BF16), pick.ref[...])
-    for load in loads[:4]:
+    for load in loads:
         load.wait()
+    halves = (low.ref, high.ref)
+    ways = 2 * (low.buffer.shape[0] // width)
     apart = jnp.sum(logit_parts(rows, slots, ways), axis=0, keepdims=True)
     gate = filled / (1.0 + jnp.exp(apart))
     gate_out.ref[...] = gate
     slope = gate * (1.0 - gate)
+    total = jnp.zeros((slots + signs.shape[0] * 8, slots), F32)
+    for way in range(0, ways, 2):
+        left = jnp.concatenate([
+            left_block(rows, near.ref, far.ref, block_of(at, odd, way + i), slots)
+            for i in range(2)
+        ], axis=1)
+        at_row = way % (ways // 2) * width
+        total += nn(left, halves[way * 2 // ways][at_row:at_row + 2 * width])
+    base = jnp.sum(diagonal(slots) * total[:slots], axis=0, keepdims=True)
+    coefs = jnp.sum(signs * total[slots:].reshape(signs.shape), axis=1)
+    table = jnp.where(iota(coefs.shape, 0) == 0, base, coefs) * slope
+    table = jnp.concatenate([table.astype(BF16)] * 2, axis=0)
+    table_out.ref[...] = jnp.broadcast_to(table[None], table_out.ref.shape)
+    table_out.flush()
+
+
+def side_kernel(ins, raws, outs, raw_outs, rows, lsems, wbuf, sems, *, tok, cap):
+    near, far, hid, gate = ins
+    picks_out, scaled_out, codes_out, product_out, mixed_out = outs
+    slots, width = hid.buffer.shape[0], near.buffer.shape[2]
+    loads = load_rows(raws[:4], rows, lsems)
+    copies = load_weights(raws[4], wbuf, sems, 0)
+    me, at, odd = place()
+    codes = layer_codes(near.ref, far.ref, codes_out.ref.shape[1])
+    codes_out.ref[...] = codes
+    codes_out.flush()
+    slot = slot_of(codes, tok, cap)
+    for i, d in enumerate(LAYER_ORDER):
+        pick = (iota((slots, slot.shape[1]), 0) == slot[i:i + 1]).astype(F32).astype(BF16)
+        picks_out.ref[me ^ d] = pick
+    picks_out.flush()
+    gate_col = jnp.sum(diagonal(slots) * gate.ref[0:1], axis=1, keepdims=True)
+    scaled_out.ref[...] = (gate_col * hid.ref[...].astype(F32)).astype(BF16)
+    scaled_out.flush()
+    for load in loads:
+        load.wait()
+    ways = wbuf.shape[0] // width
     total = jnp.zeros((slots + mixed_out.ref.shape[0], mixed_out.ref.shape[1]), F32)
     for way in range(0, ways, 2):
         left = jnp.concatenate([
             left_block(rows, near.ref, far.ref, block_of(at, odd, way + i), slots)
             for i in range(2)
         ], axis=1)
-        if way % 4 == 0:
-            loads[4 + way // 4].wait()
+        if way * len(copies) % ways == 0:
+            copies[way * len(copies) // ways].wait()
         total += nn(left, wbuf[way * width:(way + 2) * width])
-    product, mixed = total[:slots], total[slots:].astype(BF16)
-    base = jnp.sum(hid.ref[...].astype(F32) * product, axis=1, keepdims=True)
-    base = jnp.sum(diagonal(slots) * base, axis=0, keepdims=True)
-    cross = nt(mixed, hid.ref[...]).reshape(signs.shape)
-    coefs = jnp.sum(signs * cross, axis=1)
-    table = jnp.where(iota(coefs.shape, 0) == 0, base, coefs) * slope
-    table = jnp.concatenate([table.astype(BF16)] * 2, axis=0)
-    table_out.ref[...] = jnp.broadcast_to(table[None], table_out.ref.shape)
-    table_out.flush()
-    product_out.ref[...] = product
-    mixed_out.ref[...] = mixed
-
-
-def side_kernel(ins, raws, outs, raw_outs, *, tok, cap):
-    near, far, hid, gate = ins
-    picks_out, scaled_out, codes_out = outs
-    slots = hid.buffer.shape[0]
-    me, _, _ = place()
-    codes = layer_codes(near.ref, far.ref, codes_out.ref.shape[1])
-    codes_out.ref[...] = codes
-    slot = slot_of(codes, tok, cap)
-    for i, d in enumerate(LAYER_ORDER):
-        pick = (iota((slots, slot.shape[1]), 0) == slot[i:i + 1]).astype(F32).astype(BF16)
-        picks_out.ref[me ^ d] = pick
-    gate_col = jnp.sum(diagonal(slots) * gate.ref[0:1], axis=1, keepdims=True)
-    scaled_out.ref[...] = (gate_col * hid.ref[...].astype(F32)).astype(BF16)
+    product_out.ref[...] = total[:slots]
+    mixed_out.ref[...] = total[slots:].astype(BF16)
 
 
 def tail_kernel(ins, raws, outs, raw_outs, delta_ref, step_ref, rows, lsems, obuf, sems):
@@ -212,13 +249,7 @@
     layers, slots = codes.buffer.shape[0], gate.buffer.shape[1]
     tokens, width = codes.buffer.shape[1], x.buffer.shape[1]
     ways = obuf.shape[0] // width
-    size = blocks[0].shape[0]
-    loads = [
-        pltpu.make_async_copy(block, rows.at[pl.ds(n * size, size)], lsems.at[n])
-        for n, block in enumerate(blocks)
-    ]
-    for load in loads:
-        load.start()
+    loads = load_rows(blocks, rows, lsems)
     me, at, odd = place()
     parts_of = []
     for s in range(layers):
@@ -364,41 +395,63 @@
          ((micro * own, width), BF16)],
     )
 
-    group = jnp.stack([block] + [turn(block, 0, step) for step in (1, 2, 3)])
-    routers = group[:, slots:slots + experts]
+    weights = down_weight[0]
+
+    def back(after, first):
+        after, hid_after = lax.optimization_barrier((after, hid))
+        return after, call(
+            lambda *refs: back_kernel(*refs, first=first),
+            [hid_after],
+            [weights],
+            [((full // 2, slots), BF16)],
+            scratch=[pltpu.VMEM((full // 2, units), BF16), pltpu.SemaphoreType.DMA((2,))],
+            moved=full * units,
+        )[0]
+
+    block, low = back(block, 0)
+    group = [block] + [turn(block, 0, step) for step in (1, 2, 3)]
+    group, low = lax.optimization_barrier((group, low))
+    group = jnp.stack(group)
+    routers, high = back(group[:, slots:slots + experts], full // 2)
     routers = [routers] + [turn(routers, 1, step) for step in (1, 2, 3)]
+    routers, high = lax.optimization_barrier((routers, high))
     blocks = [group] + [turn(group, 1, step) for step in (1, 2, 3)]
     blocks = [b.reshape(4 * (slots + 16), width) for b in blocks]
     mine = jnp.concatenate(routers + [code[None, :experts]])
-    weights = down_weight[0]
     near = jnp.concatenate([mine] + [swap(mine, "section", d) for d in SECTION_STEPS])
     far = swap(near, "section", 1)
 
     rows_buffer = pltpu.VMEM((ways * (slots + 16), width), BF16)
-    table, product, mixed, signs, gate = call(
+    table, signs, gate = call(
         mid_kernel,
-        [hid, pick, near, far],
-        blocks + [weights],
+        [pick, near, far, low, high],
+        blocks,
         [
             ((sections * ways // 2, 2 * sections, slots), BF16),
-            ((slots, units), F32),
-            ((sections * experts, units), BF16),
             ((sections, experts, slots), F32),
             ((8, slots), F32),
         ],
-        scratch=[rows_buffer, pltpu.VMEM((full, units), BF16), pltpu.SemaphoreType.DMA((8,))],
+        scratch=[rows_buffer, pltpu.SemaphoreType.DMA((4,))],
     )
     table = table.reshape(sections * ways, sections, slots)
     got_table = lax.all_to_all(table, ("section", "dp"), 0, 0, tiled=True)
 
-    picks, scaled, codes = call(
+    picks, scaled, codes, product, mixed = call(
         lambda *refs: side_kernel(*refs, tok=tok, cap=cap),
         [near, far, hid, gate],
-        [],
+        blocks + [weights],
         [
             ((sections, slots, tokens), BF16),
             ((slots, units), BF16),
             ((sections, tokens), F32),
+            ((slots, units), F32),
+            ((sections * experts, units), BF16),
+        ],
+        scratch=[
+            rows_buffer,
+            pltpu.SemaphoreType.DMA((4,)),
+            pltpu.VMEM((full, units), BF16),
+            pltpu.SemaphoreType.DMA((4,)),
         ],
         flops=10**9,
         moved=10**7,

time: 73 us -> 69.1 us (0.947)
  waiting for transfers between devices: 23.4 us -> 12.9 us
  Pallas kernels: 16.3 us -> 24.3 us
  other arithmetic: 0.97 us -> 0.07 us
    pallas_call x4 -> x6, Pallas kernels: 16.3 us -> 24.3 us  [call(): pl.pallas_call(body, out_shape=shapes, in_specs=[HBM] * (counts[0] + coun...]
    ppermute x9, waiting for transfers between devices: 8.23 us -> 1.12 us  [turn(): return lax.ppermute(value, ('section', 'dp'), pairs)]
    all_to_all x1, waiting for transfers between devices: 9.01 us -> 5.58 us  [per_device(): got_table = lax.all_to_all(table, ('section', 'dp'), 0, 0, tiled=True)]
    ppermute x4, starting transfers between devices: 10.3 us -> 8.61 us  [swap(): return lax.ppermute(value, axis, [(i, i ^ distance) for i in range(count)])]
    all_to_all x1, starting transfers between devices: 6.76 us -> 7.96 us  [per_device(): got_table = lax.all_to_all(table, ('section', 'dp'), 0, 0, tiled=True)]
    another operation x1, other arithmetic: 0.97 us -> 0.07 us  [per_device(): group = jnp.stack(group)]
    unnamed x20 -> x24, local copies, waits for them, and re-layouts: 1.58 us -> 1.57 us
  transfers between devices with their start and end apart: 14 -> 14, of which waited for: 6 -> 4; matrix products, arithmetic and copies ran while one was open for 0% -> 0% of each run, Pallas kernels for 3% -> 19%
where the time goes in v5:
time: 69.1 us; the launch traced here: 68.9 us
  starting transfers between devices  29.1 us (42%)
  Pallas kernels  24.3 us (35%)
  waiting for transfers between devices  12.9 us (19%)
  local copies, waits for them, and re-layouts  1.61 us (2%)
  between operations  0.85 us (1%)
    pallas_call x6, Pallas kernels, call(): pl.pallas_call(body, out_shape=shapes, in_specs=[HBM] * (counts[0] + coun...  24.3 us
    ppermute x9, starting transfers between devices, turn(): return lax.ppermute(value, ('section', 'dp'), pairs)  12.6 us
    ppermute x4, starting transfers between devices, swap(): return lax.ppermute(value, axis, [(i, i ^ distance) for i in range(count)])  8.61 us
    all_to_all x1, starting transfers between devices, per_device(): got_table = lax.all_to_all(table, ('section', 'dp'), 0, 0, tiled=True)  7.96 us
    ppermute x4, waiting for transfers between devices, swap(): return lax.ppermute(value, axis, [(i, i ^ distance) for i in range(count)])  6.17 us
    all_to_all x1, waiting for transfers between devices, per_device(): got_table = lax.all_to_all(table, ('section', 'dp'), 0, 0, tiled=True)  5.58 us
    unnamed x24, local copies, waits for them, and re-layouts  1.57 us
  transfers between devices with their start and end apart: 14, of which 4 were waited for; matrix products, arithmetic and copies ran while one was open for 0% of the time, Pallas kernels for 19%

profile of v5, /device:TPU:1, one launch (start us, length us, event | category | flops | bytes accessed | tf_op | source)
XLA Modules:
  0.0 68.9 jit_solution(7872048649925332398)
XLA Ops:
  0.6 2.2 %shard_map.93 = (bf16[144,384]{1,0:T(8,128)(2,1)}, bf16[128,256]{1,0:T(8,128)(2,1)}, bf16[16,384]{1,0:T(8,128)(2,1)}, bf16[32,384]{1,0:T(8,128)(2,1)}) custom-call(s32[8,64]{1,0:T(8,128)} %bitcast.59, bf16[256,384]{1,0:T(8,128)(2,1)} %bitcast.51, bf16[256,384]{1,0:T(8,128)(2,1)} %bitcast.52, bf16[8,384]{1,0:T(8,128)(2,1)} %bitcast.58), custom_call_target="tpu_custom_call" | custom-call | tf_op jit(solution)/shard_map/pallas_call | solution.py:358
  2.9 0.0 copy-start.7
  2.9 4.5 %collective-permute-start.2 = (bf16[144,384]{1,0:T(8,128)(2,1)}, bf16[144,384]{1,0:T(8,128)(2,1)S(1)}, u32[]{:S(2)}, u32[]{:S(2)}) collective-permute-start(bf16[144,384]{1,0:T(8,128)(2,1)} %get-tuple-element.38), channel_id=1, source_target_pairs={{0,2},{1,3},{2,0},{3,1},{4,6},{5,7},{6,4},{7,5},{8,10},{9,11},{10,... | collective-permute-start | bytes 331784 | tf_op jit(solution)/shard_map/ppermute | solution.py:40
  7.4 0.4 collective-permute-start.1
  7.8 0.3 collective-permute-start
  8.1 3.5 %shard_map.94.refs_3_ = bf16[3072,128]{1,0:T(8,128)(2,1)} custom-call(bf16[128,512]{1,0:T(8,128)(2,1)} %bitcast.46, bf16[6144,512]{1,0:T(8,128)(2,1)} %bitcast.31), custom_call_target="tpu_custom_call" | custom-call | bytes 3145728 | tf_op jit(solution)/shard_map/pallas_call | solution.py:358
  11.6 0.0 collective-permute-done.2
  11.6 1.1 %collective-permute-done.1 = bf16[144,384]{1,0:T(8,128)(2,1)S(1)} collective-permute-done((bf16[144,384]{1,0:T(8,128)(2,1)}, bf16[144,384]{1,0:T(8,128)(2,1)S(1)}, u32[]{:S(2)}, u32[]{:S(2)}) %collective-permute-start.1) | collective-permute-done | bytes 110624 | tf_op jit(solution)/shard_map/ppermute | solution.py:40
  12.7 0.0 collective-permute-done
  12.7 0.0 copy-done.7
  12.7 0.1 pad_maximum_fusion
  12.8 0.0 copy-start
  12.8 2.7 %collective-permute-start.5 = (bf16[4,8,384]{2,1,0:T(8,128)(2,1)S(1)}, bf16[4,8,384]{2,1,0:T(8,128)(2,1)S(1)}, u32[]{:S(2)}, u32[]{:S(2)}) collective-permute-start(bf16[4,8,384]{2,1,0:T(8,128)(2,1)S(1)} %slice.8), channel_id=1, source_target_pairs={{0,8},{1,9},{2,10},{3,11},{4,12},{5,13},{6,14},{7,15},{8,0},{9,1},... | collective-permute-start | bytes 73736 | tf_op jit(solution)/shard_map/ppermute | solution.py:40
  15.5 0.8 %collective-permute-start.4 = (bf16[4,8,384]{2,1,0:T(8,128)(2,1)S(1)}, bf16[4,8,384]{2,1,0:T(8,128)(2,1)S(1)}, u32[]{:S(2)}, u32[]{:S(2)}) collective-permute-start(bf16[4,8,384]{2,1,0:T(8,128)(2,1)S(1)} %slice.8), channel_id=1, source_target_pairs={{0,12},{1,13},{2,14},{3,15},{4,8},{5,9},{6,10},{7,11},{8,4},{9,5},... | collective-permute-start | bytes 73736 | tf_op jit(solution)/shard_map/ppermute | solution.py:40
  16.3 0.0 collective-permute-start.3
  16.3 3.5 %shard_map.95.refs_4_ = bf16[3072,128]{1,0:T(8,128)(2,1)} custom-call(bf16[128,512]{1,0:T(8,128)(2,1)} %bitcast.47, bf16[6144,512]{1,0:T(8,128)(2,1)} %bitcast.32), custom_call_target="tpu_custom_call" | custom-call | bytes 3145728 | tf_op jit(solution)/shard_map/pallas_call | solution.py:358
  19.8 0.0 collective-permute-done.5
  19.8 0.0 collective-permute-done.4
  19.8 0.0 collective-permute-done.3
  19.9 0.0 copy-done.8
  19.9 1.3 %collective-permute-start.6 = (bf16[17,8,384]{2,1,0:T(8,128)(2,1)S(1)}, bf16[17,8,384]{2,1,0:T(8,128)(2,1)S(1)}, u32[]{:S(2)}, u32[]{:S(2)}) collective-permute-start(bf16[17,8,384]{2,1,0:T(8,128)(2,1)S(1)} %get-tuple-element.72), channel_id=1, source_target_pairs={{0,32},{16,48},{32,0},{48,16},{64,96},{80,112},{96,64},{112,80},{1... | collective-permute-start | bytes 313352 | tf_op jit(solution)/shard_map/ppermute | solution.py:31
  21.2 3.1 %collective-permute-start.12 = (bf16[4,144,384]{2,1,0:T(8,128)(2,1)S(1)}, bf16[4,144,384]{2,1,0:T(8,128)(2,1)S(1)}, u32[]{:S(2)}, u32[]{:S(2)}) collective-permute-start(bf16[4,144,384]{2,1,0:T(8,128)(2,1)S(1)} %pad_maximum_fusion), channel_id=1, source_target_pairs={{0,8},{1,9},{2,10},{3,11},{4,12},{5,13},{6,14},{7,15},{8,0},{9,1},... | collective-permute-start | bytes 1327112 | tf_op jit(solution)/shard_map/ppermute | solution.py:40
  24.2 0.8 %collective-permute-start.11 = (bf16[4,144,384]{2,1,0:T(8,128)(2,1)S(1)}, bf16[4,144,384]{2,1,0:T(8,128)(2,1)S(1)}, u32[]{:S(2)}, u32[]{:S(2)}) collective-permute-start(bf16[4,144,384]{2,1,0:T(8,128)(2,1)S(1)} %pad_maximum_fusion), channel_id=1, source_target_pairs={{0,12},{1,13},{2,14},{3,15},{4,8},{5,9},{6,10},{7,11},{8,4},{9,5},... | collective-permute-start | bytes 1327112 | tf_op jit(solution)/shard_map/ppermute | solution.py:40
  25.0 0.0 collective-permute-start.10
  25.0 2.5 %collective-permute-start.8 = (bf16[17,8,384]{2,1,0:T(8,128)(2,1)S(1)}, bf16[17,8,384]{2,1,0:T(8,128)(2,1)S(1)}, u32[]{:S(2)}, u32[]{:S(2)}) collective-permute-start(bf16[17,8,384]{2,1,0:T(8,128)(2,1)S(1)} %get-tuple-element.72), channel_id=1, source_target_pairs={{0,64},{16,80},{32,96},{48,112},{64,0},{80,16},{96,32},{112,48},{1... | collective-permute-start | bytes 313352 | tf_op jit(solution)/shard_map/ppermute | solution.py:31
  27.5 0.0 collective-permute-done.6
  27.5 0.2 collective-permute-start.7
  27.7 4.8 %collective-permute-done.7 = bf16[17,8,384]{2,1,0:T(8,128)(2,1)S(1)} collective-permute-done((bf16[17,8,384]{2,1,0:T(8,128)(2,1)S(1)}, bf16[17,8,384]{2,1,0:T(8,128)(2,1)S(1)}, u32[]{:S(2)}, u32[]{:S(2)}) %collective-permute-start.7) | collective-permute-done | bytes 104480 | tf_op jit(solution)/shard_map/ppermute | solution.py:31
  32.5 0.0 collective-permute-done.8
  32.6 0.0 copy-start.1
  32.6 4.6 %collective-permute-start.9 = (bf16[68,8,384]{2,1,0:T(8,128)(2,1)S(1)}, bf16[68,8,384]{2,1,0:T(8,128)(2,1)S(1)}, u32[]{:S(2)}, u32[]{:S(2)}) collective-permute-start(bf16[68,8,384]{2,1,0:T(8,128)(2,1)S(1)} %constant_dynamic-update-slice_fusion.5.refs_1_.refs_0_.refs_6_), channel_id=1, source_target_pairs={{0,16},{16,0},{32,48},{48,32},{64,80},{80,64},{96,112},{112,96},{1... | collective-permute-start | bytes 1253384 | tf_op jit(solution)/shard_map/ppermute | solution.py:31
  37.2 0.0 collective-permute-done.12
  37.3 0.0 collective-permute-done.11
  37.3 0.0 copy-start.3
  37.3 0.0 collective-permute-done.10
  37.3 0.0 copy-start.4
  37.3 1.3 %collective-permute-done.9.refs_2_.refs_1_.refs_7_ = bf16[68,8,384]{2,1,0:T(8,128)(2,1)S(1)} collective-permute-done((bf16[68,8,384]{2,1,0:T(8,128)(2,1)S(1)}, bf16[68,8,384]{2,1,0:T(8,128)(2,1)S(1)}, u32[]{:S(2)}, u32[]{:S(2)}) %collective-permute-start.9) | collective-permute-done | bytes 417824 | tf_op jit(solution)/shard_map/ppermute | solution.py:31
  38.6 0.0 copy-done.4
  38.6 0.8 %copy-done.5 = bf16[68,8,384]{2,1,0:T(8,128)(2,1)} copy-done((bf16[68,8,384]{2,1,0:T(8,128)(2,1)}, bf16[68,8,384]{2,1,0:T(8,128)(2,1)S(1)}, u32[]{:S(2)}) %copy-start.5) | copy-done | bytes 417816
  39.4 0.0 copy-done
  39.4 0.0 copy-done.1
  39.4 0.0 copy-done.3
  39.4 3.8 %shard_map.96 = (bf16[64,16,128]{2,1,0:T(8,128)(2,1)}, f32[8,8,128]{2,1,0:T(8,128)}, f32[8,128]{1,0:T(8,128)}) custom-call(bf16[128,256]{1,0:T(8,128)(2,1)} %get-tuple-element.34.refs_0_.refs_4_, bf16[68,8,384]{2,1,0:T(8,128)(2,1)} %copy-done.1, bf16[68,8,384]{2,1,0:T(8,128)(2,1)} %copy-done.5, bf16[3072,128]{1,0:T(8,128)(2,1)} %shard_map.94.refs_3_, ...), custom_call_target="tpu_custom_call" | custom-call | tf_op jit(solution)/shard_map/pallas_call | solution.py:358
  43.2 8.0 %all-to-all-start = ((bf16[128,8,128]{2,1,0:T(8,128)(2,1)}), bf16[128,8,128]{2,1,0:T(8,128)(2,1)S(1)}, u32[]{:S(2)}, u32[]{:S(2)}) async-start(bf16[128,8,128]{2,1,0:T(8,128)(2,1)} %bitcast.50), calls=%async_computation | async-start | bytes 524288 | tf_op jit(solution)/shard_map/all_to_all | solution.py:437
  51.2 5.9 %shard_map.97 = (bf16[8,128,256]{2,1,0:T(8,128)(2,1)}, bf16[128,512]{1,0:T(8,128)(2,1)}, f32[8,256]{1,0:T(8,128)}, f32[128,512]{1,0:T(8,128)}, bf16[64,512]{1,0:T(8,128)(2,1)}) custom-call(bf16[68,8,384]{2,1,0:T(8,128)(2,1)} %copy-done.1, bf16[68,8,384]{2,1,0:T(8,128)(2,1)} %copy-done.5, bf16[128,512]{1,0:T(8,128)(2,1)} %bitcast.48, ...), custom_call_target="tpu_custom_call" | custom-call | flops 1000000000 | bytes 10000000 | tf_op jit(solution)/shard_map/pallas_call | solution.py:358
  57.1 5.6 %all-to-all-done = bf16[128,8,128]{2,1,0:T(8,128)(2,1)S(1)} async-done(((bf16[128,8,128]{2,1,0:T(8,128)(2,1)}), bf16[128,8,128]{2,1,0:T(8,128)(2,1)S(1)}, u32[]{:S(2)}, u32[]{:S(2)}) %all-to-all-start) | async-done | bytes 262176 | tf_op jit(solution)/shard_map/all_to_all | solution.py:437
  62.7 0.7 %copy-done.6 = bf16[128,8,128]{2,1,0:T(8,128)(2,1)} copy-done((bf16[128,8,128]{2,1,0:T(8,128)(2,1)}, bf16[128,8,128]{2,1,0:T(8,128)(2,1)S(1)}, u32[]{:S(2)}) %copy-start.6) | copy-done | bytes 262168
  63.4 5.5 %shard_map.98 = (bf16[32,384]{1,0:T(8,128)(2,1)}, bf16[128,512]{1,0:T(8,128)(2,1)}, f32[8,384]{1,0:T(8,128)}, bf16[6144,512]{1,0:T(8,128)(2,1)}) custom-call(bf16[1024,128]{1,0:T(8,128)(2,1)} %bitcast.49, bf16[8,128,256]{2,1,0:T(8,128)(2,1)} %get-tuple-element.53.refs_1_, f32[8,256]{1,0:T(8,128)} %get-tuple-element.54.refs_2_, ...), custom_call_target="tpu_custom_call" | custom-call | flops 1207959552 | bytes 6291456 | tf_op jit(solution)/shard_map/pallas_call | solution.py:358
  (14 shorter events, 0.1 us)
Async XLA Ops:
  2.9 9.8 %copy-start.7 = (bf16[144,384]{1,0:T(8,128)(2,1)S(1)}, bf16[144,384]{1,0:T(8,128)(2,1)}, u32[]{:S(2)}) copy-start(bf16[144,384]{1,0:T(8,128)(2,1)} %get-tuple-element.38) | copy-start | bytes 331780
  2.9 8.7 %collective-permute-start.2 = (bf16[144,384]{1,0:T(8,128)(2,1)}, bf16[144,384]{1,0:T(8,128)(2,1)S(1)}, u32[]{:S(2)}, u32[]{:S(2)}) collective-permute-start(bf16[144,384]{1,0:T(8,128)(2,1)} %get-tuple-element.38), channel_id=1, source_target_pairs={{0,2},{1,3},{2,0},{3,1},{4,6},{5,7},{6,4},{7,5},{8,10},{9,11},{10,... | collective-permute-start | bytes 331784 | tf_op jit(solution)/shard_map/ppermute | solution.py:40
  7.4 5.3 %collective-permute-start.1 = (bf16[144,384]{1,0:T(8,128)(2,1)}, bf16[144,384]{1,0:T(8,128)(2,1)S(1)}, u32[]{:S(2)}, u32[]{:S(2)}) collective-permute-start(bf16[144,384]{1,0:T(8,128)(2,1)} %get-tuple-element.38), channel_id=1, source_target_pairs={{0,3},{1,2},{2,1},{3,0},{4,7},{5,6},{6,5},{7,4},{8,11},{9,10},{10,... | collective-permute-start | bytes 331784 | tf_op jit(solution)/shard_map/ppermute | solution.py:40
  7.8 4.9 %collective-permute-start = (bf16[144,384]{1,0:T(8,128)(2,1)}, bf16[144,384]{1,0:T(8,128)(2,1)S(1)}, u32[]{:S(2)}, u32[]{:S(2)}) collective-permute-start(bf16[144,384]{1,0:T(8,128)(2,1)} %get-tuple-element.38), channel_id=1, source_target_pairs={{0,1},{1,0},{2,3},{3,2},{4,5},{5,4},{6,7},{7,6},{8,9},{9,8},{10,11... | collective-permute-start | bytes 331784 | tf_op jit(solution)/shard_map/ppermute | solution.py:40
  8.1 11.7 %copy-start.8 = (bf16[16,384]{1,0:T(8,128)(2,1)S(1)}, bf16[16,384]{1,0:T(8,128)(2,1)}, u32[]{:S(2)}) copy-start(bf16[16,384]{1,0:T(8,128)(2,1)} %get-tuple-element.48) | copy-start | bytes 36868
  12.8 26.6 %copy-start = (bf16[4,144,384]{2,1,0:T(8,128)(2,1)}, bf16[4,144,384]{2,1,0:T(8,128)(2,1)S(1)}, u32[]{:S(2)}) copy-start(bf16[4,144,384]{2,1,0:T(8,128)(2,1)S(1)} %pad_maximum_fusion) | copy-start | bytes 1327108
  12.8 7.0 %collective-permute-start.5 = (bf16[4,8,384]{2,1,0:T(8,128)(2,1)S(1)}, bf16[4,8,384]{2,1,0:T(8,128)(2,1)S(1)}, u32[]{:S(2)}, u32[]{:S(2)}) collective-permute-start(bf16[4,8,384]{2,1,0:T(8,128)(2,1)S(1)} %slice.8), channel_id=1, source_target_pairs={{0,8},{1,9},{2,10},{3,11},{4,12},{5,13},{6,14},{7,15},{8,0},{9,1},... | collective-permute-start | bytes 73736 | tf_op jit(solution)/shard_map/ppermute | solution.py:40
  15.5 4.3 %collective-permute-start.4 = (bf16[4,8,384]{2,1,0:T(8,128)(2,1)S(1)}, bf16[4,8,384]{2,1,0:T(8,128)(2,1)S(1)}, u32[]{:S(2)}, u32[]{:S(2)}) collective-permute-start(bf16[4,8,384]{2,1,0:T(8,128)(2,1)S(1)} %slice.8), channel_id=1, source_target_pairs={{0,12},{1,13},{2,14},{3,15},{4,8},{5,9},{6,10},{7,11},{8,4},{9,5},... | collective-permute-start | bytes 73736 | tf_op jit(solution)/shard_map/ppermute | solution.py:40
  16.3 3.5 %collective-permute-start.3 = (bf16[4,8,384]{2,1,0:T(8,128)(2,1)S(1)}, bf16[4,8,384]{2,1,0:T(8,128)(2,1)S(1)}, u32[]{:S(2)}, u32[]{:S(2)}) collective-permute-start(bf16[4,8,384]{2,1,0:T(8,128)(2,1)S(1)} %slice.8), channel_id=1, source_target_pairs={{0,4},{1,5},{2,6},{3,7},{4,0},{5,1},{6,2},{7,3},{8,12},{9,13},{10,... | collective-permute-start | bytes 73736 | tf_op jit(solution)/shard_map/ppermute | solution.py:40
  19.9 7.6 %collective-permute-start.6 = (bf16[17,8,384]{2,1,0:T(8,128)(2,1)S(1)}, bf16[17,8,384]{2,1,0:T(8,128)(2,1)S(1)}, u32[]{:S(2)}, u32[]{:S(2)}) collective-permute-start(bf16[17,8,384]{2,1,0:T(8,128)(2,1)S(1)} %get-tuple-element.72), channel_id=1, source_target_pairs={{0,32},{16,48},{32,0},{48,16},{64,96},{80,112},{96,64},{112,80},{1... | collective-permute-start | bytes 313352 | tf_op jit(solution)/shard_map/ppermute | solution.py:31
  21.2 16.1 %collective-permute-start.12 = (bf16[4,144,384]{2,1,0:T(8,128)(2,1)S(1)}, bf16[4,144,384]{2,1,0:T(8,128)(2,1)S(1)}, u32[]{:S(2)}, u32[]{:S(2)}) collective-permute-start(bf16[4,144,384]{2,1,0:T(8,128)(2,1)S(1)} %pad_maximum_fusion), channel_id=1, source_target_pairs={{0,8},{1,9},{2,10},{3,11},{4,12},{5,13},{6,14},{7,15},{8,0},{9,1},... | collective-permute-start | bytes 1327112 | tf_op jit(solution)/shard_map/ppermute | solution.py:40
  24.2 13.0 %collective-permute-start.11 = (bf16[4,144,384]{2,1,0:T(8,128)(2,1)S(1)}, bf16[4,144,384]{2,1,0:T(8,128)(2,1)S(1)}, u32[]{:S(2)}, u32[]{:S(2)}) collective-permute-start(bf16[4,144,384]{2,1,0:T(8,128)(2,1)S(1)} %pad_maximum_fusion), channel_id=1, source_target_pairs={{0,12},{1,13},{2,14},{3,15},{4,8},{5,9},{6,10},{7,11},{8,4},{9,5},... | collective-permute-start | bytes 1327112 | tf_op jit(solution)/shard_map/ppermute | solution.py:40
  25.0 12.3 %collective-permute-start.10 = (bf16[4,144,384]{2,1,0:T(8,128)(2,1)S(1)}, bf16[4,144,384]{2,1,0:T(8,128)(2,1)S(1)}, u32[]{:S(2)}, u32[]{:S(2)}) collective-permute-start(bf16[4,144,384]{2,1,0:T(8,128)(2,1)S(1)} %pad_maximum_fusion), channel_id=1, source_target_pairs={{0,4},{1,5},{2,6},{3,7},{4,0},{5,1},{6,2},{7,3},{8,12},{9,13},{10,... | collective-permute-start | bytes 1327112 | tf_op jit(solution)/shard_map/ppermute | solution.py:40
  25.0 7.5 %collective-permute-start.8 = (bf16[17,8,384]{2,1,0:T(8,128)(2,1)S(1)}, bf16[17,8,384]{2,1,0:T(8,128)(2,1)S(1)}, u32[]{:S(2)}, u32[]{:S(2)}) collective-permute-start(bf16[17,8,384]{2,1,0:T(8,128)(2,1)S(1)} %get-tuple-element.72), channel_id=1, source_target_pairs={{0,64},{16,80},{32,96},{48,112},{64,0},{80,16},{96,32},{112,48},{1... | collective-permute-start | bytes 313352 | tf_op jit(solution)/shard_map/ppermute | solution.py:31
  27.5 5.0 %collective-permute-start.7 = (bf16[17,8,384]{2,1,0:T(8,128)(2,1)S(1)}, bf16[17,8,384]{2,1,0:T(8,128)(2,1)S(1)}, u32[]{:S(2)}, u32[]{:S(2)}) collective-permute-start(bf16[17,8,384]{2,1,0:T(8,128)(2,1)S(1)} %get-tuple-element.72), channel_id=1, source_target_pairs={{0,96},{16,112},{32,64},{48,80},{64,32},{80,48},{96,0},{112,16},{1... | collective-permute-start | bytes 313352 | tf_op jit(solution)/shard_map/ppermute | solution.py:31
  32.6 6.8 %copy-start.1 = (bf16[68,8,384]{2,1,0:T(8,128)(2,1)}, bf16[68,8,384]{2,1,0:T(8,128)(2,1)S(1)}, u32[]{:S(2)}) copy-start(bf16[68,8,384]{2,1,0:T(8,128)(2,1)S(1)} %constant_dynamic-update-slice_fusion.5.refs_1_.refs_0_.refs_6_) | copy-start | bytes 1253380
  32.6 6.0 %collective-permute-start.9 = (bf16[68,8,384]{2,1,0:T(8,128)(2,1)S(1)}, bf16[68,8,384]{2,1,0:T(8,128)(2,1)S(1)}, u32[]{:S(2)}, u32[]{:S(2)}) collective-permute-start(bf16[68,8,384]{2,1,0:T(8,128)(2,1)S(1)} %constant_dynamic-update-slice_fusion.5.refs_1_.refs_0_.refs_6_), channel_id=1, source_target_pairs={{0,16},{16,0},{32,48},{48,32},{64,80},{80,64},{96,112},{112,96},{1... | collective-permute-start | bytes 1253384 | tf_op jit(solution)/shard_map/ppermute | solution.py:31
  37.2 2.1 %copy-start.2 = (bf16[4,144,384]{2,1,0:T(8,128)(2,1)}, bf16[4,144,384]{2,1,0:T(8,128)(2,1)S(1)}, u32[]{:S(2)}) copy-start(bf16[4,144,384]{2,1,0:T(8,128)(2,1)S(1)} %collective-permute-done.12) | copy-start | bytes 1327108
  37.3 2.1 %copy-start.3 = (bf16[4,144,384]{2,1,0:T(8,128)(2,1)}, bf16[4,144,384]{2,1,0:T(8,128)(2,1)S(1)}, u32[]{:S(2)}) copy-start(bf16[4,144,384]{2,1,0:T(8,128)(2,1)S(1)} %collective-permute-done.11) | copy-start | bytes 1327108
  37.3 1.4 %copy-start.4 = (bf16[4,144,384]{2,1,0:T(8,128)(2,1)}, bf16[4,144,384]{2,1,0:T(8,128)(2,1)S(1)}, u32[]{:S(2)}) copy-start(bf16[4,144,384]{2,1,0:T(8,128)(2,1)S(1)} %collective-permute-done.10) | copy-start | bytes 1327108
  38.6 0.8 %copy-start.5 = (bf16[68,8,384]{2,1,0:T(8,128)(2,1)}, bf16[68,8,384]{2,1,0:T(8,128)(2,1)S(1)}, u32[]{:S(2)}) copy-start(bf16[68,8,384]{2,1,0:T(8,128)(2,1)S(1)} %collective-permute-done.9.refs_2_.refs_1_.refs_7_) | copy-start | bytes 1253380
  43.2 19.4 %all-to-all-start = ((bf16[128,8,128]{2,1,0:T(8,128)(2,1)}), bf16[128,8,128]{2,1,0:T(8,128)(2,1)S(1)}, u32[]{:S(2)}, u32[]{:S(2)}) async-start(bf16[128,8,128]{2,1,0:T(8,128)(2,1)} %bitcast.50), calls=%async_computation | async-start | bytes 524288 | tf_op jit(solution)/shard_map/all_to_all | solution.py:437
  62.7 0.7 %copy-start.6 = (bf16[128,8,128]{2,1,0:T(8,128)(2,1)}, bf16[128,8,128]{2,1,0:T(8,128)(2,1)S(1)}, u32[]{:S(2)}) copy-start(bf16[128,8,128]{2,1,0:T(8,128)(2,1)S(1)} %all-to-all-done) | copy-start | bytes 786436

commit v6 on v5

--- a/solution.py
+++ b/solution.py
@@ -253,10 +253,7 @@
     me, at, odd = place()
     parts_of = []
     for s in range(layers):
-        n = s * ways * 8
-        table = jnp.sum(
-            got.ref[n:n + ways * 8].astype(F32).reshape(ways, 8, slots), axis=0
-        )
+        table = got.ref[s]
         parts = nn(jnp.concatenate(split(table), axis=0), picks.ref[s])
         parts_of.append(parts[:8] + parts[8:16] + parts[16:])
     deltas = [None] * layers
@@ -436,6 +433,9 @@
     table = table.reshape(sections * ways, sections, slots)
     got_table = lax.all_to_all(table, ("section", "dp"), 0, 0, tiled=True)
 
+    table_sum = jnp.sum(
+        got_table.reshape(sections, ways, sections, slots).astype(F32), axis=1
+    )
     picks, scaled, codes, product, mixed = call(
         lambda *refs: side_kernel(*refs, tok=tok, cap=cap),
         [near, far, hid, gate],
@@ -459,7 +459,7 @@
     input_grad, hidden_grad, router_grad, down_grad = call(
         tail_kernel,
         [
-            got_table.reshape(-1, slots), picks, codes, signs, pick, scaled, near, far,
+            table_sum, picks, codes, signs, pick, scaled, near, far,
             product, mixed, gate, x, grads_mine,
         ],
         blocks,

time: 69.1 us -> 69 us (level)
    unnamed x24 -> x22, local copies, waits for them, and re-layouts: 1.57 us -> 0.89 us
where the time goes in v6:
time: 69 us; the launch traced here: 68.8 us
  starting transfers between devices  29.1 us (42%)
  Pallas kernels  24.3 us (35%)
  waiting for transfers between devices  12.9 us (19%)
  local copies, waits for them, and re-layouts  0.92 us (1%)
  between operations  0.85 us (1%)
  other arithmetic  0.71 us (1%)
    pallas_call x6, Pallas kernels, call(): pl.pallas_call(body, out_shape=shapes, in_specs=[HBM] * (counts[0] + coun...  24.3 us
    ppermute x9, starting transfers between devices, turn(): return lax.ppermute(value, ('section', 'dp'), pairs)  12.6 us
    ppermute x4, starting transfers between devices, swap(): return lax.ppermute(value, axis, [(i, i ^ distance) for i in range(count)])  8.61 us
    all_to_all x1, starting transfers between devices, per_device(): got_table = lax.all_to_all(table, ('section', 'dp'), 0, 0, tiled=True)  7.95 us
    ppermute x4, waiting for transfers between devices, swap(): return lax.ppermute(value, axis, [(i, i ^ distance) for i in range(count)])  6.17 us
    all_to_all x1, waiting for transfers between devices, per_device(): got_table = lax.all_to_all(table, ('section', 'dp'), 0, 0, tiled=True)  5.58 us
  transfers between devices with their start and end apart: 14, of which 4 were waited for; matrix products, arithmetic and copies ran while one was open for 0% of the time, Pallas kernels for 19%

profile of v6, /device:TPU:1, one launch (start us, length us, event | category | flops | bytes accessed | tf_op | source)
XLA Modules:
  0.0 68.8 jit_solution(14524393331684731399)
XLA Ops:
  0.6 2.2 %shard_map.93 = (bf16[144,384]{1,0:T(8,128)(2,1)}, bf16[128,256]{1,0:T(8,128)(2,1)}, bf16[16,384]{1,0:T(8,128)(2,1)}, bf16[32,384]{1,0:T(8,128)(2,1)}) custom-call(s32[8,64]{1,0:T(8,128)} %bitcast.60, bf16[256,384]{1,0:T(8,128)(2,1)} %bitcast.52, bf16[256,384]{1,0:T(8,128)(2,1)} %bitcast.53, bf16[8,384]{1,0:T(8,128)(2,1)} %bitcast.59), custom_call_target="tpu_custom_call" | custom-call | tf_op jit(solution)/shard_map/pallas_call | solution.py:355
  2.9 0.0 copy-start.6
  2.9 4.5 %collective-permute-start.2 = (bf16[144,384]{1,0:T(8,128)(2,1)}, bf16[144,384]{1,0:T(8,128)(2,1)S(1)}, u32[]{:S(2)}, u32[]{:S(2)}) collective-permute-start(bf16[144,384]{1,0:T(8,128)(2,1)} %get-tuple-element.38), channel_id=1, source_target_pairs={{0,2},{1,3},{2,0},{3,1},{4,6},{5,7},{6,4},{7,5},{8,10},{9,11},{10,... | collective-permute-start | bytes 331784 | tf_op jit(solution)/shard_map/ppermute | solution.py:40
  7.4 0.4 collective-permute-start.1
  7.8 0.3 collective-permute-start
  8.1 3.5 %shard_map.94.refs_3_ = bf16[3072,128]{1,0:T(8,128)(2,1)} custom-call(bf16[128,512]{1,0:T(8,128)(2,1)} %bitcast.48, bf16[6144,512]{1,0:T(8,128)(2,1)} %bitcast.33), custom_call_target="tpu_custom_call" | custom-call | bytes 3145728 | tf_op jit(solution)/shard_map/pallas_call | solution.py:355
  11.6 0.0 collective-permute-done.2
  11.6 1.1 %collective-permute-done.1 = bf16[144,384]{1,0:T(8,128)(2,1)S(1)} collective-permute-done((bf16[144,384]{1,0:T(8,128)(2,1)}, bf16[144,384]{1,0:T(8,128)(2,1)S(1)}, u32[]{:S(2)}, u32[]{:S(2)}) %collective-permute-start.1) | collective-permute-done | bytes 110624 | tf_op jit(solution)/shard_map/ppermute | solution.py:40
  12.7 0.0 collective-permute-done
  12.7 0.0 copy-done.6
  12.7 0.1 pad_maximum_fusion
  12.8 0.0 copy-start
  12.8 2.7 %collective-permute-start.5 = (bf16[4,8,384]{2,1,0:T(8,128)(2,1)S(1)}, bf16[4,8,384]{2,1,0:T(8,128)(2,1)S(1)}, u32[]{:S(2)}, u32[]{:S(2)}) collective-permute-start(bf16[4,8,384]{2,1,0:T(8,128)(2,1)S(1)} %slice.8), channel_id=1, source_target_pairs={{0,8},{1,9},{2,10},{3,11},{4,12},{5,13},{6,14},{7,15},{8,0},{9,1},... | collective-permute-start | bytes 73736 | tf_op jit(solution)/shard_map/ppermute | solution.py:40
  15.5 0.8 %collective-permute-start.4 = (bf16[4,8,384]{2,1,0:T(8,128)(2,1)S(1)}, bf16[4,8,384]{2,1,0:T(8,128)(2,1)S(1)}, u32[]{:S(2)}, u32[]{:S(2)}) collective-permute-start(bf16[4,8,384]{2,1,0:T(8,128)(2,1)S(1)} %slice.8), channel_id=1, source_target_pairs={{0,12},{1,13},{2,14},{3,15},{4,8},{5,9},{6,10},{7,11},{8,4},{9,5},... | collective-permute-start | bytes 73736 | tf_op jit(solution)/shard_map/ppermute | solution.py:40
  16.3 0.0 collective-permute-start.3
  16.3 3.5 %shard_map.95.refs_4_ = bf16[3072,128]{1,0:T(8,128)(2,1)} custom-call(bf16[128,512]{1,0:T(8,128)(2,1)} %bitcast.49, bf16[6144,512]{1,0:T(8,128)(2,1)} %bitcast.34), custom_call_target="tpu_custom_call" | custom-call | bytes 3145728 | tf_op jit(solution)/shard_map/pallas_call | solution.py:355
  19.7 0.0 collective-permute-done.5
  19.8 0.0 collective-permute-done.4
  19.8 0.0 collective-permute-done.3
  19.8 0.0 copy-done.7
  19.9 1.3 %collective-permute-start.6 = (bf16[17,8,384]{2,1,0:T(8,128)(2,1)S(1)}, bf16[17,8,384]{2,1,0:T(8,128)(2,1)S(1)}, u32[]{:S(2)}, u32[]{:S(2)}) collective-permute-start(bf16[17,8,384]{2,1,0:T(8,128)(2,1)S(1)} %get-tuple-element.72), channel_id=1, source_target_pairs={{0,32},{16,48},{32,0},{48,16},{64,96},{80,112},{96,64},{112,80},{1... | collective-permute-start | bytes 313352 | tf_op jit(solution)/shard_map/ppermute | solution.py:31
  21.2 3.1 %collective-permute-start.12 = (bf16[4,144,384]{2,1,0:T(8,128)(2,1)S(1)}, bf16[4,144,384]{2,1,0:T(8,128)(2,1)S(1)}, u32[]{:S(2)}, u32[]{:S(2)}) collective-permute-start(bf16[4,144,384]{2,1,0:T(8,128)(2,1)S(1)} %pad_maximum_fusion), channel_id=1, source_target_pairs={{0,8},{1,9},{2,10},{3,11},{4,12},{5,13},{6,14},{7,15},{8,0},{9,1},... | collective-permute-start | bytes 1327112 | tf_op jit(solution)/shard_map/ppermute | solution.py:40
  24.2 0.8 %collective-permute-start.11 = (bf16[4,144,384]{2,1,0:T(8,128)(2,1)S(1)}, bf16[4,144,384]{2,1,0:T(8,128)(2,1)S(1)}, u32[]{:S(2)}, u32[]{:S(2)}) collective-permute-start(bf16[4,144,384]{2,1,0:T(8,128)(2,1)S(1)} %pad_maximum_fusion), channel_id=1, source_target_pairs={{0,12},{1,13},{2,14},{3,15},{4,8},{5,9},{6,10},{7,11},{8,4},{9,5},... | collective-permute-start | bytes 1327112 | tf_op jit(solution)/shard_map/ppermute | solution.py:40
  25.0 0.0 collective-permute-start.10
  25.0 2.5 %collective-permute-start.8 = (bf16[17,8,384]{2,1,0:T(8,128)(2,1)S(1)}, bf16[17,8,384]{2,1,0:T(8,128)(2,1)S(1)}, u32[]{:S(2)}, u32[]{:S(2)}) collective-permute-start(bf16[17,8,384]{2,1,0:T(8,128)(2,1)S(1)} %get-tuple-element.72), channel_id=1, source_target_pairs={{0,64},{16,80},{32,96},{48,112},{64,0},{80,16},{96,32},{112,48},{1... | collective-permute-start | bytes 313352 | tf_op jit(solution)/shard_map/ppermute | solution.py:31
  27.5 0.0 collective-permute-done.6
  27.5 0.2 collective-permute-start.7
  27.7 4.8 %collective-permute-done.7 = bf16[17,8,384]{2,1,0:T(8,128)(2,1)S(1)} collective-permute-done((bf16[17,8,384]{2,1,0:T(8,128)(2,1)S(1)}, bf16[17,8,384]{2,1,0:T(8,128)(2,1)S(1)}, u32[]{:S(2)}, u32[]{:S(2)}) %collective-permute-start.7) | collective-permute-done | bytes 104480 | tf_op jit(solution)/shard_map/ppermute | solution.py:31
  32.5 0.0 collective-permute-done.8
  32.6 0.0 copy-start.1
  32.6 4.6 %collective-permute-start.9 = (bf16[68,8,384]{2,1,0:T(8,128)(2,1)S(1)}, bf16[68,8,384]{2,1,0:T(8,128)(2,1)S(1)}, u32[]{:S(2)}, u32[]{:S(2)}) collective-permute-start(bf16[68,8,384]{2,1,0:T(8,128)(2,1)S(1)} %constant_dynamic-update-slice_fusion.5.refs_1_.refs_0_.refs_6_), channel_id=1, source_target_pairs={{0,16},{16,0},{32,48},{48,32},{64,80},{80,64},{96,112},{112,96},{1... | collective-permute-start | bytes 1253384 | tf_op jit(solution)/shard_map/ppermute | solution.py:31
  37.2 0.0 collective-permute-done.12
  37.2 0.0 collective-permute-done.11
  37.2 0.0 copy-start.3
  37.3 0.0 collective-permute-done.10
  37.3 0.0 copy-start.4
  37.3 1.3 %collective-permute-done.9.refs_2_.refs_1_.refs_7_ = bf16[68,8,384]{2,1,0:T(8,128)(2,1)S(1)} collective-permute-done((bf16[68,8,384]{2,1,0:T(8,128)(2,1)S(1)}, bf16[68,8,384]{2,1,0:T(8,128)(2,1)S(1)}, u32[]{:S(2)}, u32[]{:S(2)}) %collective-permute-start.9) | collective-permute-done | bytes 417824 | tf_op jit(solution)/shard_map/ppermute | solution.py:31
  38.6 0.0 copy-done.4
  38.6 0.8 %copy-done.5 = bf16[68,8,384]{2,1,0:T(8,128)(2,1)} copy-done((bf16[68,8,384]{2,1,0:T(8,128)(2,1)}, bf16[68,8,384]{2,1,0:T(8,128)(2,1)S(1)}, u32[]{:S(2)}) %copy-start.5) | copy-done | bytes 417816
  39.4 0.0 copy-done
  39.4 0.0 copy-done.1
  39.4 0.0 copy-done.2
  39.4 3.8 %shard_map.96 = (bf16[64,16,128]{2,1,0:T(8,128)(2,1)}, f32[8,8,128]{2,1,0:T(8,128)}, f32[8,128]{1,0:T(8,128)}) custom-call(bf16[128,256]{1,0:T(8,128)(2,1)} %get-tuple-element.34.refs_0_.refs_4_, bf16[68,8,384]{2,1,0:T(8,128)(2,1)} %copy-done.1, bf16[68,8,384]{2,1,0:T(8,128)(2,1)} %copy-done.5, bf16[3072,128]{1,0:T(8,128)(2,1)} %shard_map.94.refs_3_, ...), custom_call_target="tpu_custom_call" | custom-call | tf_op jit(solution)/shard_map/pallas_call | solution.py:355
  43.3 8.0 %all-to-all-start = ((bf16[128,8,128]{2,1,0:T(8,128)(2,1)}), bf16[128,8,128]{2,1,0:T(8,128)(2,1)S(1)}, u32[]{:S(2)}, u32[]{:S(2)}) async-start(bf16[128,8,128]{2,1,0:T(8,128)(2,1)} %bitcast.51), calls=%async_computation | async-start | bytes 524288 | tf_op jit(solution)/shard_map/all_to_all | solution.py:434
  51.2 5.9 %shard_map.97 = (bf16[8,128,256]{2,1,0:T(8,128)(2,1)}, bf16[128,512]{1,0:T(8,128)(2,1)}, f32[8,256]{1,0:T(8,128)}, f32[128,512]{1,0:T(8,128)}, bf16[64,512]{1,0:T(8,128)(2,1)}) custom-call(bf16[68,8,384]{2,1,0:T(8,128)(2,1)} %copy-done.1, bf16[68,8,384]{2,1,0:T(8,128)(2,1)} %copy-done.5, bf16[128,512]{1,0:T(8,128)(2,1)} %bitcast.50, ...), custom_call_target="tpu_custom_call" | custom-call | flops 1000000000 | bytes 10000000 | tf_op jit(solution)/shard_map/pallas_call | solution.py:355
  57.1 5.6 %all-to-all-done = bf16[128,8,128]{2,1,0:T(8,128)(2,1)S(1)} async-done(((bf16[128,8,128]{2,1,0:T(8,128)(2,1)}), bf16[128,8,128]{2,1,0:T(8,128)(2,1)S(1)}, u32[]{:S(2)}, u32[]{:S(2)}) %all-to-all-start) | async-done | bytes 262176 | tf_op jit(solution)/shard_map/all_to_all | solution.py:434
  62.7 0.6 convert_reduce_fusion.refs_0_
  63.3 5.4 %shard_map.98 = (bf16[32,384]{1,0:T(8,128)(2,1)}, bf16[128,512]{1,0:T(8,128)(2,1)}, f32[8,384]{1,0:T(8,128)}, bf16[6144,512]{1,0:T(8,128)(2,1)}) custom-call(f32[8,8,128]{2,1,0:T(8,128)} %convert_reduce_fusion.refs_0_, bf16[8,128,256]{2,1,0:T(8,128)(2,1)} %get-tuple-element.53.refs_1_, f32[8,256]{1,0:T(8,128)} %get-tuple-element.54.refs_2_, ...), custom_call_target="tpu_custom_call" | custom-call | flops 1207959552 | bytes 6291456 | tf_op jit(solution)/shard_map/pallas_call | solution.py:355
  (13 shorter events, 0.1 us)
Async XLA Ops:
  2.9 9.8 %copy-start.6 = (bf16[144,384]{1,0:T(8,128)(2,1)S(1)}, bf16[144,384]{1,0:T(8,128)(2,1)}, u32[]{:S(2)}) copy-start(bf16[144,384]{1,0:T(8,128)(2,1)} %get-tuple-element.38) | copy-start | bytes 331780
  2.9 8.7 %collective-permute-start.2 = (bf16[144,384]{1,0:T(8,128)(2,1)}, bf16[144,384]{1,0:T(8,128)(2,1)S(1)}, u32[]{:S(2)}, u32[]{:S(2)}) collective-permute-start(bf16[144,384]{1,0:T(8,128)(2,1)} %get-tuple-element.38), channel_id=1, source_target_pairs={{0,2},{1,3},{2,0},{3,1},{4,6},{5,7},{6,4},{7,5},{8,10},{9,11},{10,... | collective-permute-start | bytes 331784 | tf_op jit(solution)/shard_map/ppermute | solution.py:40
  7.4 5.3 %collective-permute-start.1 = (bf16[144,384]{1,0:T(8,128)(2,1)}, bf16[144,384]{1,0:T(8,128)(2,1)S(1)}, u32[]{:S(2)}, u32[]{:S(2)}) collective-permute-start(bf16[144,384]{1,0:T(8,128)(2,1)} %get-tuple-element.38), channel_id=1, source_target_pairs={{0,3},{1,2},{2,1},{3,0},{4,7},{5,6},{6,5},{7,4},{8,11},{9,10},{10,... | collective-permute-start | bytes 331784 | tf_op jit(solution)/shard_map/ppermute | solution.py:40
  7.8 4.9 %collective-permute-start = (bf16[144,384]{1,0:T(8,128)(2,1)}, bf16[144,384]{1,0:T(8,128)(2,1)S(1)}, u32[]{:S(2)}, u32[]{:S(2)}) collective-permute-start(bf16[144,384]{1,0:T(8,128)(2,1)} %get-tuple-element.38), channel_id=1, source_target_pairs={{0,1},{1,0},{2,3},{3,2},{4,5},{5,4},{6,7},{7,6},{8,9},{9,8},{10,11... | collective-permute-start | bytes 331784 | tf_op jit(solution)/shard_map/ppermute | solution.py:40
  8.1 11.7 %copy-start.7 = (bf16[16,384]{1,0:T(8,128)(2,1)S(1)}, bf16[16,384]{1,0:T(8,128)(2,1)}, u32[]{:S(2)}) copy-start(bf16[16,384]{1,0:T(8,128)(2,1)} %get-tuple-element.48) | copy-start | bytes 36868
  12.8 26.6 %copy-start = (bf16[4,144,384]{2,1,0:T(8,128)(2,1)}, bf16[4,144,384]{2,1,0:T(8,128)(2,1)S(1)}, u32[]{:S(2)}) copy-start(bf16[4,144,384]{2,1,0:T(8,128)(2,1)S(1)} %pad_maximum_fusion) | copy-start | bytes 1327108
  12.8 7.0 %collective-permute-start.5 = (bf16[4,8,384]{2,1,0:T(8,128)(2,1)S(1)}, bf16[4,8,384]{2,1,0:T(8,128)(2,1)S(1)}, u32[]{:S(2)}, u32[]{:S(2)}) collective-permute-start(bf16[4,8,384]{2,1,0:T(8,128)(2,1)S(1)} %slice.8), channel_id=1, source_target_pairs={{0,8},{1,9},{2,10},{3,11},{4,12},{5,13},{6,14},{7,15},{8,0},{9,1},... | collective-permute-start | bytes 73736 | tf_op jit(solution)/shard_map/ppermute | solution.py:40
  15.5 4.3 %collective-permute-start.4 = (bf16[4,8,384]{2,1,0:T(8,128)(2,1)S(1)}, bf16[4,8,384]{2,1,0:T(8,128)(2,1)S(1)}, u32[]{:S(2)}, u32[]{:S(2)}) collective-permute-start(bf16[4,8,384]{2,1,0:T(8,128)(2,1)S(1)} %slice.8), channel_id=1, source_target_pairs={{0,12},{1,13},{2,14},{3,15},{4,8},{5,9},{6,10},{7,11},{8,4},{9,5},... | collective-permute-start | bytes 73736 | tf_op jit(solution)/shard_map/ppermute | solution.py:40
  16.3 3.5 %collective-permute-start.3 = (bf16[4,8,384]{2,1,0:T(8,128)(2,1)S(1)}, bf16[4,8,384]{2,1,0:T(8,128)(2,1)S(1)}, u32[]{:S(2)}, u32[]{:S(2)}) collective-permute-start(bf16[4,8,384]{2,1,0:T(8,128)(2,1)S(1)} %slice.8), channel_id=1, source_target_pairs={{0,4},{1,5},{2,6},{3,7},{4,0},{5,1},{6,2},{7,3},{8,12},{9,13},{10,... | collective-permute-start | bytes 73736 | tf_op jit(solution)/shard_map/ppermute | solution.py:40
  19.9 7.6 %collective-permute-start.6 = (bf16[17,8,384]{2,1,0:T(8,128)(2,1)S(1)}, bf16[17,8,384]{2,1,0:T(8,128)(2,1)S(1)}, u32[]{:S(2)}, u32[]{:S(2)}) collective-permute-start(bf16[17,8,384]{2,1,0:T(8,128)(2,1)S(1)} %get-tuple-element.72), channel_id=1, source_target_pairs={{0,32},{16,48},{32,0},{48,16},{64,96},{80,112},{96,64},{112,80},{1... | collective-permute-start | bytes 313352 | tf_op jit(solution)/shard_map/ppermute | solution.py:31
  21.2 16.1 %collective-permute-start.12 = (bf16[4,144,384]{2,1,0:T(8,128)(2,1)S(1)}, bf16[4,144,384]{2,1,0:T(8,128)(2,1)S(1)}, u32[]{:S(2)}, u32[]{:S(2)}) collective-permute-start(bf16[4,144,384]{2,1,0:T(8,128)(2,1)S(1)} %pad_maximum_fusion), channel_id=1, source_target_pairs={{0,8},{1,9},{2,10},{3,11},{4,12},{5,13},{6,14},{7,15},{8,0},{9,1},... | collective-permute-start | bytes 1327112 | tf_op jit(solution)/shard_map/ppermute | solution.py:40
  24.2 13.0 %collective-permute-start.11 = (bf16[4,144,384]{2,1,0:T(8,128)(2,1)S(1)}, bf16[4,144,384]{2,1,0:T(8,128)(2,1)S(1)}, u32[]{:S(2)}, u32[]{:S(2)}) collective-permute-start(bf16[4,144,384]{2,1,0:T(8,128)(2,1)S(1)} %pad_maximum_fusion), channel_id=1, source_target_pairs={{0,12},{1,13},{2,14},{3,15},{4,8},{5,9},{6,10},{7,11},{8,4},{9,5},... | collective-permute-start | bytes 1327112 | tf_op jit(solution)/shard_map/ppermute | solution.py:40
  25.0 12.3 %collective-permute-start.10 = (bf16[4,144,384]{2,1,0:T(8,128)(2,1)S(1)}, bf16[4,144,384]{2,1,0:T(8,128)(2,1)S(1)}, u32[]{:S(2)}, u32[]{:S(2)}) collective-permute-start(bf16[4,144,384]{2,1,0:T(8,128)(2,1)S(1)} %pad_maximum_fusion), channel_id=1, source_target_pairs={{0,4},{1,5},{2,6},{3,7},{4,0},{5,1},{6,2},{7,3},{8,12},{9,13},{10,... | collective-permute-start | bytes 1327112 | tf_op jit(solution)/shard_map/ppermute | solution.py:40
  25.0 7.5 %collective-permute-start.8 = (bf16[17,8,384]{2,1,0:T(8,128)(2,1)S(1)}, bf16[17,8,384]{2,1,0:T(8,128)(2,1)S(1)}, u32[]{:S(2)}, u32[]{:S(2)}) collective-permute-start(bf16[17,8,384]{2,1,0:T(8,128)(2,1)S(1)} %get-tuple-element.72), channel_id=1, source_target_pairs={{0,64},{16,80},{32,96},{48,112},{64,0},{80,16},{96,32},{112,48},{1... | collective-permute-start | bytes 313352 | tf_op jit(solution)/shard_map/ppermute | solution.py:31
  27.5 5.0 %collective-permute-start.7 = (bf16[17,8,384]{2,1,0:T(8,128)(2,1)S(1)}, bf16[17,8,384]{2,1,0:T(8,128)(2,1)S(1)}, u32[]{:S(2)}, u32[]{:S(2)}) collective-permute-start(bf16[17,8,384]{2,1,0:T(8,128)(2,1)S(1)} %get-tuple-element.72), channel_id=1, source_target_pairs={{0,96},{16,112},{32,64},{48,80},{64,32},{80,48},{96,0},{112,16},{1... | collective-permute-start | bytes 313352 | tf_op jit(solution)/shard_map/ppermute | solution.py:31
  32.6 6.8 %copy-start.1 = (bf16[68,8,384]{2,1,0:T(8,128)(2,1)}, bf16[68,8,384]{2,1,0:T(8,128)(2,1)S(1)}, u32[]{:S(2)}) copy-start(bf16[68,8,384]{2,1,0:T(8,128)(2,1)S(1)} %constant_dynamic-update-slice_fusion.5.refs_1_.refs_0_.refs_6_) | copy-start | bytes 1253380
  32.6 6.0 %collective-permute-start.9 = (bf16[68,8,384]{2,1,0:T(8,128)(2,1)S(1)}, bf16[68,8,384]{2,1,0:T(8,128)(2,1)S(1)}, u32[]{:S(2)}, u32[]{:S(2)}) collective-permute-start(bf16[68,8,384]{2,1,0:T(8,128)(2,1)S(1)} %constant_dynamic-update-slice_fusion.5.refs_1_.refs_0_.refs_6_), channel_id=1, source_target_pairs={{0,16},{16,0},{32,48},{48,32},{64,80},{80,64},{96,112},{112,96},{1... | collective-permute-start | bytes 1253384 | tf_op jit(solution)/shard_map/ppermute | solution.py:31
  37.2 2.2 %copy-start.2 = (bf16[4,144,384]{2,1,0:T(8,128)(2,1)}, bf16[4,144,384]{2,1,0:T(8,128)(2,1)S(1)}, u32[]{:S(2)}) copy-start(bf16[4,144,384]{2,1,0:T(8,128)(2,1)S(1)} %collective-permute-done.12) | copy-start | bytes 1327108
  37.2 2.2 %copy-start.3 = (bf16[4,144,384]{2,1,0:T(8,128)(2,1)}, bf16[4,144,384]{2,1,0:T(8,128)(2,1)S(1)}, u32[]{:S(2)}) copy-start(bf16[4,144,384]{2,1,0:T(8,128)(2,1)S(1)} %collective-permute-done.11) | copy-start | bytes 1327108
  37.3 1.4 %copy-start.4 = (bf16[4,144,384]{2,1,0:T(8,128)(2,1)}, bf16[4,144,384]{2,1,0:T(8,128)(2,1)S(1)}, u32[]{:S(2)}) copy-start(bf16[4,144,384]{2,1,0:T(8,128)(2,1)S(1)} %collective-permute-done.10) | copy-start | bytes 1327108
  38.6 0.8 %copy-start.5 = (bf16[68,8,384]{2,1,0:T(8,128)(2,1)}, bf16[68,8,384]{2,1,0:T(8,128)(2,1)S(1)}, u32[]{:S(2)}) copy-start(bf16[68,8,384]{2,1,0:T(8,128)(2,1)S(1)} %collective-permute-done.9.refs_2_.refs_1_.refs_7_) | copy-start | bytes 1253380
  43.3 19.4 %all-to-all-start = ((bf16[128,8,128]{2,1,0:T(8,128)(2,1)}), bf16[128,8,128]{2,1,0:T(8,128)(2,1)S(1)}, u32[]{:S(2)}, u32[]{:S(2)}) async-start(bf16[128,8,128]{2,1,0:T(8,128)(2,1)} %bitcast.51), calls=%async_computation | async-start | bytes 524288 | tf_op jit(solution)/shard_map/all_to_all | solution.py:434

commit v7 on v6

--- a/solution.py
+++ b/solution.py
@@ -93,7 +93,7 @@
 
 def pre_kernel(ins, raws, outs, raw_outs, *, cap):
     ids, grads, x, router = ins
-    block, pick_out, code_out, mine_out = outs
+    block, pick_out, code_out = outs
     slots, tokens = pick_out.ref.shape
     tok = ids.ref.shape[1]
     micro = tokens // tok
@@ -109,14 +109,6 @@
     pick_out.ref[...] = pick
     pick_out.flush()
     block.ref[:slots, :] = nn(pick, grads.ref[...]).astype(BF16)
-    me, _, _ = place()
-    count = mine_out.ref.shape[0]
-    own = count // micro
-    wanted = iota((count, 1), 0)
-    wanted = (wanted // own) * tok + me * own + wanted % own
-    choose = (iota((count, tokens), 1) == wanted).astype(F32).astype(BF16)
-    mine_out.ref[...] = nn(choose, grads.ref[...]).astype(BF16)
-    mine_out.flush()
     logits = nt(router.ref[...], x.ref[...])
     apart = -jnp.sum(expert_signs(code[0:1])[0] * logits, axis=0, keepdims=True)
     parts = jnp.concatenate(split(apart) + [jnp.zeros((5, tokens), BF16)], axis=0)
@@ -183,6 +175,7 @@
     layer = jnp.concatenate([jnp.full((1, 8, slots), d, jnp.int32) for d in LAYER_ORDER]) ^ me
     signs = jnp.where(layer > me, signs, 0.0)
     signs_out.ref[...] = signs
+    signs_out.flush()
     filled = nt(jnp.ones((8, pick.buffer.shape[1]), BF16), pick.ref[...])
     for load in loads:
         load.wait()
@@ -191,6 +184,7 @@
     apart = jnp.sum(logit_parts(rows, slots, ways), axis=0, keepdims=True)
     gate = filled / (1.0 + jnp.exp(apart))
     gate_out.ref[...] = gate
+    gate_out.flush()
     slope = gate * (1.0 - gate)
     total = jnp.zeros((slots + signs.shape[0] * 8, slots), F32)
     for way in range(0, ways, 2):
@@ -209,8 +203,8 @@
 
 
 def side_kernel(ins, raws, outs, raw_outs, rows, lsems, wbuf, sems, *, tok, cap):
-    near, far, hid, gate = ins
-    picks_out, scaled_out, codes_out, product_out, mixed_out = outs
+    near, far, hid, gate, grads = ins
+    picks_out, scaled_out, codes_out, mine_out, product_out, mixed_out = outs
     slots, width = hid.buffer.shape[0], near.buffer.shape[2]
     loads = load_rows(raws[:4], rows, lsems)
     copies = load_weights(raws[4], wbuf, sems, 0)
@@ -226,6 +220,13 @@
     gate_col = jnp.sum(diagonal(slots) * gate.ref[0:1], axis=1, keepdims=True)
     scaled_out.ref[...] = (gate_col * hid.ref[...].astype(F32)).astype(BF16)
     scaled_out.flush()
+    count, tokens = mine_out.ref.shape[0], grads.buffer.shape[0]
+    own = count * tok // tokens
+    wanted = iota((count, 1), 0)
+    wanted = (wanted // own) * tok + me * own + wanted % own
+    choose = (iota((count, tokens), 1) == wanted).astype(F32).astype(BF16)
+    mine_out.ref[...] = nn(choose, grads.ref[...]).astype(BF16)
+    mine_out.flush()
     for load in loads:
         load.wait()
     ways = wbuf.shape[0] // width
@@ -384,12 +385,11 @@
     grads = grad_out.reshape(tokens, width)
 
     own = tok // sections
-    block, pick, code, grads_mine = call(
+    block, pick, code = call(
         lambda *refs: pre_kernel(*refs, cap=cap),
         [expert_ids[0].transpose(0, 2, 1).reshape(2 * micro, tok), grads, x, router],
         [],
-        [((slots + 16, width), BF16), ((slots, tokens), BF16), ((16, width), BF16),
-         ((micro * own, width), BF16)],
+        [((slots + 16, width), BF16), ((slots, tokens), BF16), ((16, width), BF16)],
     )
 
     weights = down_weight[0]
@@ -436,14 +436,15 @@
     table_sum = jnp.sum(
         got_table.reshape(sections, ways, sections, slots).astype(F32), axis=1
     )
-    picks, scaled, codes, product, mixed = call(
+    picks, scaled, codes, grads_mine, product, mixed = call(
         lambda *refs: side_kernel(*refs, tok=tok, cap=cap),
-        [near, far, hid, gate],
+        [near, far, hid, gate, grads],
         blocks + [weights],
         [
             ((sections, slots, tokens), BF16),
             ((slots, units), BF16),
             ((sections, tokens), F32),
+            ((micro * own, width), BF16),
             ((slots, units), F32),
             ((sections * experts, units), BF16),
         ],

time: 69 us -> 68.9 us (level)
  no operation moved by 1% of the time
where the time goes in v7:
time: 68.9 us; the launch traced here: 68.7 us
  starting transfers between devices  29.1 us (42%)
  Pallas kernels  24.3 us (35%)
  waiting for transfers between devices  12.8 us (19%)
  local copies, waits for them, and re-layouts  0.92 us (1%)
  between operations  0.85 us (1%)
  other arithmetic  0.71 us (1%)
    pallas_call x6, Pallas kernels, call(): pl.pallas_call(body, out_shape=shapes, in_specs=[HBM] * (counts[0] + coun...  24.3 us
    ppermute x9, starting transfers between devices, turn(): return lax.ppermute(value, ('section', 'dp'), pairs)  12.6 us
    ppermute x4, starting transfers between devices, swap(): return lax.ppermute(value, axis, [(i, i ^ distance) for i in range(count)])  8.61 us
    all_to_all x1, starting transfers between devices, per_device(): got_table = lax.all_to_all(table, ('section', 'dp'), 0, 0, tiled=True)  7.96 us
    ppermute x4, waiting for transfers between devices, swap(): return lax.ppermute(value, axis, [(i, i ^ distance) for i in range(count)])  6.17 us
    all_to_all x1, waiting for transfers between devices, per_device(): got_table = lax.all_to_all(table, ('section', 'dp'), 0, 0, tiled=True)  5.5 us
  transfers between devices with their start and end apart: 14, of which 4 were waited for; matrix products, arithmetic and copies ran while one was open for 0% of the time, Pallas kernels for 19%

profile of v7, /device:TPU:1, one launch (start us, length us, event | category | flops | bytes accessed | tf_op | source)
XLA Modules:
  0.0 68.7 jit_solution(1943853373486701652)
XLA Ops:
  0.6 2.2 %shard_map.93 = (bf16[144,384]{1,0:T(8,128)(2,1)}, bf16[128,256]{1,0:T(8,128)(2,1)}, bf16[16,384]{1,0:T(8,128)(2,1)}) custom-call(s32[8,64]{1,0:T(8,128)} %bitcast.61, bf16[256,384]{1,0:T(8,128)(2,1)} %bitcast.51, bf16[256,384]{1,0:T(8,128)(2,1)} %bitcast.54, bf16[8,384]{1,0:T(8,128)(2,1)} %bitcast.60), custom_call_target="tpu_custom_call" | custom-call | tf_op jit(solution)/shard_map/pallas_call | solution.py:356
  2.8 0.0 copy-start.6
  2.8 4.5 %collective-permute-start.2 = (bf16[144,384]{1,0:T(8,128)(2,1)}, bf16[144,384]{1,0:T(8,128)(2,1)S(1)}, u32[]{:S(2)}, u32[]{:S(2)}) collective-permute-start(bf16[144,384]{1,0:T(8,128)(2,1)} %get-tuple-element.38), channel_id=1, source_target_pairs={{0,2},{1,3},{2,0},{3,1},{4,6},{5,7},{6,4},{7,5},{8,10},{9,11},{10,... | collective-permute-start | bytes 331784 | tf_op jit(solution)/shard_map/ppermute | solution.py:40
  7.3 0.4 collective-permute-start.1
  7.7 0.3 collective-permute-start
  8.1 3.5 %shard_map.94.refs_3_ = bf16[3072,128]{1,0:T(8,128)(2,1)} custom-call(bf16[128,512]{1,0:T(8,128)(2,1)} %bitcast.48, bf16[6144,512]{1,0:T(8,128)(2,1)} %bitcast.33), custom_call_target="tpu_custom_call" | custom-call | bytes 3145728 | tf_op jit(solution)/shard_map/pallas_call | solution.py:356
  11.5 0.0 collective-permute-done.2
  11.6 1.1 %collective-permute-done.1 = bf16[144,384]{1,0:T(8,128)(2,1)S(1)} collective-permute-done((bf16[144,384]{1,0:T(8,128)(2,1)}, bf16[144,384]{1,0:T(8,128)(2,1)S(1)}, u32[]{:S(2)}, u32[]{:S(2)}) %collective-permute-start.1) | collective-permute-done | bytes 110624 | tf_op jit(solution)/shard_map/ppermute | solution.py:40
  12.6 0.0 collective-permute-done
  12.6 0.0 copy-done.6
  12.6 0.1 pad_maximum_fusion
  12.7 0.0 copy-start
  12.7 2.7 %collective-permute-start.5 = (bf16[4,8,384]{2,1,0:T(8,128)(2,1)S(1)}, bf16[4,8,384]{2,1,0:T(8,128)(2,1)S(1)}, u32[]{:S(2)}, u32[]{:S(2)}) collective-permute-start(bf16[4,8,384]{2,1,0:T(8,128)(2,1)S(1)} %slice.8), channel_id=1, source_target_pairs={{0,8},{1,9},{2,10},{3,11},{4,12},{5,13},{6,14},{7,15},{8,0},{9,1},... | collective-permute-start | bytes 73736 | tf_op jit(solution)/shard_map/ppermute | solution.py:40
  15.4 0.8 %collective-permute-start.4 = (bf16[4,8,384]{2,1,0:T(8,128)(2,1)S(1)}, bf16[4,8,384]{2,1,0:T(8,128)(2,1)S(1)}, u32[]{:S(2)}, u32[]{:S(2)}) collective-permute-start(bf16[4,8,384]{2,1,0:T(8,128)(2,1)S(1)} %slice.8), channel_id=1, source_target_pairs={{0,12},{1,13},{2,14},{3,15},{4,8},{5,9},{6,10},{7,11},{8,4},{9,5},... | collective-permute-start | bytes 73736 | tf_op jit(solution)/shard_map/ppermute | solution.py:40
  16.2 0.0 collective-permute-start.3
  16.2 3.5 %shard_map.95.refs_4_ = bf16[3072,128]{1,0:T(8,128)(2,1)} custom-call(bf16[128,512]{1,0:T(8,128)(2,1)} %bitcast.49, bf16[6144,512]{1,0:T(8,128)(2,1)} %bitcast.34), custom_call_target="tpu_custom_call" | custom-call | bytes 3145728 | tf_op jit(solution)/shard_map/pallas_call | solution.py:356
  19.7 0.0 collective-permute-done.5
  19.7 0.0 collective-permute-done.4
  19.7 0.0 collective-permute-done.3
  19.8 0.0 copy-done.7
  19.8 1.3 %collective-permute-start.6 = (bf16[17,8,384]{2,1,0:T(8,128)(2,1)S(1)}, bf16[17,8,384]{2,1,0:T(8,128)(2,1)S(1)}, u32[]{:S(2)}, u32[]{:S(2)}) collective-permute-start(bf16[17,8,384]{2,1,0:T(8,128)(2,1)S(1)} %get-tuple-element.72), channel_id=1, source_target_pairs={{0,32},{16,48},{32,0},{48,16},{64,96},{80,112},{96,64},{112,80},{1... | collective-permute-start | bytes 313352 | tf_op jit(solution)/shard_map/ppermute | solution.py:31
  21.1 3.1 %collective-permute-start.12 = (bf16[4,144,384]{2,1,0:T(8,128)(2,1)S(1)}, bf16[4,144,384]{2,1,0:T(8,128)(2,1)S(1)}, u32[]{:S(2)}, u32[]{:S(2)}) collective-permute-start(bf16[4,144,384]{2,1,0:T(8,128)(2,1)S(1)} %pad_maximum_fusion), channel_id=1, source_target_pairs={{0,8},{1,9},{2,10},{3,11},{4,12},{5,13},{6,14},{7,15},{8,0},{9,1},... | collective-permute-start | bytes 1327112 | tf_op jit(solution)/shard_map/ppermute | solution.py:40
  24.2 0.8 %collective-permute-start.11 = (bf16[4,144,384]{2,1,0:T(8,128)(2,1)S(1)}, bf16[4,144,384]{2,1,0:T(8,128)(2,1)S(1)}, u32[]{:S(2)}, u32[]{:S(2)}) collective-permute-start(bf16[4,144,384]{2,1,0:T(8,128)(2,1)S(1)} %pad_maximum_fusion), channel_id=1, source_target_pairs={{0,12},{1,13},{2,14},{3,15},{4,8},{5,9},{6,10},{7,11},{8,4},{9,5},... | collective-permute-start | bytes 1327112 | tf_op jit(solution)/shard_map/ppermute | solution.py:40
  25.0 0.0 collective-permute-start.10
  25.0 2.5 %collective-permute-start.8 = (bf16[17,8,384]{2,1,0:T(8,128)(2,1)S(1)}, bf16[17,8,384]{2,1,0:T(8,128)(2,1)S(1)}, u32[]{:S(2)}, u32[]{:S(2)}) collective-permute-start(bf16[17,8,384]{2,1,0:T(8,128)(2,1)S(1)} %get-tuple-element.72), channel_id=1, source_target_pairs={{0,64},{16,80},{32,96},{48,112},{64,0},{80,16},{96,32},{112,48},{1... | collective-permute-start | bytes 313352 | tf_op jit(solution)/shard_map/ppermute | solution.py:31
  27.4 0.0 collective-permute-done.6
  27.4 0.2 collective-permute-start.7
  27.6 4.8 %collective-permute-done.7 = bf16[17,8,384]{2,1,0:T(8,128)(2,1)S(1)} collective-permute-done((bf16[17,8,384]{2,1,0:T(8,128)(2,1)S(1)}, bf16[17,8,384]{2,1,0:T(8,128)(2,1)S(1)}, u32[]{:S(2)}, u32[]{:S(2)}) %collective-permute-start.7) | collective-permute-done | bytes 104480 | tf_op jit(solution)/shard_map/ppermute | solution.py:31
  32.5 0.0 collective-permute-done.8
  32.5 0.0 copy-start.1
  32.5 4.7 %collective-permute-start.9 = (bf16[68,8,384]{2,1,0:T(8,128)(2,1)S(1)}, bf16[68,8,384]{2,1,0:T(8,128)(2,1)S(1)}, u32[]{:S(2)}, u32[]{:S(2)}) collective-permute-start(bf16[68,8,384]{2,1,0:T(8,128)(2,1)S(1)} %constant_dynamic-update-slice_fusion.5.refs_1_.refs_0_.refs_6_), channel_id=1, source_target_pairs={{0,16},{16,0},{32,48},{48,32},{64,80},{80,64},{96,112},{112,96},{1... | collective-permute-start | bytes 1253384 | tf_op jit(solution)/shard_map/ppermute | solution.py:31
  37.2 0.0 collective-permute-done.12
  37.2 0.0 collective-permute-done.11
  37.2 0.0 copy-start.3
  37.2 0.0 collective-permute-done.10
  37.2 0.0 copy-start.4
  37.2 1.3 %collective-permute-done.9.refs_2_.refs_1_.refs_7_ = bf16[68,8,384]{2,1,0:T(8,128)(2,1)S(1)} collective-permute-done((bf16[68,8,384]{2,1,0:T(8,128)(2,1)S(1)}, bf16[68,8,384]{2,1,0:T(8,128)(2,1)S(1)}, u32[]{:S(2)}, u32[]{:S(2)}) %collective-permute-start.9) | collective-permute-done | bytes 417824 | tf_op jit(solution)/shard_map/ppermute | solution.py:31
  38.6 0.0 copy-done.4
  38.6 0.8 %copy-done.5 = bf16[68,8,384]{2,1,0:T(8,128)(2,1)} copy-done((bf16[68,8,384]{2,1,0:T(8,128)(2,1)}, bf16[68,8,384]{2,1,0:T(8,128)(2,1)S(1)}, u32[]{:S(2)}) %copy-start.5) | copy-done | bytes 417816
  39.4 0.0 copy-done
  39.4 0.0 copy-done.1
  39.4 0.0 copy-done.2
  39.4 3.8 %shard_map.96 = (bf16[64,16,128]{2,1,0:T(8,128)(2,1)}, f32[8,8,128]{2,1,0:T(8,128)}, f32[8,128]{1,0:T(8,128)}) custom-call(bf16[128,256]{1,0:T(8,128)(2,1)} %get-tuple-element.34.refs_0_.refs_4_, bf16[68,8,384]{2,1,0:T(8,128)(2,1)} %copy-done.1, bf16[68,8,384]{2,1,0:T(8,128)(2,1)} %copy-done.5, bf16[3072,128]{1,0:T(8,128)(2,1)} %shard_map.94.refs_3_, ...), custom_call_target="tpu_custom_call" | custom-call | tf_op jit(solution)/shard_map/pallas_call | solution.py:356
  43.2 8.0 %all-to-all-start = ((bf16[128,8,128]{2,1,0:T(8,128)(2,1)}), bf16[128,8,128]{2,1,0:T(8,128)(2,1)S(1)}, u32[]{:S(2)}, u32[]{:S(2)}) async-start(bf16[128,8,128]{2,1,0:T(8,128)(2,1)} %bitcast.53), calls=%async_computation | async-start | bytes 524288 | tf_op jit(solution)/shard_map/all_to_all | solution.py:434
  51.2 5.9 %shard_map.97 = (bf16[8,128,256]{2,1,0:T(8,128)(2,1)}, bf16[128,512]{1,0:T(8,128)(2,1)}, f32[8,256]{1,0:T(8,128)}, bf16[32,384]{1,0:T(8,128)(2,1)}, f32[128,512]{1,0:T(8,128)}, /*index=5*/bf16[64,512]{1,0:T(8,128)(2,1)}) custom-call(bf16[68,8,384]{2,1,0:T(8,128)(2,1)} %copy-done.1, bf16[68,8,384]{2,1,0:T(8,128)(2,1)} %copy-done.5, ...), custom_call_target="tpu_custom_call" | custom-call | flops 1000000000 | bytes 10000000 | tf_op jit(solution)/shard_map/pallas_call | solution.py:356
  57.1 5.5 %all-to-all-done = bf16[128,8,128]{2,1,0:T(8,128)(2,1)S(1)} async-done(((bf16[128,8,128]{2,1,0:T(8,128)(2,1)}), bf16[128,8,128]{2,1,0:T(8,128)(2,1)S(1)}, u32[]{:S(2)}, u32[]{:S(2)}) %all-to-all-start) | async-done | bytes 262176 | tf_op jit(solution)/shard_map/all_to_all | solution.py:434
  62.6 0.6 convert_reduce_fusion.refs_0_
  63.3 5.4 %shard_map.98 = (bf16[32,384]{1,0:T(8,128)(2,1)}, bf16[128,512]{1,0:T(8,128)(2,1)}, f32[8,384]{1,0:T(8,128)}, bf16[6144,512]{1,0:T(8,128)(2,1)}) custom-call(f32[8,8,128]{2,1,0:T(8,128)} %convert_reduce_fusion.refs_0_, bf16[8,128,256]{2,1,0:T(8,128)(2,1)} %get-tuple-element.53.refs_1_, f32[8,256]{1,0:T(8,128)} %get-tuple-element.54.refs_2_, ...), custom_call_target="tpu_custom_call" | custom-call | flops 1207959552 | bytes 6291456 | tf_op jit(solution)/shard_map/pallas_call | solution.py:356
  (13 shorter events, 0.1 us)
Async XLA Ops:
  2.8 9.8 %copy-start.6 = (bf16[144,384]{1,0:T(8,128)(2,1)S(1)}, bf16[144,384]{1,0:T(8,128)(2,1)}, u32[]{:S(2)}) copy-start(bf16[144,384]{1,0:T(8,128)(2,1)} %get-tuple-element.38) | copy-start | bytes 331780
  2.8 8.7 %collective-permute-start.2 = (bf16[144,384]{1,0:T(8,128)(2,1)}, bf16[144,384]{1,0:T(8,128)(2,1)S(1)}, u32[]{:S(2)}, u32[]{:S(2)}) collective-permute-start(bf16[144,384]{1,0:T(8,128)(2,1)} %get-tuple-element.38), channel_id=1, source_target_pairs={{0,2},{1,3},{2,0},{3,1},{4,6},{5,7},{6,4},{7,5},{8,10},{9,11},{10,... | collective-permute-start | bytes 331784 | tf_op jit(solution)/shard_map/ppermute | solution.py:40
  7.3 5.3 %collective-permute-start.1 = (bf16[144,384]{1,0:T(8,128)(2,1)}, bf16[144,384]{1,0:T(8,128)(2,1)S(1)}, u32[]{:S(2)}, u32[]{:S(2)}) collective-permute-start(bf16[144,384]{1,0:T(8,128)(2,1)} %get-tuple-element.38), channel_id=1, source_target_pairs={{0,3},{1,2},{2,1},{3,0},{4,7},{5,6},{6,5},{7,4},{8,11},{9,10},{10,... | collective-permute-start | bytes 331784 | tf_op jit(solution)/shard_map/ppermute | solution.py:40
  7.7 4.9 %collective-permute-start = (bf16[144,384]{1,0:T(8,128)(2,1)}, bf16[144,384]{1,0:T(8,128)(2,1)S(1)}, u32[]{:S(2)}, u32[]{:S(2)}) collective-permute-start(bf16[144,384]{1,0:T(8,128)(2,1)} %get-tuple-element.38), channel_id=1, source_target_pairs={{0,1},{1,0},{2,3},{3,2},{4,5},{5,4},{6,7},{7,6},{8,9},{9,8},{10,11... | collective-permute-start | bytes 331784 | tf_op jit(solution)/shard_map/ppermute | solution.py:40
  8.1 11.7 %copy-start.7 = (bf16[16,384]{1,0:T(8,128)(2,1)S(1)}, bf16[16,384]{1,0:T(8,128)(2,1)}, u32[]{:S(2)}) copy-start(bf16[16,384]{1,0:T(8,128)(2,1)} %get-tuple-element.48) | copy-start | bytes 36868
  12.7 26.6 %copy-start = (bf16[4,144,384]{2,1,0:T(8,128)(2,1)}, bf16[4,144,384]{2,1,0:T(8,128)(2,1)S(1)}, u32[]{:S(2)}) copy-start(bf16[4,144,384]{2,1,0:T(8,128)(2,1)S(1)} %pad_maximum_fusion) | copy-start | bytes 1327108
  12.7 7.0 %collective-permute-start.5 = (bf16[4,8,384]{2,1,0:T(8,128)(2,1)S(1)}, bf16[4,8,384]{2,1,0:T(8,128)(2,1)S(1)}, u32[]{:S(2)}, u32[]{:S(2)}) collective-permute-start(bf16[4,8,384]{2,1,0:T(8,128)(2,1)S(1)} %slice.8), channel_id=1, source_target_pairs={{0,8},{1,9},{2,10},{3,11},{4,12},{5,13},{6,14},{7,15},{8,0},{9,1},... | collective-permute-start | bytes 73736 | tf_op jit(solution)/shard_map/ppermute | solution.py:40
  15.4 4.3 %collective-permute-start.4 = (bf16[4,8,384]{2,1,0:T(8,128)(2,1)S(1)}, bf16[4,8,384]{2,1,0:T(8,128)(2,1)S(1)}, u32[]{:S(2)}, u32[]{:S(2)}) collective-permute-start(bf16[4,8,384]{2,1,0:T(8,128)(2,1)S(1)} %slice.8), channel_id=1, source_target_pairs={{0,12},{1,13},{2,14},{3,15},{4,8},{5,9},{6,10},{7,11},{8,4},{9,5},... | collective-permute-start | bytes 73736 | tf_op jit(solution)/shard_map/ppermute | solution.py:40
  16.2 3.5 %collective-permute-start.3 = (bf16[4,8,384]{2,1,0:T(8,128)(2,1)S(1)}, bf16[4,8,384]{2,1,0:T(8,128)(2,1)S(1)}, u32[]{:S(2)}, u32[]{:S(2)}) collective-permute-start(bf16[4,8,384]{2,1,0:T(8,128)(2,1)S(1)} %slice.8), channel_id=1, source_target_pairs={{0,4},{1,5},{2,6},{3,7},{4,0},{5,1},{6,2},{7,3},{8,12},{9,13},{10,... | collective-permute-start | bytes 73736 | tf_op jit(solution)/shard_map/ppermute | solution.py:40
  19.8 7.6 %collective-permute-start.6 = (bf16[17,8,384]{2,1,0:T(8,128)(2,1)S(1)}, bf16[17,8,384]{2,1,0:T(8,128)(2,1)S(1)}, u32[]{:S(2)}, u32[]{:S(2)}) collective-permute-start(bf16[17,8,384]{2,1,0:T(8,128)(2,1)S(1)} %get-tuple-element.72), channel_id=1, source_target_pairs={{0,32},{16,48},{32,0},{48,16},{64,96},{80,112},{96,64},{112,80},{1... | collective-permute-start | bytes 313352 | tf_op jit(solution)/shard_map/ppermute | solution.py:31
  21.1 16.1 %collective-permute-start.12 = (bf16[4,144,384]{2,1,0:T(8,128)(2,1)S(1)}, bf16[4,144,384]{2,1,0:T(8,128)(2,1)S(1)}, u32[]{:S(2)}, u32[]{:S(2)}) collective-permute-start(bf16[4,144,384]{2,1,0:T(8,128)(2,1)S(1)} %pad_maximum_fusion), channel_id=1, source_target_pairs={{0,8},{1,9},{2,10},{3,11},{4,12},{5,13},{6,14},{7,15},{8,0},{9,1},... | collective-permute-start | bytes 1327112 | tf_op jit(solution)/shard_map/ppermute | solution.py:40
  24.2 13.0 %collective-permute-start.11 = (bf16[4,144,384]{2,1,0:T(8,128)(2,1)S(1)}, bf16[4,144,384]{2,1,0:T(8,128)(2,1)S(1)}, u32[]{:S(2)}, u32[]{:S(2)}) collective-permute-start(bf16[4,144,384]{2,1,0:T(8,128)(2,1)S(1)} %pad_maximum_fusion), channel_id=1, source_target_pairs={{0,12},{1,13},{2,14},{3,15},{4,8},{5,9},{6,10},{7,11},{8,4},{9,5},... | collective-permute-start | bytes 1327112 | tf_op jit(solution)/shard_map/ppermute | solution.py:40
  25.0 12.3 %collective-permute-start.10 = (bf16[4,144,384]{2,1,0:T(8,128)(2,1)S(1)}, bf16[4,144,384]{2,1,0:T(8,128)(2,1)S(1)}, u32[]{:S(2)}, u32[]{:S(2)}) collective-permute-start(bf16[4,144,384]{2,1,0:T(8,128)(2,1)S(1)} %pad_maximum_fusion), channel_id=1, source_target_pairs={{0,4},{1,5},{2,6},{3,7},{4,0},{5,1},{6,2},{7,3},{8,12},{9,13},{10,... | collective-permute-start | bytes 1327112 | tf_op jit(solution)/shard_map/ppermute | solution.py:40
  25.0 7.5 %collective-permute-start.8 = (bf16[17,8,384]{2,1,0:T(8,128)(2,1)S(1)}, bf16[17,8,384]{2,1,0:T(8,128)(2,1)S(1)}, u32[]{:S(2)}, u32[]{:S(2)}) collective-permute-start(bf16[17,8,384]{2,1,0:T(8,128)(2,1)S(1)} %get-tuple-element.72), channel_id=1, source_target_pairs={{0,64},{16,80},{32,96},{48,112},{64,0},{80,16},{96,32},{112,48},{1... | collective-permute-start | bytes 313352 | tf_op jit(solution)/shard_map/ppermute | solution.py:31
  27.4 5.0 %collective-permute-start.7 = (bf16[17,8,384]{2,1,0:T(8,128)(2,1)S(1)}, bf16[17,8,384]{2,1,0:T(8,128)(2,1)S(1)}, u32[]{:S(2)}, u32[]{:S(2)}) collective-permute-start(bf16[17,8,384]{2,1,0:T(8,128)(2,1)S(1)} %get-tuple-element.72), channel_id=1, source_target_pairs={{0,96},{16,112},{32,64},{48,80},{64,32},{80,48},{96,0},{112,16},{1... | collective-permute-start | bytes 313352 | tf_op jit(solution)/shard_map/ppermute | solution.py:31
  32.5 6.8 %copy-start.1 = (bf16[68,8,384]{2,1,0:T(8,128)(2,1)}, bf16[68,8,384]{2,1,0:T(8,128)(2,1)S(1)}, u32[]{:S(2)}) copy-start(bf16[68,8,384]{2,1,0:T(8,128)(2,1)S(1)} %constant_dynamic-update-slice_fusion.5.refs_1_.refs_0_.refs_6_) | copy-start | bytes 1253380
  32.5 6.0 %collective-permute-start.9 = (bf16[68,8,384]{2,1,0:T(8,128)(2,1)S(1)}, bf16[68,8,384]{2,1,0:T(8,128)(2,1)S(1)}, u32[]{:S(2)}, u32[]{:S(2)}) collective-permute-start(bf16[68,8,384]{2,1,0:T(8,128)(2,1)S(1)} %constant_dynamic-update-slice_fusion.5.refs_1_.refs_0_.refs_6_), channel_id=1, source_target_pairs={{0,16},{16,0},{32,48},{48,32},{64,80},{80,64},{96,112},{112,96},{1... | collective-permute-start | bytes 1253384 | tf_op jit(solution)/shard_map/ppermute | solution.py:31
  37.2 2.2 %copy-start.2 = (bf16[4,144,384]{2,1,0:T(8,128)(2,1)}, bf16[4,144,384]{2,1,0:T(8,128)(2,1)S(1)}, u32[]{:S(2)}) copy-start(bf16[4,144,384]{2,1,0:T(8,128)(2,1)S(1)} %collective-permute-done.12) | copy-start | bytes 1327108
  37.2 2.2 %copy-start.3 = (bf16[4,144,384]{2,1,0:T(8,128)(2,1)}, bf16[4,144,384]{2,1,0:T(8,128)(2,1)S(1)}, u32[]{:S(2)}) copy-start(bf16[4,144,384]{2,1,0:T(8,128)(2,1)S(1)} %collective-permute-done.11) | copy-start | bytes 1327108
  37.2 1.4 %copy-start.4 = (bf16[4,144,384]{2,1,0:T(8,128)(2,1)}, bf16[4,144,384]{2,1,0:T(8,128)(2,1)S(1)}, u32[]{:S(2)}) copy-start(bf16[4,144,384]{2,1,0:T(8,128)(2,1)S(1)} %collective-permute-done.10) | copy-start | bytes 1327108
  38.6 0.8 %copy-start.5 = (bf16[68,8,384]{2,1,0:T(8,128)(2,1)}, bf16[68,8,384]{2,1,0:T(8,128)(2,1)S(1)}, u32[]{:S(2)}) copy-start(bf16[68,8,384]{2,1,0:T(8,128)(2,1)S(1)} %collective-permute-done.9.refs_2_.refs_1_.refs_7_) | copy-start | bytes 1253380
  43.2 19.4 %all-to-all-start = ((bf16[128,8,128]{2,1,0:T(8,128)(2,1)}), bf16[128,8,128]{2,1,0:T(8,128)(2,1)S(1)}, u32[]{:S(2)}, u32[]{:S(2)}) async-start(bf16[128,8,128]{2,1,0:T(8,128)(2,1)} %bitcast.53), calls=%async_computation | async-start | bytes 524288 | tf_op jit(solution)/shard_map/all_to_all | solution.py:434

commit v8 on v6

--- a/solution.py
+++ b/solution.py
@@ -250,6 +250,8 @@
     tokens, width = codes.buffer.shape[1], x.buffer.shape[1]
     ways = obuf.shape[0] // width
     loads = load_rows(blocks, rows, lsems)
+    for item in (product, mixed, gate, x, grads):
+        item.copy.start()
     me, at, odd = place()
     parts_of = []
     for s in range(layers):
@@ -304,7 +306,6 @@
 class Staged:
     def __init__(self, source, buffer, semaphore):
         self.copy = pltpu.make_async_copy(source, buffer, semaphore)
-        self.copy.start()
         self.buffer, self.waited = buffer, False
 
     @property
@@ -327,7 +328,7 @@
             self.sent = True
 
 
-def call(kernel, staged, raw, results, raw_results=(), scratch=(), flops=0, moved=0):
+def call(kernel, staged, raw, results, raw_results=(), scratch=(), late=0, flops=0, moved=0):
     counts = (len(staged), len(raw), len(results), len(raw_results))
 
     def body(*refs):
@@ -338,6 +339,8 @@
         sources, raws, targets, raw_targets, ibufs, obufs = groups
         sems, rest = refs[at], refs[at + 1:]
         ins = [Staged(r, v, sems.at[n]) for n, (r, v) in enumerate(zip(sources, ibufs))]
+        for item in ins[:counts[0] - late]:
+            item.copy.start()
         outs = [
             Result(v, r, sems.at[counts[0] + n]) for n, (r, v) in enumerate(zip(targets, obufs))
         ]
@@ -477,6 +480,7 @@
             pltpu.VMEM((full, units), BF16),
             pltpu.SemaphoreType.DMA((ways // 2,)),
         ],
+        late=5,
         flops=2 * 192 * full * units,
         moved=full * units * 2,
     )

time: 69 us -> 68.9 us (level)
  no operation moved by 1% of the time
where the time goes in v8:
time: 68.9 us; the launch traced here: 68.8 us
  starting transfers between devices  29.1 us (42%)
  Pallas kernels  24.3 us (35%)
  waiting for transfers between devices  12.9 us (19%)
  local copies, waits for them, and re-layouts  0.92 us (1%)
  between operations  0.85 us (1%)
  other arithmetic  0.71 us (1%)
    pallas_call x6, Pallas kernels, call(): pl.pallas_call(body, out_shape=shapes, in_specs=[HBM] * (counts[0] + coun...  24.3 us
    ppermute x9, starting transfers between devices, turn(): return lax.ppermute(value, ('section', 'dp'), pairs)  12.6 us
    ppermute x4, starting transfers between devices, swap(): return lax.ppermute(value, axis, [(i, i ^ distance) for i in range(count)])  8.61 us
    all_to_all x1, starting transfers between devices, per_device(): got_table = lax.all_to_all(table, ('section', 'dp'), 0, 0, tiled=True)  7.95 us
    ppermute x4, waiting for transfers between devices, swap(): return lax.ppermute(value, axis, [(i, i ^ distance) for i in range(count)])  6.17 us
    all_to_all x1, waiting for transfers between devices, per_device(): got_table = lax.all_to_all(table, ('section', 'dp'), 0, 0, tiled=True)  5.58 us
  transfers between devices with their start and end apart: 14, of which 4 were waited for; matrix products, arithmetic and copies ran while one was open for 0% of the time, Pallas kernels for 19%

profile of v8, /device:TPU:1, one launch (start us, length us, event | category | flops | bytes accessed | tf_op | source)
XLA Modules:
  0.0 68.8 jit_solution(1269961872716031693)
XLA Ops:
  0.6 2.2 %shard_map.93 = (bf16[144,384]{1,0:T(8,128)(2,1)}, bf16[128,256]{1,0:T(8,128)(2,1)}, bf16[16,384]{1,0:T(8,128)(2,1)}, bf16[32,384]{1,0:T(8,128)(2,1)}) custom-call(s32[8,64]{1,0:T(8,128)} %bitcast.60, bf16[256,384]{1,0:T(8,128)(2,1)} %bitcast.52, bf16[256,384]{1,0:T(8,128)(2,1)} %bitcast.53, bf16[8,384]{1,0:T(8,128)(2,1)} %bitcast.59), custom_call_target="tpu_custom_call" | custom-call | tf_op jit(solution)/shard_map/pallas_call | solution.py:358
  2.9 0.0 copy-start.6
  2.9 4.5 %collective-permute-start.2 = (bf16[144,384]{1,0:T(8,128)(2,1)}, bf16[144,384]{1,0:T(8,128)(2,1)S(1)}, u32[]{:S(2)}, u32[]{:S(2)}) collective-permute-start(bf16[144,384]{1,0:T(8,128)(2,1)} %get-tuple-element.38), channel_id=1, source_target_pairs={{0,2},{1,3},{2,0},{3,1},{4,6},{5,7},{6,4},{7,5},{8,10},{9,11},{10,... | collective-permute-start | bytes 331784 | tf_op jit(solution)/shard_map/ppermute | solution.py:40
  7.4 0.4 collective-permute-start.1
  7.8 0.3 collective-permute-start
  8.1 3.5 %shard_map.94.refs_3_ = bf16[3072,128]{1,0:T(8,128)(2,1)} custom-call(bf16[128,512]{1,0:T(8,128)(2,1)} %bitcast.48, bf16[6144,512]{1,0:T(8,128)(2,1)} %bitcast.33), custom_call_target="tpu_custom_call" | custom-call | bytes 3145728 | tf_op jit(solution)/shard_map/pallas_call | solution.py:358
  11.6 0.0 collective-permute-done.2
  11.6 1.1 %collective-permute-done.1 = bf16[144,384]{1,0:T(8,128)(2,1)S(1)} collective-permute-done((bf16[144,384]{1,0:T(8,128)(2,1)}, bf16[144,384]{1,0:T(8,128)(2,1)S(1)}, u32[]{:S(2)}, u32[]{:S(2)}) %collective-permute-start.1) | collective-permute-done | bytes 110624 | tf_op jit(solution)/shard_map/ppermute | solution.py:40
  12.7 0.0 collective-permute-done
  12.7 0.0 copy-done.6
  12.7 0.1 pad_maximum_fusion
  12.8 0.0 copy-start
  12.8 2.7 %collective-permute-start.5 = (bf16[4,8,384]{2,1,0:T(8,128)(2,1)S(1)}, bf16[4,8,384]{2,1,0:T(8,128)(2,1)S(1)}, u32[]{:S(2)}, u32[]{:S(2)}) collective-permute-start(bf16[4,8,384]{2,1,0:T(8,128)(2,1)S(1)} %slice.8), channel_id=1, source_target_pairs={{0,8},{1,9},{2,10},{3,11},{4,12},{5,13},{6,14},{7,15},{8,0},{9,1},... | collective-permute-start | bytes 73736 | tf_op jit(solution)/shard_map/ppermute | solution.py:40
  15.5 0.8 %collective-permute-start.4 = (bf16[4,8,384]{2,1,0:T(8,128)(2,1)S(1)}, bf16[4,8,384]{2,1,0:T(8,128)(2,1)S(1)}, u32[]{:S(2)}, u32[]{:S(2)}) collective-permute-start(bf16[4,8,384]{2,1,0:T(8,128)(2,1)S(1)} %slice.8), channel_id=1, source_target_pairs={{0,12},{1,13},{2,14},{3,15},{4,8},{5,9},{6,10},{7,11},{8,4},{9,5},... | collective-permute-start | bytes 73736 | tf_op jit(solution)/shard_map/ppermute | solution.py:40
  16.3 0.0 collective-permute-start.3
  16.3 3.5 %shard_map.95.refs_4_ = bf16[3072,128]{1,0:T(8,128)(2,1)} custom-call(bf16[128,512]{1,0:T(8,128)(2,1)} %bitcast.49, bf16[6144,512]{1,0:T(8,128)(2,1)} %bitcast.34), custom_call_target="tpu_custom_call" | custom-call | bytes 3145728 | tf_op jit(solution)/shard_map/pallas_call | solution.py:358
  19.7 0.0 collective-permute-done.5
  19.8 0.0 collective-permute-done.4
  19.8 0.0 collective-permute-done.3
  19.8 0.0 copy-done.7
  19.9 1.3 %collective-permute-start.6 = (bf16[17,8,384]{2,1,0:T(8,128)(2,1)S(1)}, bf16[17,8,384]{2,1,0:T(8,128)(2,1)S(1)}, u32[]{:S(2)}, u32[]{:S(2)}) collective-permute-start(bf16[17,8,384]{2,1,0:T(8,128)(2,1)S(1)} %get-tuple-element.72), channel_id=1, source_target_pairs={{0,32},{16,48},{32,0},{48,16},{64,96},{80,112},{96,64},{112,80},{1... | collective-permute-start | bytes 313352 | tf_op jit(solution)/shard_map/ppermute | solution.py:31
  21.2 3.1 %collective-permute-start.12 = (bf16[4,144,384]{2,1,0:T(8,128)(2,1)S(1)}, bf16[4,144,384]{2,1,0:T(8,128)(2,1)S(1)}, u32[]{:S(2)}, u32[]{:S(2)}) collective-permute-start(bf16[4,144,384]{2,1,0:T(8,128)(2,1)S(1)} %pad_maximum_fusion), channel_id=1, source_target_pairs={{0,8},{1,9},{2,10},{3,11},{4,12},{5,13},{6,14},{7,15},{8,0},{9,1},... | collective-permute-start | bytes 1327112 | tf_op jit(solution)/shard_map/ppermute | solution.py:40
  24.2 0.8 %collective-permute-start.11 = (bf16[4,144,384]{2,1,0:T(8,128)(2,1)S(1)}, bf16[4,144,384]{2,1,0:T(8,128)(2,1)S(1)}, u32[]{:S(2)}, u32[]{:S(2)}) collective-permute-start(bf16[4,144,384]{2,1,0:T(8,128)(2,1)S(1)} %pad_maximum_fusion), channel_id=1, source_target_pairs={{0,12},{1,13},{2,14},{3,15},{4,8},{5,9},{6,10},{7,11},{8,4},{9,5},... | collective-permute-start | bytes 1327112 | tf_op jit(solution)/shard_map/ppermute | solution.py:40
  25.0 0.0 collective-permute-start.10
  25.0 2.5 %collective-permute-start.8 = (bf16[17,8,384]{2,1,0:T(8,128)(2,1)S(1)}, bf16[17,8,384]{2,1,0:T(8,128)(2,1)S(1)}, u32[]{:S(2)}, u32[]{:S(2)}) collective-permute-start(bf16[17,8,384]{2,1,0:T(8,128)(2,1)S(1)} %get-tuple-element.72), channel_id=1, source_target_pairs={{0,64},{16,80},{32,96},{48,112},{64,0},{80,16},{96,32},{112,48},{1... | collective-permute-start | bytes 313352 | tf_op jit(solution)/shard_map/ppermute | solution.py:31
  27.5 0.0 collective-permute-done.6
  27.5 0.2 collective-permute-start.7
  27.7 4.8 %collective-permute-done.7 = bf16[17,8,384]{2,1,0:T(8,128)(2,1)S(1)} collective-permute-done((bf16[17,8,384]{2,1,0:T(8,128)(2,1)S(1)}, bf16[17,8,384]{2,1,0:T(8,128)(2,1)S(1)}, u32[]{:S(2)}, u32[]{:S(2)}) %collective-permute-start.7) | collective-permute-done | bytes 104480 | tf_op jit(solution)/shard_map/ppermute | solution.py:31
  32.5 0.0 collective-permute-done.8
  32.6 0.0 copy-start.1
  32.6 4.6 %collective-permute-start.9 = (bf16[68,8,384]{2,1,0:T(8,128)(2,1)S(1)}, bf16[68,8,384]{2,1,0:T(8,128)(2,1)S(1)}, u32[]{:S(2)}, u32[]{:S(2)}) collective-permute-start(bf16[68,8,384]{2,1,0:T(8,128)(2,1)S(1)} %constant_dynamic-update-slice_fusion.5.refs_1_.refs_0_.refs_6_), channel_id=1, source_target_pairs={{0,16},{16,0},{32,48},{48,32},{64,80},{80,64},{96,112},{112,96},{1... | collective-permute-start | bytes 1253384 | tf_op jit(solution)/shard_map/ppermute | solution.py:31
  37.2 0.0 collective-permute-done.12
  37.2 0.0 collective-permute-done.11
  37.2 0.0 copy-start.3
  37.3 0.0 collective-permute-done.10
  37.3 0.0 copy-start.4
  37.3 1.3 %collective-permute-done.9.refs_2_.refs_1_.refs_7_ = bf16[68,8,384]{2,1,0:T(8,128)(2,1)S(1)} collective-permute-done((bf16[68,8,384]{2,1,0:T(8,128)(2,1)S(1)}, bf16[68,8,384]{2,1,0:T(8,128)(2,1)S(1)}, u32[]{:S(2)}, u32[]{:S(2)}) %collective-permute-start.9) | collective-permute-done | bytes 417824 | tf_op jit(solution)/shard_map/ppermute | solution.py:31
  38.6 0.0 copy-done.4
  38.6 0.8 %copy-done.5 = bf16[68,8,384]{2,1,0:T(8,128)(2,1)} copy-done((bf16[68,8,384]{2,1,0:T(8,128)(2,1)}, bf16[68,8,384]{2,1,0:T(8,128)(2,1)S(1)}, u32[]{:S(2)}) %copy-start.5) | copy-done | bytes 417816
  39.4 0.0 copy-done
  39.4 0.0 copy-done.1
  39.4 0.0 copy-done.2
  39.4 3.8 %shard_map.96 = (bf16[64,16,128]{2,1,0:T(8,128)(2,1)}, f32[8,8,128]{2,1,0:T(8,128)}, f32[8,128]{1,0:T(8,128)}) custom-call(bf16[128,256]{1,0:T(8,128)(2,1)} %get-tuple-element.34.refs_0_.refs_4_, bf16[68,8,384]{2,1,0:T(8,128)(2,1)} %copy-done.1, bf16[68,8,384]{2,1,0:T(8,128)(2,1)} %copy-done.5, bf16[3072,128]{1,0:T(8,128)(2,1)} %shard_map.94.refs_3_, ...), custom_call_target="tpu_custom_call" | custom-call | tf_op jit(solution)/shard_map/pallas_call | solution.py:358
  43.3 8.0 %all-to-all-start = ((bf16[128,8,128]{2,1,0:T(8,128)(2,1)}), bf16[128,8,128]{2,1,0:T(8,128)(2,1)S(1)}, u32[]{:S(2)}, u32[]{:S(2)}) async-start(bf16[128,8,128]{2,1,0:T(8,128)(2,1)} %bitcast.51), calls=%async_computation | async-start | bytes 524288 | tf_op jit(solution)/shard_map/all_to_all | solution.py:437
  51.2 5.9 %shard_map.97 = (bf16[8,128,256]{2,1,0:T(8,128)(2,1)}, bf16[128,512]{1,0:T(8,128)(2,1)}, f32[8,256]{1,0:T(8,128)}, f32[128,512]{1,0:T(8,128)}, bf16[64,512]{1,0:T(8,128)(2,1)}) custom-call(bf16[68,8,384]{2,1,0:T(8,128)(2,1)} %copy-done.1, bf16[68,8,384]{2,1,0:T(8,128)(2,1)} %copy-done.5, bf16[128,512]{1,0:T(8,128)(2,1)} %bitcast.50, ...), custom_call_target="tpu_custom_call" | custom-call | flops 1000000000 | bytes 10000000 | tf_op jit(solution)/shard_map/pallas_call | solution.py:358
  57.1 5.6 %all-to-all-done = bf16[128,8,128]{2,1,0:T(8,128)(2,1)S(1)} async-done(((bf16[128,8,128]{2,1,0:T(8,128)(2,1)}), bf16[128,8,128]{2,1,0:T(8,128)(2,1)S(1)}, u32[]{:S(2)}, u32[]{:S(2)}) %all-to-all-start) | async-done | bytes 262176 | tf_op jit(solution)/shard_map/all_to_all | solution.py:437
  62.7 0.6 convert_reduce_fusion.refs_0_
  63.3 5.4 %shard_map.98 = (bf16[32,384]{1,0:T(8,128)(2,1)}, bf16[128,512]{1,0:T(8,128)(2,1)}, f32[8,384]{1,0:T(8,128)}, bf16[6144,512]{1,0:T(8,128)(2,1)}) custom-call(f32[8,8,128]{2,1,0:T(8,128)} %convert_reduce_fusion.refs_0_, bf16[8,128,256]{2,1,0:T(8,128)(2,1)} %get-tuple-element.53.refs_1_, f32[8,256]{1,0:T(8,128)} %get-tuple-element.54.refs_2_, ...), custom_call_target="tpu_custom_call" | custom-call | flops 1207959552 | bytes 6291456 | tf_op jit(solution)/shard_map/pallas_call | solution.py:358
  (13 shorter events, 0.1 us)
Async XLA Ops:
  2.9 9.8 %copy-start.6 = (bf16[144,384]{1,0:T(8,128)(2,1)S(1)}, bf16[144,384]{1,0:T(8,128)(2,1)}, u32[]{:S(2)}) copy-start(bf16[144,384]{1,0:T(8,128)(2,1)} %get-tuple-element.38) | copy-start | bytes 331780
  2.9 8.7 %collective-permute-start.2 = (bf16[144,384]{1,0:T(8,128)(2,1)}, bf16[144,384]{1,0:T(8,128)(2,1)S(1)}, u32[]{:S(2)}, u32[]{:S(2)}) collective-permute-start(bf16[144,384]{1,0:T(8,128)(2,1)} %get-tuple-element.38), channel_id=1, source_target_pairs={{0,2},{1,3},{2,0},{3,1},{4,6},{5,7},{6,4},{7,5},{8,10},{9,11},{10,... | collective-permute-start | bytes 331784 | tf_op jit(solution)/shard_map/ppermute | solution.py:40
  7.4 5.3 %collective-permute-start.1 = (bf16[144,384]{1,0:T(8,128)(2,1)}, bf16[144,384]{1,0:T(8,128)(2,1)S(1)}, u32[]{:S(2)}, u32[]{:S(2)}) collective-permute-start(bf16[144,384]{1,0:T(8,128)(2,1)} %get-tuple-element.38), channel_id=1, source_target_pairs={{0,3},{1,2},{2,1},{3,0},{4,7},{5,6},{6,5},{7,4},{8,11},{9,10},{10,... | collective-permute-start | bytes 331784 | tf_op jit(solution)/shard_map/ppermute | solution.py:40
  7.8 4.9 %collective-permute-start = (bf16[144,384]{1,0:T(8,128)(2,1)}, bf16[144,384]{1,0:T(8,128)(2,1)S(1)}, u32[]{:S(2)}, u32[]{:S(2)}) collective-permute-start(bf16[144,384]{1,0:T(8,128)(2,1)} %get-tuple-element.38), channel_id=1, source_target_pairs={{0,1},{1,0},{2,3},{3,2},{4,5},{5,4},{6,7},{7,6},{8,9},{9,8},{10,11... | collective-permute-start | bytes 331784 | tf_op jit(solution)/shard_map/ppermute | solution.py:40
  8.1 11.7 %copy-start.7 = (bf16[16,384]{1,0:T(8,128)(2,1)S(1)}, bf16[16,384]{1,0:T(8,128)(2,1)}, u32[]{:S(2)}) copy-start(bf16[16,384]{1,0:T(8,128)(2,1)} %get-tuple-element.48) | copy-start | bytes 36868
  12.8 26.6 %copy-start = (bf16[4,144,384]{2,1,0:T(8,128)(2,1)}, bf16[4,144,384]{2,1,0:T(8,128)(2,1)S(1)}, u32[]{:S(2)}) copy-start(bf16[4,144,384]{2,1,0:T(8,128)(2,1)S(1)} %pad_maximum_fusion) | copy-start | bytes 1327108
  12.8 7.0 %collective-permute-start.5 = (bf16[4,8,384]{2,1,0:T(8,128)(2,1)S(1)}, bf16[4,8,384]{2,1,0:T(8,128)(2,1)S(1)}, u32[]{:S(2)}, u32[]{:S(2)}) collective-permute-start(bf16[4,8,384]{2,1,0:T(8,128)(2,1)S(1)} %slice.8), channel_id=1, source_target_pairs={{0,8},{1,9},{2,10},{3,11},{4,12},{5,13},{6,14},{7,15},{8,0},{9,1},... | collective-permute-start | bytes 73736 | tf_op jit(solution)/shard_map/ppermute | solution.py:40
  15.5 4.3 %collective-permute-start.4 = (bf16[4,8,384]{2,1,0:T(8,128)(2,1)S(1)}, bf16[4,8,384]{2,1,0:T(8,128)(2,1)S(1)}, u32[]{:S(2)}, u32[]{:S(2)}) collective-permute-start(bf16[4,8,384]{2,1,0:T(8,128)(2,1)S(1)} %slice.8), channel_id=1, source_target_pairs={{0,12},{1,13},{2,14},{3,15},{4,8},{5,9},{6,10},{7,11},{8,4},{9,5},... | collective-permute-start | bytes 73736 | tf_op jit(solution)/shard_map/ppermute | solution.py:40
  16.3 3.5 %collective-permute-start.3 = (bf16[4,8,384]{2,1,0:T(8,128)(2,1)S(1)}, bf16[4,8,384]{2,1,0:T(8,128)(2,1)S(1)}, u32[]{:S(2)}, u32[]{:S(2)}) collective-permute-start(bf16[4,8,384]{2,1,0:T(8,128)(2,1)S(1)} %slice.8), channel_id=1, source_target_pairs={{0,4},{1,5},{2,6},{3,7},{4,0},{5,1},{6,2},{7,3},{8,12},{9,13},{10,... | collective-permute-start | bytes 73736 | tf_op jit(solution)/shard_map/ppermute | solution.py:40
  19.9 7.6 %collective-permute-start.6 = (bf16[17,8,384]{2,1,0:T(8,128)(2,1)S(1)}, bf16[17,8,384]{2,1,0:T(8,128)(2,1)S(1)}, u32[]{:S(2)}, u32[]{:S(2)}) collective-permute-start(bf16[17,8,384]{2,1,0:T(8,128)(2,1)S(1)} %get-tuple-element.72), channel_id=1, source_target_pairs={{0,32},{16,48},{32,0},{48,16},{64,96},{80,112},{96,64},{112,80},{1... | collective-permute-start | bytes 313352 | tf_op jit(solution)/shard_map/ppermute | solution.py:31
  21.2 16.1 %collective-permute-start.12 = (bf16[4,144,384]{2,1,0:T(8,128)(2,1)S(1)}, bf16[4,144,384]{2,1,0:T(8,128)(2,1)S(1)}, u32[]{:S(2)}, u32[]{:S(2)}) collective-permute-start(bf16[4,144,384]{2,1,0:T(8,128)(2,1)S(1)} %pad_maximum_fusion), channel_id=1, source_target_pairs={{0,8},{1,9},{2,10},{3,11},{4,12},{5,13},{6,14},{7,15},{8,0},{9,1},... | collective-permute-start | bytes 1327112 | tf_op jit(solution)/shard_map/ppermute | solution.py:40
  24.2 13.0 %collective-permute-start.11 = (bf16[4,144,384]{2,1,0:T(8,128)(2,1)S(1)}, bf16[4,144,384]{2,1,0:T(8,128)(2,1)S(1)}, u32[]{:S(2)}, u32[]{:S(2)}) collective-permute-start(bf16[4,144,384]{2,1,0:T(8,128)(2,1)S(1)} %pad_maximum_fusion), channel_id=1, source_target_pairs={{0,12},{1,13},{2,14},{3,15},{4,8},{5,9},{6,10},{7,11},{8,4},{9,5},... | collective-permute-start | bytes 1327112 | tf_op jit(solution)/shard_map/ppermute | solution.py:40
  25.0 12.3 %collective-permute-start.10 = (bf16[4,144,384]{2,1,0:T(8,128)(2,1)S(1)}, bf16[4,144,384]{2,1,0:T(8,128)(2,1)S(1)}, u32[]{:S(2)}, u32[]{:S(2)}) collective-permute-start(bf16[4,144,384]{2,1,0:T(8,128)(2,1)S(1)} %pad_maximum_fusion), channel_id=1, source_target_pairs={{0,4},{1,5},{2,6},{3,7},{4,0},{5,1},{6,2},{7,3},{8,12},{9,13},{10,... | collective-permute-start | bytes 1327112 | tf_op jit(solution)/shard_map/ppermute | solution.py:40
  25.0 7.5 %collective-permute-start.8 = (bf16[17,8,384]{2,1,0:T(8,128)(2,1)S(1)}, bf16[17,8,384]{2,1,0:T(8,128)(2,1)S(1)}, u32[]{:S(2)}, u32[]{:S(2)}) collective-permute-start(bf16[17,8,384]{2,1,0:T(8,128)(2,1)S(1)} %get-tuple-element.72), channel_id=1, source_target_pairs={{0,64},{16,80},{32,96},{48,112},{64,0},{80,16},{96,32},{112,48},{1... | collective-permute-start | bytes 313352 | tf_op jit(solution)/shard_map/ppermute | solution.py:31
  27.5 5.0 %collective-permute-start.7 = (bf16[17,8,384]{2,1,0:T(8,128)(2,1)S(1)}, bf16[17,8,384]{2,1,0:T(8,128)(2,1)S(1)}, u32[]{:S(2)}, u32[]{:S(2)}) collective-permute-start(bf16[17,8,384]{2,1,0:T(8,128)(2,1)S(1)} %get-tuple-element.72), channel_id=1, source_target_pairs={{0,96},{16,112},{32,64},{48,80},{64,32},{80,48},{96,0},{112,16},{1... | collective-permute-start | bytes 313352 | tf_op jit(solution)/shard_map/ppermute | solution.py:31
  32.6 6.8 %copy-start.1 = (bf16[68,8,384]{2,1,0:T(8,128)(2,1)}, bf16[68,8,384]{2,1,0:T(8,128)(2,1)S(1)}, u32[]{:S(2)}) copy-start(bf16[68,8,384]{2,1,0:T(8,128)(2,1)S(1)} %constant_dynamic-update-slice_fusion.5.refs_1_.refs_0_.refs_6_) | copy-start | bytes 1253380
  32.6 6.0 %collective-permute-start.9 = (bf16[68,8,384]{2,1,0:T(8,128)(2,1)S(1)}, bf16[68,8,384]{2,1,0:T(8,128)(2,1)S(1)}, u32[]{:S(2)}, u32[]{:S(2)}) collective-permute-start(bf16[68,8,384]{2,1,0:T(8,128)(2,1)S(1)} %constant_dynamic-update-slice_fusion.5.refs_1_.refs_0_.refs_6_), channel_id=1, source_target_pairs={{0,16},{16,0},{32,48},{48,32},{64,80},{80,64},{96,112},{112,96},{1... | collective-permute-start | bytes 1253384 | tf_op jit(solution)/shard_map/ppermute | solution.py:31
  37.2 2.2 %copy-start.2 = (bf16[4,144,384]{2,1,0:T(8,128)(2,1)}, bf16[4,144,384]{2,1,0:T(8,128)(2,1)S(1)}, u32[]{:S(2)}) copy-start(bf16[4,144,384]{2,1,0:T(8,128)(2,1)S(1)} %collective-permute-done.12) | copy-start | bytes 1327108
  37.2 2.2 %copy-start.3 = (bf16[4,144,384]{2,1,0:T(8,128)(2,1)}, bf16[4,144,384]{2,1,0:T(8,128)(2,1)S(1)}, u32[]{:S(2)}) copy-start(bf16[4,144,384]{2,1,0:T(8,128)(2,1)S(1)} %collective-permute-done.11) | copy-start | bytes 1327108
  37.3 1.4 %copy-start.4 = (bf16[4,144,384]{2,1,0:T(8,128)(2,1)}, bf16[4,144,384]{2,1,0:T(8,128)(2,1)S(1)}, u32[]{:S(2)}) copy-start(bf16[4,144,384]{2,1,0:T(8,128)(2,1)S(1)} %collective-permute-done.10) | copy-start | bytes 1327108
  38.6 0.8 %copy-start.5 = (bf16[68,8,384]{2,1,0:T(8,128)(2,1)}, bf16[68,8,384]{2,1,0:T(8,128)(2,1)S(1)}, u32[]{:S(2)}) copy-start(bf16[68,8,384]{2,1,0:T(8,128)(2,1)S(1)} %collective-permute-done.9.refs_2_.refs_1_.refs_7_) | copy-start | bytes 1253380
  43.3 19.4 %all-to-all-start = ((bf16[128,8,128]{2,1,0:T(8,128)(2,1)}), bf16[128,8,128]{2,1,0:T(8,128)(2,1)S(1)}, u32[]{:S(2)}, u32[]{:S(2)}) async-start(bf16[128,8,128]{2,1,0:T(8,128)(2,1)} %bitcast.51), calls=%async_computation | async-start | bytes 524288 | tf_op jit(solution)/shard_map/all_to_all | solution.py:437
